TPU v7x, 32 devices: a whole 2x2x4 slice. The times are simulated.
32 devices in a mesh: wide: 16 (over z, x, core), narrow: 2 (over y).
Axes of the slice: x: 2, y: 2, z: 4, core: 2. Of those that a mesh axis runs over, the one named last changes fastest.
Arguments:
- activation_cache: bfloat16 [16, 128, 8192], P('wide', None, 'narrow'), may hold values from -6 to 6
- token_ids: int32 [16, 128], P('wide'), may hold values from 0 to 127
- cotangent: bfloat16 [16, 128, 37120], P('wide', None, 'narrow'), may hold values from -6 to 6
- adapter_b: float32 [16, 16, 8192], P('wide', None, 'narrow'), may hold values from -4 to 4
- first_b: float32 [16, 16, 8192], P('wide', None, 'narrow'), may hold values from -0.3 to 0.3
- second_b: float32 [16, 16, 8192], P('wide', None, 'narrow'), may hold values from 0.0001 to 0.002
- adapter_a: float32 [16, 16, 37120], P('wide', None, 'narrow'), may hold values from -4 to 4
- first_a: float32 [16, 16, 37120], P('wide', None, 'narrow'), may hold values from -0.3 to 0.3
- second_a: float32 [16, 16, 37120], P('wide', None, 'narrow'), may hold values from 0.0001 to 0.002
- resident: bfloat16 [8192, 37120], P('narrow', 'wide'), may hold values from -6 to 6
- block_owner: int32 [16], replicated, may hold values from 0 to 15, each once
- next_rows: bfloat16 [512, 8192], P('wide', 'narrow'), may hold values from -6 to 6
Outputs:
- merged: bfloat16 [8192, 37120], P('narrow', 'wide')
- projected: bfloat16 [512, 37120], P('narrow', 'wide')
Inputs may be any that keep to these rules, and one draw needn't show every extreme that they name: `block_owner`: each column block is stored at exactly one position.
All inputs are finite; a program needn't handle non-finite values.
Results may differ from a plain program's by a relative error of at most 0.0058.
Values may be sent and summed in bfloat16 or wider, within the bound.
No kernel may reach another device: no remote copies, remote signals or barrier semaphores. Data moves between devices by JAX's collectives and lax.ppermute only.
A program may use at most 128 MiB of HBM per device.

v0:
```python
import math

import jax
import jax.numpy as jnp
from jax import lax
from jax.sharding import PartitionSpec as P

D = 8192
WORKER_TOKENS = 128


adapter_scale = 4.0
rate = 0.2
beta_one = 0.9
beta_two = 0.999
bias_one = 1.0 - 0.9**20
bias_two = 1.0 - 0.999**20
eps_adam = 1e-08


def adam_step(param, first, second, grad):
    first_new = beta_one * first + (1.0 - beta_one) * grad
    second_new = beta_two * second + (1.0 - beta_two) * grad * grad
    update = first_new / bias_one / (jnp.sqrt(second_new / bias_two) + eps_adam)
    return (param - rate * update).astype(jnp.bfloat16)


def per_device(
    activation_cache,
    token_ids,
    cotangent,
    adapter_b,
    first_b,
    second_b,
    adapter_a,
    first_a,
    second_a,
    resident,
    block_owner,
    next_rows,
):
    inverse_root = 1.0 / math.sqrt(D)
    highest_precision = lax.Precision.HIGHEST
    worker_group = lax.axis_size("wide")
    block_cols = resident.shape[1]
    selected_rows = jnp.take(activation_cache[0], token_ids[0], axis=0).astype(jnp.float32)
    incoming_gradient = cotangent[0].astype(jnp.float32)
    factor_b = adapter_b[0]
    factor_a = adapter_a[0]
    part_hidden = jnp.dot(selected_rows, factor_b.T, precision=highest_precision)
    part_upstream = jnp.dot(incoming_gradient, factor_a.T, precision=highest_precision)
    hidden_state, upstream_gradient = lax.psum((part_hidden, part_upstream), "narrow")
    hidden_state = hidden_state * inverse_root
    gradient_left = (
        adapter_scale
        / WORKER_TOKENS
        * jnp.dot(hidden_state.T, incoming_gradient, precision=highest_precision)
    )
    gradient_right = (
        adapter_scale
        * inverse_root
        / WORKER_TOKENS
        * jnp.dot(upstream_gradient.T, selected_rows, precision=highest_precision)
    )
    new_b = adam_step(factor_b, first_b[0], second_b[0], gradient_right)
    new_a = adam_step(factor_a, first_a[0], second_a[0], gradient_left)
    full_a = lax.all_gather(new_a, "narrow", axis=1, tiled=True)
    blocks = full_a.reshape(full_a.shape[0], worker_group, block_cols)
    ordered = jnp.take(blocks, block_owner, axis=1)
    arrived = lax.all_to_all(ordered, "wide", split_axis=1, concat_axis=0, tiled=True)
    right_rows = arrived.reshape(worker_group * full_a.shape[0], block_cols)
    weight_change = lax.dot_general(
        lax.all_gather(new_b, "wide", axis=0, tiled=True),
        right_rows,
        (((0,), (0,)), ((), ())),
        preferred_element_type=jnp.float32,
    )
    merged = (resident.astype(jnp.float32) + adapter_scale / worker_group * weight_change).astype(
        jnp.bfloat16
    )
    all_next = lax.all_gather(next_rows, "wide", axis=0, tiled=True)
    summed = lax.psum_scatter(
        jnp.dot(all_next, merged, preferred_element_type=jnp.float32),
        "narrow",
        scatter_dimension=0,
        tiled=True,
    )
    projected = (summed * inverse_root).astype(jnp.bfloat16)
    return (merged, projected)


def solution(mesh):
    return jax.shard_map(
        per_device,
        mesh=mesh,
        in_specs=(
            P("wide", None, "narrow"),
            P("wide", None),
            P("wide", None, "narrow"),
            P("wide", None, "narrow"),
            P("wide", None, "narrow"),
            P("wide", None, "narrow"),
            P("wide", None, "narrow"),
            P("wide", None, "narrow"),
            P("wide", None, "narrow"),
            P("narrow", "wide"),
            P(),
            P("wide", "narrow"),
        ),
        out_specs=(P("narrow", "wide"), P("narrow", "wide")),
        check_vma=False,
    )
```

profile of v0, /device:TPU:9, one launch (start us, length us, event | category | flops | bytes accessed | tf_op | source)
XLA Modules:
  0.0 245.4 jit_solution(827709427198518695)
XLA Ops:
  7.2 0.0 copy-start
  7.2 0.0 all-gather.6.cloned.1.call-start
  7.2 0.7 compare_and_fusion.1
  8.0 0.7 fusion.30
  8.6 6.0 %fusion.2 = f32[128,16]{1,0:T(8,128)S(1)} fusion(bf16[1,128,18560]{2,1,0:T(8,128)(2,1)} %param.14, f32[1,16,18560]{2,1,0:T(8,128)} %param.18), kind=kOutput, calls=%fused_computation.6 | convolution fusion | flops 456130560 | bytes 5947392 | tf_op jit(solution)/shard_map/dot_general | solution.py:51
  14.6 1.2 gather_fusion
  15.8 0.0 copy-start.2
  15.9 2.1 fusion.17
  17.9 7.6 %all-reduce = (f32[128,16]{1,0:T(8,128)S(1)}, f32[128,16]{1,0:T(8,128)S(1)}) all-reduce(f32[128,16]{1,0:T(8,128)S(1)} %fusion.2, f32[128,16]{1,0:T(8,128)S(1)} %fusion.17), channel_id=1, replica_groups=mesh['wide'=16,'narrow'=2] {'narrow'}, use_global_device_ids=true, to_apply=%region_0.1 | all-reduce | flops 4096 | bytes 32768 | tf_op jit(solution)/shard_map/psum | solution.py:52
  25.6 0.0 copy-start.5
  25.6 6.3 %fusion.14 = bf16[16,18560]{1,0:T(8,128)(2,1)} fusion(f32[1,16,18560]{2,1,0:T(8,128)} %param.20, bf16[1,128,18560]{2,1,0:T(8,128)(2,1)} %param.14, f32[1,16,18560]{2,1,0:T(8,128)S(1)} %copy-done.2, f32[1,16,18560]{2,1,0:T(8,128)} %param.19, f32[128,16]{1,0:T(8,128)S(1)} %get-tuple-element.3), kind=kOutput, calls=%fused_computation.20 | convolution fusion | flops 460587008 | bytes 8916992 | tf_op jit(solution)/shard_map/dot_general | solution.py:57
  31.9 0.0 all-gather.6.cloned.1.call-update
  31.9 0.0 all-gather.4.cloned.1.call-start
  32.0 0.0 copy-start.6
  32.0 1.4 fusion.27
  33.4 0.0 all-gather.4.cloned.1.call-update
  33.4 0.0 all-gather.8.cloned.1.call-start
  33.5 0.7 all-gather.8.cloned.1.call-update
  34.2 0.0 reduce-scatter.2.cloned.1.call-start
  34.3 22.9 %all-gather.6.cloned.1.call-done = bf16[16,37120]{1,0:T(8,128)(2,1)} async-done(((bf16[16,18560]{1,0:T(8,128)(2,1)}), bf16[16,37120]{1,0:T(8,128)(2,1)}) %all-gather.6.cloned.1.call-update) | async-done | bytes 1187856 | tf_op jit(solution)/shard_map/all_gather | solution.py:67
  57.2 2.8 %reshape.58 = bf16[16,16,2320]{2,1,0:T(8,128)(2,1)S(1)} reshape(bf16[16,37120]{1,0:T(8,128)(2,1)} %all-gather.6.cloned.1.call-done) | data formatting | bytes 2375680 | tf_op jit(solution)/shard_map/reshape | solution.py:68
  60.0 0.2 copy.14
  60.2 0.7 gather_fusion.1
  60.9 0.2 select_bitcast_fusion
  61.1 48.6 %all_to_all.15 = bf16[16,16,2320]{2,0,1:T(8,128)(2,1)S(1)} all-to-all(bf16[16,16,2320]{2,0,1:T(8,128)(2,1)S(1)} %select_bitcast_fusion), channel_id=1, replica_groups=mesh['wide'=16,'narrow'=2] {'wide'}, dimensions={1} | all-to-all | bytes 2375680 | tf_op jit(solution)/shard_map/all_to_all | solution.py:70
  109.8 16.0 %add_convert_fusion = bf16[4096,2320]{0,1:T(8,128)(2,1)} fusion(bf16[4096,2320]{0,1:T(8,128)(2,1)} %param.21, bf16[256,4096]{1,0:T(8,128)(2,1)} %all-gather.4.cloned.1.call-done, bf16[256,2320]{1,0:T(8,128)(2,1)S(1)} %bitcast.91), kind=kOutput, calls=%fused_computation.2 | convolution fusion | flops 4903403520 | bytes 41295872 | tf_op jit(solution)/shard_map/dot_general | solution.py:72
  125.7 35.0 %all-gather.8.cloned.1.call-done = bf16[512,4096]{1,0:T(8,128)(2,1)} async-done(((bf16[32,4096]{1,0:T(8,128)(2,1)}), bf16[512,4096]{1,0:T(8,128)(2,1)}) %all-gather.8.cloned.1.call-update) | async-done | bytes 4194320 | tf_op jit(solution)/shard_map/all_gather | solution.py:81
  160.8 16.6 %convolution_bitcast_fusion = f32[512,2320]{0,1:T(8,128)} fusion(bf16[4096,2320]{0,1:T(8,128)(2,1)} %add_convert_fusion, bf16[512,4096]{1,0:T(8,128)(2,1)} %all-gather.8.cloned.1.call-done), kind=kOutput, calls=%fused_computation.3 | convolution fusion | flops 9730785280 | bytes 27951104 | tf_op jit(solution)/shard_map/dot_general | solution.py:83
  177.4 0.0 reduce-scatter.2.cloned.1.call-update
  177.4 0.0 copy-start.1
  177.4 58.6 %reduce-scatter.2.cloned.1.call-done = f32[256,2320]{0,1:T(8,128)} async-done(((f32[512,2320]{0,1:T(8,128)}), f32[256,2320]{0,1:T(8,128)}) %reduce-scatter.2.cloned.1.call-update) | async-done | bytes 2375696 | tf_op jit(solution)/shard_map/reduce_scatter | solution.py:82
  236.0 2.9 %multiply_convert_fusion = bf16[256,2320]{0,1:T(8,128)(2,1)} fusion(f32[256,2320]{0,1:T(8,128)} %reduce-scatter.2.cloned.1.call-done), kind=kLoop, calls=%fused_computation.8 | loop fusion | flops 1187840 | bytes 3563520 | tf_op jit(solution)/shard_map/convert_element_type | solution.py:88
  (14 shorter events, 0.1 us)
Async XLA Ops:
  7.2 7.5 %copy-start = (bf16[1,128,4096]{2,1,0:T(8,128)(2,1)S(1)}, bf16[1,128,4096]{2,1,0:T(8,128)(2,1)}, u32[]{:S(2)}) copy-start(bf16[1,128,4096]{2,1,0:T(8,128)(2,1)} %param.12) | copy-start | bytes 3145732
  7.2 50.0 %all-gather.6.cloned.1.call-start = ((), (), s32[]{:S(2)}) async-start(), calls=%async_computation.3 | async-start | bytes 1781760 | tf_op jit(solution)/shard_map/all_gather | solution.py:67
  15.8 9.7 %copy-start.2 = (f32[1,16,18560]{2,1,0:T(8,128)S(1)}, f32[1,16,18560]{2,1,0:T(8,128)}, u32[]{:S(2)}) copy-start(f32[1,16,18560]{2,1,0:T(8,128)} %param.18) | copy-start | bytes 3563524
  25.6 6.4 %copy-start.3 = (f32[1,16,4096]{2,1,0:T(8,128)S(1)}, f32[1,16,4096]{2,1,0:T(8,128)}, u32[]{:S(2)}) copy-start(f32[1,16,4096]{2,1,0:T(8,128)} %param.15) | copy-start | bytes 786436
  25.6 6.4 %copy-start.4 = (f32[1,16,4096]{2,1,0:T(8,128)S(1)}, f32[1,16,4096]{2,1,0:T(8,128)}, u32[]{:S(2)}) copy-start(f32[1,16,4096]{2,1,0:T(8,128)} %param.17) | copy-start | bytes 786436
  25.6 6.4 %copy-start.5 = (f32[1,16,4096]{2,1,0:T(8,128)S(1)}, f32[1,16,4096]{2,1,0:T(8,128)}, u32[]{:S(2)}) copy-start(f32[1,16,4096]{2,1,0:T(8,128)} %param.16) | copy-start | bytes 786436
  31.9 77.8 %all-gather.4.cloned.1.call-start = ((), (), s32[]{:S(2)}) async-start(), calls=%async_computation.2 | async-start | bytes 2228224 | tf_op jit(solution)/shard_map/all_gather | solution.py:73
  32.0 2.2 copy-start.6
  33.4 127.3 %all-gather.8.cloned.1.call-start = ((), (), s32[]{:S(2)}) async-start(), calls=%async_computation.4 | async-start | bytes 4456448 | tf_op jit(solution)/shard_map/all_gather | solution.py:81
  34.2 201.8 %reduce-scatter.2.cloned.1.call-start = ((), (), s32[]{:S(2)}) async-start(), calls=%async_computation.5 | async-start | bytes 7127040 | tf_op jit(solution)/shard_map/reduce_scatter | solution.py:82
  177.4 61.5 %copy-start.1 = (bf16[1,128,4096]{2,1,0:T(8,128)(2,1)S(1)}, bf16[1,128,4096]{2,1,0:T(8,128)(2,1)}, u32[]{:S(2)}) copy-start(bf16[1,128,4096]{2,1,0:T(8,128)(2,1)} %param.12) | copy-start | bytes 3145732
Sparse Core Ops, SparseCore 0:
  32.1 25.0 all-gather.5
  59.9 47.9 all-gather.3
  110.1 50.6 all-gather.7
  177.5 58.4 reduce-scatter.1
where the time goes:
time: 247 us; the launch traced here: 245 us
  waiting for transfers between devices  117 us (47%)
  blocking collectives  56.3 us (23%)
  matrix products  48.3 us (20%)
  between operations  14 us (6%)
  local copies, waits for them, and re-layouts  4.95 us (2%)
  other arithmetic  4.55 us (2%)
    reduce_scatter x1, waiting for transfers between devices, per_device(): lax.psum_scatter(jnp.dot(all_next, merged, preferred_element_type=jnp.flo...  58.6 us
    all_to_all x1, blocking collectives, per_device(): lax.all_to_all(ordered, 'wide', split_axis=1, concat_axis=0, tiled=True)  48.6 us
    all_gather x1, waiting for transfers between devices, per_device(): all_next = lax.all_gather(next_rows, 'wide', axis=0, tiled=True)  35 us
    all_gather x1, waiting for transfers between devices, per_device(): full_a = lax.all_gather(new_a, 'narrow', axis=1, tiled=True)  22.9 us
    dot_general x1, matrix products, per_device(): jnp.dot(all_next, merged, preferred_element_type=jnp.float32)  16.6 us
    dot_general x1, matrix products, per_device(): lax.dot_general(lax.all_gather(new_b, 'wide', axis=0, tiled=True), right_...  16 us
    psum x1, blocking collectives, per_device(): lax.psum((part_hidden, part_upstream), 'narrow')  7.63 us
    dot_general x1, matrix products, per_device(): jnp.dot(hidden_state.T, incoming_gradient, precision=highest_precision)  6.31 us
  transfers between devices with their start and end apart: 4, of which 3 were waited for; matrix products, arithmetic and copies ran while one was open for 9% of the time, Pallas kernels for 0%

commit v1 on v0

--- a/solution.py
+++ b/solution.py
@@ -1,13 +1,12 @@
+import functools
 import math
 
 import jax
 import jax.numpy as jnp
 from jax import lax
+from jax.experimental import pallas as pl
+from jax.experimental.pallas import tpu as pltpu
 from jax.sharding import PartitionSpec as P
-
-D = 8192
-WORKER_TOKENS = 128
-
 
 adapter_scale = 4.0
 rate = 0.2
@@ -17,12 +16,437 @@
 bias_two = 1.0 - 0.999**20
 eps_adam = 1e-08
 
+F32 = jnp.float32
+BF16 = jnp.bfloat16
+MIB = 1024 * 1024
+VMEM_LIMIT = 56 * MIB
+
 
 def adam_step(param, first, second, grad):
     first_new = beta_one * first + (1.0 - beta_one) * grad
     second_new = beta_two * second + (1.0 - beta_two) * grad * grad
-    update = first_new / bias_one / (jnp.sqrt(second_new / bias_two) + eps_adam)
-    return (param - rate * update).astype(jnp.bfloat16)
+    root = jnp.sqrt(second_new * (1.0 / bias_two)) + eps_adam
+    return (param - (rate / bias_one) * first_new / root).astype(BF16)
+
+
+def plain_call(kernel, flops, moved, **kw):
+    return pl.pallas_call(
+        kernel,
+        compiler_params=pltpu.CompilerParams(
+            vmem_limit_bytes=VMEM_LIMIT,
+            dimension_semantics=("arbitrary",) * len(kw.get("grid", ())),
+        ),
+        cost_estimate=pl.CostEstimate(flops=flops, bytes_accessed=moved, transcendentals=0),
+        **kw,
+    )
+
+
+def in_vmem():
+    return pl.BlockSpec(memory_space=pltpu.VMEM)
+
+
+def anywhere():
+    return pl.BlockSpec(memory_space=pl.ANY)
+
+
+def split(value):
+    top = value.astype(BF16)
+    left = value - top.astype(F32)
+    middle = left.astype(BF16)
+    bottom = (left - middle.astype(F32)).astype(BF16)
+    return jnp.concatenate([top, middle, bottom], axis=0)
+
+
+def fold(value):
+    rows = value.shape[0] // 3
+    return value[:rows] + (value[rows : 2 * rows] + value[2 * rows :])
+
+
+def dot_rows(value, other):
+    return fold(
+        lax.dot_general(split(value), other, (((1,), (1,)), ((), ())), preferred_element_type=F32)
+    )
+
+
+def dot_plain(parts, other):
+    return fold(jnp.dot(parts, other, preferred_element_type=F32))
+
+
+def column_tile(columns, most):
+    count = columns // 128
+    best = max(d for d in range(1, count + 1) if count % d == 0 and d * 128 <= most)
+    return best * 128
+
+
+def row_tile(rows, most):
+    return max(d for d in range(16, most + 1, 16) if rows % d == 0)
+
+
+def products(cache, factor_b, cotangent, factor_a):
+    _, rank, columns = factor_a.shape
+    tokens = cotangent.shape[1]
+    pool, features = cache.shape[1:]
+    tile = column_tile(columns, 4096)
+
+    def kernel(cache_ref, b_ref, cot_ref, a_ref, out_ref):
+        @pl.when(pl.program_id(0) == 0)
+        def _():
+            out_ref[:rank] = dot_rows(b_ref[...], cache_ref[...])
+            out_ref[rank:] = jnp.zeros((rank, tokens), F32)
+
+        out_ref[rank:] += dot_rows(a_ref[...], cot_ref[...])
+
+    return plain_call(
+        kernel,
+        6 * rank * (tokens * columns + pool * features),
+        2 * tokens * columns + 4 * rank * columns + 2 * pool * features + 4 * rank * features,
+        grid=(columns // tile,),
+        in_specs=[
+            pl.BlockSpec((None, pool, features), lambda i: (0, 0, 0)),
+            pl.BlockSpec((None, rank, features), lambda i: (0, 0, 0)),
+            pl.BlockSpec((None, tokens, tile), lambda i: (0, 0, i)),
+            pl.BlockSpec((None, rank, tile), lambda i: (0, 0, i)),
+        ],
+        out_specs=pl.BlockSpec((2 * rank, tokens), lambda i: (0, 0)),
+        out_shape=jax.ShapeDtypeStruct((2 * rank, tokens), F32),
+        name="products",
+    )(cache, factor_b, cotangent, factor_a)
+
+
+def adam(ids, own, other, cache, b_set, cotangent, a_set, block_cols, inverse_root, after):
+    _, rank, columns = a_set[0].shape
+    tokens = cotangent.shape[1]
+    pool, features = cache.shape[1:]
+    tile = column_tile(columns, 4096)
+    steps = columns // tile
+    blocks = columns // block_cols
+    count = len(after)
+
+    def kernel(ids_ref, own_ref, other_ref, cache_ref, b0, b1, b2, cot_ref, a0, a1, a2, *rest):
+        out_b, out_a, whole, hidden = rest[count:]
+        step = pl.program_id(0)
+
+        @pl.when(step == 0)
+        def _():
+            sums = own_ref[...] + other_ref[...]
+            chosen = lax.broadcasted_iota(jnp.int32, (pool, tokens), 0) == ids_ref[...]
+            chosen = chosen.astype(F32).astype(BF16)
+            hidden[...] = split(dot_plain(split(sums[:rank] * inverse_root), chosen))
+            upstream = dot_rows(sums[rank:], chosen)
+            grad = (adapter_scale * inverse_root / tokens) * dot_plain(
+                split(upstream), cache_ref[...]
+            )
+            out_b[...] = adam_step(b0[...], b1[...], b2[...], grad)
+
+        grad = (adapter_scale / tokens) * dot_plain(hidden[...], cot_ref[...])
+        new = adam_step(a0[...], a1[...], a2[...], grad)
+        for s in range(steps):
+
+            @pl.when(step == s)
+            def _():
+                whole[:, s * tile : (s + 1) * tile] = new
+
+        @pl.when(step == steps - 1)
+        def _():
+            for c in range(blocks):
+                out_a[c] = whole[:, c * block_cols : (c + 1) * block_cols]
+
+    fixed = lambda i: (0, 0, 0)
+    return plain_call(
+        kernel,
+        6 * rank * (tokens * columns + pool * features),
+        2 * tokens * columns + 14 * rank * columns + 2 * pool * features + 14 * rank * features,
+        grid=(steps,),
+        in_specs=[
+            pl.BlockSpec((1, tokens), lambda i: (0, 0)),
+            pl.BlockSpec((2 * rank, tokens), lambda i: (0, 0)),
+            pl.BlockSpec((2 * rank, tokens), lambda i: (0, 0)),
+            pl.BlockSpec((None, pool, features), fixed),
+        ]
+        + [pl.BlockSpec((None, rank, features), fixed)] * 3
+        + [pl.BlockSpec((None, tokens, tile), lambda i: (0, 0, i))]
+        + [pl.BlockSpec((None, rank, tile), lambda i: (0, 0, i))] * 3
+        + [anywhere()] * count,
+        out_specs=[
+            pl.BlockSpec((rank, features), lambda i: (0, 0)),
+            pl.BlockSpec((blocks, rank, block_cols), fixed),
+        ],
+        out_shape=[
+            jax.ShapeDtypeStruct((rank, features), BF16),
+            jax.ShapeDtypeStruct((blocks, rank, block_cols), BF16),
+        ],
+        scratch_shapes=[
+            pltpu.VMEM((rank, columns), BF16),
+            pltpu.VMEM((3 * rank, tokens), BF16),
+        ],
+        name="adam",
+    )(ids, own, other, cache, *b_set, cotangent, *a_set, *after)
+
+
+def across(value, wide, flip):
+    return lax.ppermute(value, "wide", [(i, i ^ flip) for i in range(wide)])
+
+
+def other_side(value):
+    return lax.ppermute(value, "narrow", [(0, 1), (1, 0)])
+
+
+def ring_pair(at, pairs):
+    return jnp.where(at < pairs // 2, 2 * at, 2 * pairs - 1 - 2 * at)
+
+
+def ring_place(pair, pairs):
+    return jnp.where(pair % 2 == 0, pair // 2, pairs - 1 - pair // 2)
+
+
+def ring_links(wide, step):
+    pairs = wide // 2
+    order = list(range(0, pairs, 2)) + list(range(pairs - 1, 0, -2))
+    return [
+        (2 * pair + core, 2 * order[(at + step) % pairs] + core)
+        for at, pair in enumerate(order)
+        for core in (0, 1)
+    ]
+
+
+def along(value, wide, step):
+    return lax.ppermute(value, "wide", ring_links(wide, step))
+
+
+def piece_plan(wide, rows):
+    pairs = wide // 2
+    plan = [(0, 0)]
+    for step in range(1, pairs // 2):
+        plan += [(-step, 0), (step, 0)]
+    return plan + [(-(pairs // 2), 0), (pairs // 2, rows // 2)]
+
+
+def early_projection(pieces, plan, whole_next, resident, wide, rows, first, last, tile, after):
+    columns, depth = resident.shape
+    total = wide * rows
+    half = total // 2
+    pairs = wide // 2
+    count = len(pieces)
+    gather = whole_next is None
+    height = (last - first) * tile
+
+    def kernel(*refs):
+        res_ref = refs[0]
+        if gather:
+            piece_refs = refs[1 : 1 + count]
+            own_ref, away_ref, rows_ref, sems = refs[1 + count + len(after) :]
+
+            @pl.when(pl.program_id(0) == 0)
+            def _():
+                side = lax.axis_index("narrow")
+                device = lax.axis_index("wide")
+                at = ring_place(device // 2, pairs)
+                copies = []
+                for i, ref in enumerate(piece_refs):
+                    distance, offset = plan[i // 2]
+                    pair = ring_pair((at + distance + pairs) % pairs, pairs)
+                    source = 2 * pair + (device + i) % 2
+                    row = ((source // pairs + side) % 2) * half + (source % pairs) * rows + offset
+                    copy = pltpu.make_async_copy(
+                        ref,
+                        rows_ref.at[pl.ds(pl.multiple_of(row, 16), ref.shape[0])],
+                        sems.at[i],
+                    )
+                    copy.start()
+                    copies.append(copy)
+                for copy in copies:
+                    copy.wait()
+
+        else:
+            rows_ref = refs[1]
+            own_ref, away_ref = refs[2 + len(after) :]
+        value = lax.dot_general(
+            res_ref[...], rows_ref[...], (((1,), (1,)), ((), ())), preferred_element_type=F32
+        )
+        own_ref[...] = value[:, :half]
+        away_ref[...] = value[:, half:].astype(BF16)
+
+    out_specs = [pl.BlockSpec((tile, half), lambda i: (i, 0))] * 2
+    out_shape = [
+        jax.ShapeDtypeStruct((height, half), F32),
+        jax.ShapeDtypeStruct((height, half), BF16),
+    ]
+    scratch = []
+    if gather:
+        out_specs.append(pl.BlockSpec((total, depth), lambda i: (0, 0)))
+        out_shape.append(jax.ShapeDtypeStruct((total, depth), BF16))
+        scratch = [pltpu.SemaphoreType.DMA((count,))]
+        operands = list(pieces)
+        specs = [anywhere()] * count
+    else:
+        operands = [whole_next]
+        specs = [pl.BlockSpec((total, depth), lambda i: (0, 0))]
+    return plain_call(
+        kernel,
+        2 * total * depth * height,
+        2 * depth * height + 2 * total * depth + 6 * half * height,
+        grid=(last - first,),
+        in_specs=[pl.BlockSpec((tile, depth), lambda i: (first + i, 0))]
+        + specs
+        + [anywhere()] * len(after),
+        out_specs=out_specs,
+        out_shape=out_shape,
+        scratch_shapes=scratch,
+        name="early_projection",
+    )(resident, *operands, *after)
+
+
+def low_rank_rows(all_next, left):
+    total, depth = all_next.shape
+    ranks = left.shape[0]
+    half = total // 2
+    tile = column_tile(depth, 1024)
+
+    def kernel(next_ref, left_ref, own_ref, away_ref):
+        @pl.when(pl.program_id(0) == 0)
+        def _():
+            own_ref[...] = jnp.zeros_like(own_ref)
+            away_ref[...] = jnp.zeros_like(away_ref)
+
+        value = lax.dot_general(
+            left_ref[...], next_ref[...], (((1,), (1,)), ((), ())), preferred_element_type=F32
+        )
+        own_ref[...] += value[:, :half]
+        away_ref[...] += value[:, half:]
+
+    return plain_call(
+        kernel,
+        2 * total * depth * ranks,
+        2 * depth * (total + ranks) + 4 * total * ranks,
+        grid=(depth // tile,),
+        in_specs=[
+            pl.BlockSpec((total, tile), lambda i: (0, i)),
+            pl.BlockSpec((ranks, tile), lambda i: (0, i)),
+        ],
+        out_specs=[pl.BlockSpec((ranks, half), lambda i: (0, 0))] * 2,
+        out_shape=[jax.ShapeDtypeStruct((ranks, half), F32)] * 2,
+        name="low_rank_rows",
+    )(all_next, left)
+
+
+def sort_blocks(block_owner, own, other, wide):
+    blocks, rank, block_cols = own.shape
+    pairs = wide // 2
+
+    def kernel(owner_ref, own_ref, other_ref, mine_ref, yours_ref):
+        side = lax.axis_index("narrow")
+        device = lax.axis_index("wide")
+        core = device % 2
+        for flip in range(pairs):
+            for o, out_ref in ((0, mine_ref), (1, yours_ref)):
+                block = owner_ref[2 * ((device // 2) ^ flip) + (core + o) % 2]
+                here = block // blocks == side
+
+                @pl.when(here)
+                def _():
+                    out_ref[flip] = own_ref[block % blocks]
+
+                @pl.when(jnp.logical_not(here))
+                def _():
+                    out_ref[flip] = other_ref[block % blocks]
+
+    shape = jax.ShapeDtypeStruct((pairs, rank, block_cols), own.dtype)
+    return plain_call(
+        kernel,
+        0,
+        8 * pairs * rank * block_cols,
+        in_specs=[pl.BlockSpec(memory_space=pltpu.SMEM), in_vmem(), in_vmem()],
+        out_specs=[in_vmem(), in_vmem()],
+        out_shape=[shape, shape],
+        name="sort_blocks",
+    )(block_owner, own, other)
+
+
+def merge(resident, left, pieces, scale):
+    columns, depth = resident.shape
+    ranks = left.shape[0]
+    rank = pieces[0].shape[1]
+    tile = column_tile(depth, 512)
+    count = len(pieces)
+
+    def kernel(res_ref, left_ref, *refs):
+        out_ref, turned_ref, right_ref = refs[count:]
+
+        @pl.when(pl.program_id(0) == 0)
+        def _():
+            device = lax.axis_index("wide")
+            for flip, ref in enumerate(refs[:count]):
+                for o in (0, 1):
+                    worker = 2 * ((device // 2) ^ flip) + (device + o) % 2
+                    right_ref[pl.ds(pl.multiple_of(worker * rank, rank), rank), :] = ref[o]
+            for at in range(0, columns, 256):
+                width = min(256, columns - at)
+                unit = lax.broadcasted_iota(jnp.int32, (width, width), 0)
+                unit = unit == lax.broadcasted_iota(jnp.int32, (width, width), 1)
+                turned_ref[at : at + width] = lax.dot_general(
+                    unit.astype(F32).astype(BF16),
+                    right_ref[:, at : at + width],
+                    (((1,), (1,)), ((), ())),
+                    preferred_element_type=F32,
+                ).astype(BF16)
+
+        delta = jnp.dot(turned_ref[...], left_ref[...], preferred_element_type=F32)
+        out_ref[...] = (res_ref[...].astype(F32) + scale * delta).astype(BF16)
+
+    return plain_call(
+        kernel,
+        2 * depth * columns * ranks,
+        4 * depth * columns + 2 * ranks * (depth + columns),
+        grid=(depth // tile,),
+        in_specs=[
+            pl.BlockSpec((columns, tile), lambda i: (0, i)),
+            pl.BlockSpec((ranks, tile), lambda i: (0, i)),
+        ]
+        + [pl.BlockSpec(pieces[0].shape, lambda i: (0, 0, 0))] * count,
+        out_specs=[
+            pl.BlockSpec((columns, tile), lambda i: (0, i)),
+            pl.BlockSpec((columns, ranks), lambda i: (0, 0)),
+        ],
+        out_shape=[
+            jax.ShapeDtypeStruct((columns, depth), BF16),
+            jax.ShapeDtypeStruct((columns, ranks), BF16),
+        ],
+        scratch_shapes=[pltpu.VMEM((ranks, columns), BF16)],
+        name="merge",
+    )(resident, left, *pieces)
+
+
+def finish(parts, low_own, low_other, turned, scale, inverse_root):
+    ranks, half = low_own.shape
+    columns = turned.shape[0]
+
+    def kernel(own_low_ref, other_low_ref, turned_ref, *refs):
+        out_ref = refs[-1]
+        low = own_low_ref[...] + other_low_ref[...]
+        high = low.astype(BF16)
+        rest = (low - high.astype(F32)).astype(BF16)
+        at = 0
+        for i in range(len(parts)):
+            own, other = refs[2 * i : 2 * i + 2]
+            height = own.shape[0]
+            right = turned_ref[at : at + height]
+            shift = jnp.dot(right, high, preferred_element_type=F32) + jnp.dot(
+                right, rest, preferred_element_type=F32
+            )
+            out_ref[at : at + height] = (
+                (own[...] + other[...].astype(F32) + scale * shift) * inverse_root
+            ).astype(BF16)
+            at += height
+
+    return plain_call(
+        kernel,
+        4 * half * ranks * columns,
+        8 * half * columns + 2 * ranks * columns,
+        in_specs=[in_vmem()] * (2 * len(parts) + 3),
+        out_specs=in_vmem(),
+        out_shape=jax.ShapeDtypeStruct((columns, half), BF16),
+        name="finish",
+    )(low_own, low_other, turned, *[x for part in parts for x in part])
 
 
 def per_device(
@@ -39,7 +463,91 @@
     block_owner,
     next_rows,
 ):
-    inverse_root = 1.0 / math.sqrt(D)
+    inverse_root = 1.0 / math.sqrt(2 * next_rows.shape[1])
+    wide = lax.axis_size("wide")
+    pairs = wide // 2
+    rows = next_rows.shape[0]
+    resident = resident.T
+    block_cols = resident.shape[0]
+    scale = adapter_scale / wide
+    hold = lax.optimization_barrier
+
+    plan = piece_plan(wide, rows)
+    pieces = [next_rows, across(next_rows, wide, 1)]
+
+    def keep(piece):
+        pieces.extend([piece, across(piece, wide, 1)])
+
+    ahead, behind = along(next_rows, wide, 1), along(next_rows, wide, -1)
+    own_sums = products(activation_cache, adapter_b, cotangent, adapter_a)
+    other_sums = other_side(own_sums)
+    ahead, behind, own_sums = hold((ahead, behind, own_sums))
+    keep(ahead)
+    keep(behind)
+    new_b, own_blocks = adam(
+        token_ids,
+        own_sums,
+        other_sums,
+        activation_cache,
+        (adapter_b, first_b, second_b),
+        cotangent,
+        (adapter_a, first_a, second_a),
+        block_cols,
+        inverse_root,
+        (ahead, behind),
+    )
+    left = lax.all_gather(new_b, "wide", axis=0, tiled=True)
+    other_blocks = other_side(own_blocks)
+    for step in range(2, pairs // 2):
+        ahead, behind = along(ahead, wide, 1), along(behind, wide, -1)
+        keep(ahead)
+        keep(behind)
+    keep(along(ahead[: rows // 2], wide, 1))
+    keep(along(behind[rows // 2 :], wide, -1))
+
+    mine, yours = sort_blocks(block_owner, own_blocks, other_blocks, wide)
+    handed = across(yours, wide, 1)
+
+    tile = row_tile(block_cols, 512)
+    tiles = block_cols // tile
+    cut = (tiles + 1) // 2
+    own_0, away_0, all_next = early_projection(
+        pieces, plan, None, resident, wide, rows, 0, cut, tile, ()
+    )
+    got_0 = other_side(away_0)
+    right = []
+    for flip in range(pairs):
+        piece = jnp.stack([mine[flip], handed[flip]])
+        right.append(across(piece, wide, 2 * flip) if flip else piece)
+    own_1, away_1 = early_projection(
+        [], plan, all_next, resident, wide, rows, cut, tiles, tile, ()
+    )
+    got_1 = other_side(away_1)
+
+    low_own, low_away = low_rank_rows(all_next, left)
+    low_other = other_side(low_away)
+    merged, turned = merge(resident, left, right, scale)
+    projected = finish(
+        ((own_0, got_0), (own_1, got_1)), low_own, low_other, turned, scale, inverse_root
+    )
+    return (merged.T, projected.T)
+
+
+def any_mesh(
+    activation_cache,
+    token_ids,
+    cotangent,
+    adapter_b,
+    first_b,
+    second_b,
+    adapter_a,
+    first_a,
+    second_a,
+    resident,
+    block_owner,
+    next_rows,
+):
+    inverse_root = 1.0 / math.sqrt(next_rows.shape[1] * lax.axis_size("narrow"))
     highest_precision = lax.Precision.HIGHEST
     worker_group = lax.axis_size("wide")
     block_cols = resident.shape[1]
@@ -53,13 +561,13 @@
     hidden_state = hidden_state * inverse_root
     gradient_left = (
         adapter_scale
-        / WORKER_TOKENS
+        / token_ids.shape[1]
         * jnp.dot(hidden_state.T, incoming_gradient, precision=highest_precision)
     )
     gradient_right = (
         adapter_scale
         * inverse_root
-        / WORKER_TOKENS
+        / token_ids.shape[1]
         * jnp.dot(upstream_gradient.T, selected_rows, precision=highest_precision)
     )
     new_b = adam_step(factor_b, first_b[0], second_b[0], gradient_right)
@@ -90,8 +598,9 @@
 
 
 def solution(mesh):
+    paired = mesh.shape["narrow"] == 2 and mesh.shape["wide"] == 16
     return jax.shard_map(
-        per_device,
+        per_device if paired else any_mesh,
         mesh=mesh,
         in_specs=(
             P("wide", None, "narrow"),

time: 247 us -> 143 us (0.58)
  waiting for transfers between devices: 117 us -> 23.6 us
  Pallas kernels: 0 us -> 66.2 us
  blocking collectives: 56.3 us -> 0 us
  matrix products: 48.3 us -> 0 us
  starting transfers between devices: 0.16 us -> 32.4 us
  other arithmetic: 4.55 us -> 0.84 us
    pallas_call x0 -> x8, Pallas kernels: none -> 66.2 us  [the longest x2 20.9 us: early_projection(): plain_call(kernel, 2 * total * depth * height, 2 * depth * height + 2 * t...]
    reduce_scatter x1 -> x0, waiting for transfers between devices: 58.6 us -> none  [per_device(): lax.psum_scatter(jnp.dot(all_next, merged, preferred_element_type=jnp.flo...]
    all_gather x3 -> x1, waiting for transfers between devices: 58 us -> 0.01 us  [per_device(): left = lax.all_gather(new_b, 'wide', axis=0, tiled=True)]
    all_to_all x1 -> x0, blocking collectives: 48.6 us -> none  [per_device(): lax.all_to_all(ordered, 'wide', split_axis=1, concat_axis=0, tiled=True)]
    dot_general x6 -> x0, matrix products: 48.3 us -> none  [the longest x1 16.6 us: per_device(): jnp.dot(all_next, merged, preferred_element_type=jnp.float32)]
    ppermute x0 -> x30, starting transfers between devices: none -> 32.4 us  [the longest x17 20.7 us: across(): return lax.ppermute(value, 'wide', [(i, i ^ flip) for i in range(wide)])]
    ppermute x0 -> x30, waiting for transfers between devices: none -> 23.6 us  [the longest x17 21.1 us: across(): return lax.ppermute(value, 'wide', [(i, i ^ flip) for i in range(wide)])]
    psum x1 -> x0, blocking collectives: 7.63 us -> none  [per_device(): lax.psum((part_hidden, part_upstream), 'narrow')]
  transfers between devices with their start and end apart: 4 -> 31, of which waited for: 3 -> 8; matrix products, arithmetic and copies ran while one was open for 9% -> 1% of each run, Pallas kernels for 0% -> 43%
where the time goes in v1:
time: 143 us
  Pallas kernels  66.2 us (46%)
  starting transfers between devices  32.4 us (23%)
  waiting for transfers between devices  23.6 us (17%)
  between operations  14.4 us (10%)
  local copies, waits for them, and re-layouts  5.14 us (4%)
    ppermute x17, waiting for transfers between devices, across(): return lax.ppermute(value, 'wide', [(i, i ^ flip) for i in range(wide)])  21.1 us
    pallas_call x2, Pallas kernels, early_projection(): plain_call(kernel, 2 * total * depth * height, 2 * depth * height + 2 * t...  20.9 us
    ppermute x17, starting transfers between devices, across(): return lax.ppermute(value, 'wide', [(i, i ^ flip) for i in range(wide)])  20.7 us
    pallas_call x1, Pallas kernels, merge(): plain_call(kernel, 2 * depth * columns * ranks, 4 * depth * columns + 2 *...  18.7 us
    pallas_call x1, Pallas kernels, adam(): plain_call(kernel, 6 * rank * (tokens * columns + pool * features), 2 * t...  7.73 us
    pallas_call x1, Pallas kernels, products(): plain_call(kernel, 6 * rank * (tokens * columns + pool * features), 2 * t...  6.6 us
    ppermute x8, starting transfers between devices, along(): return lax.ppermute(value, 'wide', ring_links(wide, step))  6.01 us
    ppermute x5, starting transfers between devices, other_side(): return lax.ppermute(value, 'narrow', [(0, 1), (1, 0)])  5.69 us
  transfers between devices with their start and end apart: 31, of which 8 were waited for; matrix products, arithmetic and copies ran while one was open for 1% of the time, Pallas kernels for 43%

profile of v1, /device:TPU:9, one launch (start us, length us, event | category | flops | bytes accessed | tf_op | source)
XLA Modules:
  0.0 142.6 jit_solution(442667123003195409)
XLA Ops:
  7.3 1.5 %collective-permute-start = (bf16[32,4096]{1,0:T(8,128)(2,1)}, bf16[32,4096]{1,0:T(8,128)(2,1)S(1)}, u32[]{:S(2)}, u32[]{:S(2)}) collective-permute-start(bf16[32,4096]{1,0:T(8,128)(2,1)} %refs_1_.1), channel_id=1, source_target_pairs={{0,8},{2,10},{8,16},{10,18},{16,24},{18,26},{24,28},{26,30},{28,20... | collective-permute-start | bytes 786440 | tf_op jit(solution)/shard_map/ppermute | solution.py:213
  8.7 6.6 %products.1.own_ref = f32[32,128]{1,0:T(8,128)} custom-call(bf16[1,128,4096]{2,1,0:T(8,128)(2,1)} %cache_ref.3, f32[1,16,4096]{2,1,0:T(8,128)} %b0.1, bf16[1,128,18560]{2,1,0:T(8,128)(2,1)} %cot_ref.3, f32[1,16,18560]{2,1,0:T(8,128)} %a0.1), custom_call_target="tpu_custom_call" | custom-call | flops 278396928 | bytes 7249920 | tf_op jit(solution)/shard_map/products/pallas_call | solution.py:99
  15.4 1.3 collective-permute-start.15
  16.9 1.2 collective-permute-start.2
  18.1 1.9 %collective-permute-done.2.other_ref = f32[32,128]{1,0:T(8,128)S(1)} collective-permute-done((f32[32,128]{1,0:T(8,128)}, f32[32,128]{1,0:T(8,128)S(1)}, u32[]{:S(2)}, u32[]{:S(2)}) %collective-permute-start.2) | collective-permute-done | bytes 16416 | tf_op jit(solution)/shard_map/ppermute | solution.py:191
  20.6 7.7 %adam.1 = (bf16[16,4096]{1,0:T(8,128)(2,1)}, bf16[8,16,2320]{2,1,0:T(8,128)(2,1)}) custom-call(s32[1,128]{1,0:T(1,128)} %ids_ref.1, f32[32,128]{1,0:T(8,128)} %products.1.own_ref, f32[32,128]{1,0:T(8,128)} %copy-done.29, bf16[1,128,4096]{2,1,0:T(8,128)(2,1)} %cache_ref.3, f32[1,16,4096]{2,1,0:T(8,128)} %b0.1, f32[1,16,4096]{2,1,0:T(8,128)} %b1.1, ...), custom_call_target="tpu_custom_call" | custom-call | flops 278396928 | bytes 10874880 | tf_op jit(solution)/shard_map/adam/pallas_call | solution.py:155
  28.3 1.2 collective-permute-start.3
  29.6 1.3 collective-permute-start.19
  31.0 3.5 %collective-permute-start.12 = (bf16[32,4096]{1,0:T(8,128)(2,1)S(1)}, bf16[32,4096]{1,0:T(8,128)(2,1)S(1)}, u32[]{:S(2)}, u32[]{:S(2)}) collective-permute-start(bf16[32,4096]{1,0:T(8,128)(2,1)S(1)} %copy-done.7), channel_id=1, source_target_pairs={{0,2},{2,0},{4,6},{6,4},{8,10},{10,8},{12,14},{14,12},{16,18},{18,... | collective-permute-start | bytes 786440 | tf_op jit(solution)/shard_map/ppermute | solution.py:187
  35.1 3.8 %collective-permute-start.14 = (bf16[32,4096]{1,0:T(8,128)(2,1)}, bf16[32,4096]{1,0:T(8,128)(2,1)S(1)}, u32[]{:S(2)}, u32[]{:S(2)}) collective-permute-start(bf16[32,4096]{1,0:T(8,128)(2,1)} %copy-done), channel_id=1, source_target_pairs={{0,2},{2,0},{4,6},{6,4},{8,10},{10,8},{12,14},{14,12},{16,18},{18,... | collective-permute-start | bytes 786440 | tf_op jit(solution)/shard_map/ppermute | solution.py:187
  38.9 1.6 %collective-permute-start.16 = (bf16[32,4096]{1,0:T(8,128)(2,1)S(1)}, bf16[32,4096]{1,0:T(8,128)(2,1)S(1)}, u32[]{:S(2)}, u32[]{:S(2)}) collective-permute-start(bf16[32,4096]{1,0:T(8,128)(2,1)S(1)} %collective-permute-done.15.refs_7_), channel_id=1, source_target_pairs={{0,2},{2,0},{4,6},{6,4},{8,10},{10,8},{12,14},{14,12},{16,18},{18,... | collective-permute-start | bytes 786440 | tf_op jit(solution)/shard_map/ppermute | solution.py:187
  40.5 1.4 collective-permute-start.23
  42.7 2.8 %sort_blocks.1 = (bf16[8,16,2320]{2,1,0:T(8,128)(2,1)}, bf16[8,16,2320]{2,1,0:T(8,128)(2,1)}) custom-call(s32[16]{0:T(128)} %owner_ref.1, bf16[8,16,2320]{2,1,0:T(8,128)(2,1)} %get-tuple-element.22.own_ref, bf16[8,16,2320]{2,1,0:T(8,128)(2,1)} %copy-done.3), custom_call_target="tpu_custom_call" | custom-call | bytes 2375680 | tf_op jit(solution)/shard_map/sort_blocks/pallas_call | solution.py:354
  45.5 3.1 %collective-permute-start.18 = (bf16[32,4096]{1,0:T(8,128)(2,1)S(1)}, bf16[32,4096]{1,0:T(8,128)(2,1)S(1)}, u32[]{:S(2)}, u32[]{:S(2)}) collective-permute-start(bf16[32,4096]{1,0:T(8,128)(2,1)S(1)} %collective-permute-done.17.refs_9_), channel_id=1, source_target_pairs={{0,2},{2,0},{4,6},{6,4},{8,10},{10,8},{12,14},{14,12},{16,18},{18,... | collective-permute-start | bytes 786440 | tf_op jit(solution)/shard_map/ppermute | solution.py:187
  49.9 1.2 fusion
  52.2 12.3 %early_projection.2 = (f32[1392,256]{1,0:T(8,128)}, bf16[1392,256]{1,0:T(8,128)(2,1)}, bf16[512,4096]{1,0:T(8,128)(2,1)}) custom-call(bf16[2320,4096]{1,0:T(8,128)(2,1)} %bitcast.3, bf16[32,4096]{1,0:T(8,128)(2,1)} %refs_1_.1, bf16[32,4096]{1,0:T(8,128)(2,1)} %copy-done.10, bf16[32,4096]{1,0:T(8,128)(2,1)} %copy-done.1, bf16[32,4096]{1,0:T(8,128)(2,1)} %copy-done.11, ...), custom_call_target="tpu_custom_call" | custom-call | flops 5838471168 | bytes 17735680 | tf_op jit(solution)/shard_map/early_projection/pallas_call | solution.py:284
  64.6 1.3 collective-permute-start.28
  65.9 8.6 %early_projection.3 = (f32[928,256]{1,0:T(8,128)}, bf16[928,256]{1,0:T(8,128)(2,1)}) custom-call(bf16[2320,4096]{1,0:T(8,128)(2,1)} %bitcast.4, bf16[512,4096]{1,0:T(8,128)(2,1)} %get-tuple-element.26.next_ref.refs_1_), custom_call_target="tpu_custom_call" | custom-call | flops 3892314112 | bytes 13221888 | tf_op jit(solution)/shard_map/early_projection/pallas_call | solution.py:284
  74.5 1.7 %collective-permute-start.5 = (bf16[2,16,2320]{2,1,0:T(8,128)(2,1)S(1)}, bf16[2,16,2320]{2,1,0:T(8,128)(2,1)S(1)}, u32[]{:S(2)}, u32[]{:S(2)}) collective-permute-start(bf16[2,16,2320]{2,1,0:T(8,128)(2,1)S(1)} %pad_maximum_fusion.1), channel_id=1, source_target_pairs={{0,4},{2,6},{4,0},{6,2},{8,12},{10,14},{12,8},{14,10},{16,20},{18,... | collective-permute-start | bytes 445448 | tf_op jit(solution)/shard_map/ppermute | solution.py:187
  76.5 1.1 collective-permute-start.7
  77.7 2.2 %collective-permute-start.8 = (bf16[2,16,2320]{2,1,0:T(8,128)(2,1)S(1)}, bf16[2,16,2320]{2,1,0:T(8,128)(2,1)S(1)}, u32[]{:S(2)}, u32[]{:S(2)}) collective-permute-start(bf16[2,16,2320]{2,1,0:T(8,128)(2,1)S(1)} %pad_maximum_fusion.4), channel_id=1, source_target_pairs={{0,16},{2,18},{4,20},{6,22},{8,24},{10,26},{12,28},{14,30},{16,0},... | collective-permute-start | bytes 445448 | tf_op jit(solution)/shard_map/ppermute | solution.py:187
  79.9 2.1 %collective-permute-done.5.refs_1_ = bf16[2,16,2320]{2,1,0:T(8,128)(2,1)S(1)} collective-permute-done((bf16[2,16,2320]{2,1,0:T(8,128)(2,1)S(1)}, bf16[2,16,2320]{2,1,0:T(8,128)(2,1)S(1)}, u32[]{:S(2)}, u32[]{:S(2)}) %collective-permute-start.5) | collective-permute-done | bytes 148512 | tf_op jit(solution)/shard_map/ppermute | solution.py:187
  82.1 2.0 %collective-permute-start.9 = (bf16[2,16,2320]{2,1,0:T(8,128)(2,1)S(1)}, bf16[2,16,2320]{2,1,0:T(8,128)(2,1)S(1)}, u32[]{:S(2)}, u32[]{:S(2)}) collective-permute-start(bf16[2,16,2320]{2,1,0:T(8,128)(2,1)S(1)} %pad_maximum_fusion.5), channel_id=1, source_target_pairs={{0,20},{2,22},{4,16},{6,18},{8,28},{10,30},{12,24},{14,26},{16,4},... | collective-permute-start | bytes 445448 | tf_op jit(solution)/shard_map/ppermute | solution.py:187
  84.0 6.8 %collective-permute-done.6.refs_2_ = bf16[2,16,2320]{2,1,0:T(8,128)(2,1)S(1)} collective-permute-done((bf16[2,16,2320]{2,1,0:T(8,128)(2,1)S(1)}, bf16[2,16,2320]{2,1,0:T(8,128)(2,1)S(1)}, u32[]{:S(2)}, u32[]{:S(2)}) %collective-permute-start.6) | collective-permute-done | bytes 148512 | tf_op jit(solution)/shard_map/ppermute | solution.py:187
  90.8 3.7 %collective-permute-done.7.refs_3_ = bf16[2,16,2320]{2,1,0:T(8,128)(2,1)S(1)} collective-permute-done((bf16[2,16,2320]{2,1,0:T(8,128)(2,1)S(1)}, bf16[2,16,2320]{2,1,0:T(8,128)(2,1)S(1)}, u32[]{:S(2)}, u32[]{:S(2)}) %collective-permute-start.7) | collective-permute-done | bytes 148512 | tf_op jit(solution)/shard_map/ppermute | solution.py:187
  95.2 0.9 collective-permute-start.29
  96.1 5.1 %low_rank_rows.1 = (f32[256,256]{1,0:T(8,128)}, f32[256,256]{1,0:T(8,128)}) custom-call(bf16[512,4096]{1,0:T(8,128)(2,1)} %get-tuple-element.26.next_ref.refs_1_, bf16[256,4096]{1,0:T(8,128)(2,1)} %all-gather.2.cloned.1.call-done.left_ref), custom_call_target="tpu_custom_call" | custom-call | flops 1073741824 | bytes 6815744 | tf_op jit(solution)/shard_map/low_rank_rows/pallas_call | solution.py:317
  102.2 1.0 collective-permute-start.27
  103.2 4.1 %collective-permute-done.10.refs_6_ = bf16[2,16,2320]{2,1,0:T(8,128)(2,1)S(1)} collective-permute-done((bf16[2,16,2320]{2,1,0:T(8,128)(2,1)S(1)}, bf16[2,16,2320]{2,1,0:T(8,128)(2,1)S(1)}, u32[]{:S(2)}, u32[]{:S(2)}) %collective-permute-start.10) | collective-permute-done | bytes 148512 | tf_op jit(solution)/shard_map/ppermute | solution.py:187
  107.3 3.6 %collective-permute-done.11.refs_7_ = bf16[2,16,2320]{2,1,0:T(8,128)(2,1)S(1)} collective-permute-done((bf16[2,16,2320]{2,1,0:T(8,128)(2,1)S(1)}, bf16[2,16,2320]{2,1,0:T(8,128)(2,1)S(1)}, u32[]{:S(2)}, u32[]{:S(2)}) %collective-permute-start.11) | collective-permute-done | bytes 148512 | tf_op jit(solution)/shard_map/ppermute | solution.py:187
  111.5 18.7 %merge.1 = (bf16[2320,4096]{1,0:T(8,128)(2,1)}, bf16[2320,256]{1,0:T(8,128)(2,1)}) custom-call(bf16[2320,4096]{1,0:T(8,128)(2,1)} %bitcast.5, bf16[256,4096]{1,0:T(8,128)(2,1)} %all-gather.2.cloned.1.call-done.left_ref, bf16[2,16,2320]{2,1,0:T(8,128)(2,1)} %pad_maximum_fusion.refs_0_, bf16[2,16,2320]{2,1,0:T(8,128)(2,1)} %copy-done.18, ...), custom_call_target="tpu_custom_call" | custom-call | flops 4865392640 | bytes 41295872 | tf_op jit(solution)/shard_map/merge/pallas_call | solution.py:396
  131.4 4.4 %finish.1 = bf16[2320,256]{1,0:T(8,128)(2,1)} custom-call(f32[256,256]{1,0:T(8,128)} %get-tuple-element.27.own_low_ref, f32[256,256]{1,0:T(8,128)} %copy-done.17, bf16[2320,256]{1,0:T(8,128)(2,1)} %get-tuple-element.29.turned_ref, f32[1392,256]{1,0:T(8,128)} %get-tuple-element.30.refs_0_, bf16[1392,256]{1,0:T(8,128)(2,1)} %copy-done.2, ...), custom_call_target="tpu_custom_call" | custom-call | flops 608174080 | bytes 5939200 | tf_op jit(solution)/shard_map/finish/pallas_call | solution.py:441
  (113 shorter events, 8.6 us)
Async XLA Ops:
  7.2 89.0 %all-gather.2.cloned.1.call-start = ((), (), s32[]{:S(2)}) async-start(), calls=%async_computation | async-start | bytes 2228224 | tf_op jit(solution)/shard_map/all_gather | solution.py:499
  7.2 8.1 %collective-permute-start.1 = (bf16[32,4096]{1,0:T(8,128)(2,1)}, bf16[32,4096]{1,0:T(8,128)(2,1)S(1)}, u32[]{:S(2)}, u32[]{:S(2)}) collective-permute-start(bf16[32,4096]{1,0:T(8,128)(2,1)} %refs_1_.1), channel_id=1, source_target_pairs={{0,4},{2,6},{8,0},{10,2},{16,8},{18,10},{24,16},{26,18},{28,24},{3... | collective-permute-start | bytes 786440 | tf_op jit(solution)/shard_map/ppermute | solution.py:213
  7.3 8.1 %collective-permute-start = (bf16[32,4096]{1,0:T(8,128)(2,1)}, bf16[32,4096]{1,0:T(8,128)(2,1)S(1)}, u32[]{:S(2)}, u32[]{:S(2)}) collective-permute-start(bf16[32,4096]{1,0:T(8,128)(2,1)} %refs_1_.1), channel_id=1, source_target_pairs={{0,8},{2,10},{8,16},{10,18},{16,24},{18,26},{24,28},{26,30},{28,20... | collective-permute-start | bytes 786440 | tf_op jit(solution)/shard_map/ppermute | solution.py:213
  15.4 14.2 %collective-permute-start.15 = (bf16[32,4096]{1,0:T(8,128)(2,1)S(1)}, bf16[32,4096]{1,0:T(8,128)(2,1)S(1)}, u32[]{:S(2)}, u32[]{:S(2)}) collective-permute-start(bf16[32,4096]{1,0:T(8,128)(2,1)S(1)} %collective-permute-done.rest_0_.refs_3_), channel_id=1, source_target_pairs={{0,8},{2,10},{8,16},{10,18},{16,24},{18,26},{24,28},{26,30},{28,20... | collective-permute-start | bytes 786440 | tf_op jit(solution)/shard_map/ppermute | solution.py:213
  16.7 14.1 %collective-permute-start.17 = (bf16[32,4096]{1,0:T(8,128)(2,1)S(1)}, bf16[32,4096]{1,0:T(8,128)(2,1)S(1)}, u32[]{:S(2)}, u32[]{:S(2)}) collective-permute-start(bf16[32,4096]{1,0:T(8,128)(2,1)S(1)} %collective-permute-done.1.rest_1_.refs_5_), channel_id=1, source_target_pairs={{0,4},{2,6},{8,0},{10,2},{16,8},{18,10},{24,16},{26,18},{28,24},{3... | collective-permute-start | bytes 786440 | tf_op jit(solution)/shard_map/ppermute | solution.py:213
  16.9 3.1 %collective-permute-start.2 = (f32[32,128]{1,0:T(8,128)}, f32[32,128]{1,0:T(8,128)S(1)}, u32[]{:S(2)}, u32[]{:S(2)}) collective-permute-start(f32[32,128]{1,0:T(8,128)} %products.1.own_ref), channel_id=1, source_target_pairs={{0,1},{1,0},{2,3},{3,2},{4,5},{5,4},{6,7},{7,6},{8,9},{9,8},{10,11... | collective-permute-start | bytes 49160 | tf_op jit(solution)/shard_map/ppermute | solution.py:191
  28.3 13.5 %collective-permute-start.3 = (bf16[8,16,2320]{2,1,0:T(8,128)(2,1)}, bf16[8,16,2320]{2,1,0:T(8,128)(2,1)S(1)}, u32[]{:S(2)}, u32[]{:S(2)}) collective-permute-start(bf16[8,16,2320]{2,1,0:T(8,128)(2,1)} %get-tuple-element.22.own_ref), channel_id=1, source_target_pairs={{0,1},{1,0},{2,3},{3,2},{4,5},{5,4},{6,7},{7,6},{8,9},{9,8},{10,11... | collective-permute-start | bytes 1781768 | tf_op jit(solution)/shard_map/ppermute | solution.py:191
  29.6 21.8 %copy-start.8 = (bf16[32,4096]{1,0:T(8,128)(2,1)}, bf16[32,4096]{1,0:T(8,128)(2,1)S(1)}, u32[]{:S(2)}) copy-start(bf16[32,4096]{1,0:T(8,128)(2,1)S(1)} %collective-permute-done.15.refs_7_) | copy-start | bytes 786436
  29.6 5.5 %collective-permute-start.19 = (bf16[32,4096]{1,0:T(8,128)(2,1)S(1)}, bf16[32,4096]{1,0:T(8,128)(2,1)S(1)}, u32[]{:S(2)}, u32[]{:S(2)}) collective-permute-start(bf16[32,4096]{1,0:T(8,128)(2,1)S(1)} %collective-permute-done.15.refs_7_), channel_id=1, source_target_pairs={{0,8},{2,10},{8,16},{10,18},{16,24},{18,26},{24,28},{26,30},{28,20... | collective-permute-start | bytes 786440 | tf_op jit(solution)/shard_map/ppermute | solution.py:213
  30.9 8.0 %collective-permute-start.21 = (bf16[32,4096]{1,0:T(8,128)(2,1)S(1)}, bf16[32,4096]{1,0:T(8,128)(2,1)S(1)}, u32[]{:S(2)}, u32[]{:S(2)}) collective-permute-start(bf16[32,4096]{1,0:T(8,128)(2,1)S(1)} %collective-permute-done.17.refs_9_), channel_id=1, source_target_pairs={{0,4},{2,6},{8,0},{10,2},{16,8},{18,10},{24,16},{26,18},{28,24},{3... | collective-permute-start | bytes 786440 | tf_op jit(solution)/shard_map/ppermute | solution.py:213
  31.0 9.4 %collective-permute-start.12 = (bf16[32,4096]{1,0:T(8,128)(2,1)S(1)}, bf16[32,4096]{1,0:T(8,128)(2,1)S(1)}, u32[]{:S(2)}, u32[]{:S(2)}) collective-permute-start(bf16[32,4096]{1,0:T(8,128)(2,1)S(1)} %copy-done.7), channel_id=1, source_target_pairs={{0,2},{2,0},{4,6},{6,4},{8,10},{10,8},{12,14},{14,12},{16,18},{18,... | collective-permute-start | bytes 786440 | tf_op jit(solution)/shard_map/ppermute | solution.py:187
  34.5 10.9 %collective-permute-start.13 = (bf16[32,4096]{1,0:T(8,128)(2,1)}, bf16[32,4096]{1,0:T(8,128)(2,1)S(1)}, u32[]{:S(2)}, u32[]{:S(2)}) collective-permute-start(bf16[32,4096]{1,0:T(8,128)(2,1)} %copy-done.1), channel_id=1, source_target_pairs={{0,2},{2,0},{4,6},{6,4},{8,10},{10,8},{12,14},{14,12},{16,18},{18,... | collective-permute-start | bytes 786440 | tf_op jit(solution)/shard_map/ppermute | solution.py:187
  35.1 13.5 %collective-permute-start.14 = (bf16[32,4096]{1,0:T(8,128)(2,1)}, bf16[32,4096]{1,0:T(8,128)(2,1)S(1)}, u32[]{:S(2)}, u32[]{:S(2)}) collective-permute-start(bf16[32,4096]{1,0:T(8,128)(2,1)} %copy-done), channel_id=1, source_target_pairs={{0,2},{2,0},{4,6},{6,4},{8,10},{10,8},{12,14},{14,12},{16,18},{18,... | collective-permute-start | bytes 786440 | tf_op jit(solution)/shard_map/ppermute | solution.py:187
  38.9 9.8 %collective-permute-start.16 = (bf16[32,4096]{1,0:T(8,128)(2,1)S(1)}, bf16[32,4096]{1,0:T(8,128)(2,1)S(1)}, u32[]{:S(2)}, u32[]{:S(2)}) collective-permute-start(bf16[32,4096]{1,0:T(8,128)(2,1)S(1)} %collective-permute-done.15.refs_7_), channel_id=1, source_target_pairs={{0,2},{2,0},{4,6},{6,4},{8,10},{10,8},{12,14},{14,12},{16,18},{18,... | collective-permute-start | bytes 786440 | tf_op jit(solution)/shard_map/ppermute | solution.py:187
  40.5 8.6 %collective-permute-start.23 = (bf16[16,4096]{1,0:T(8,128)(2,1)S(1)}, bf16[16,4096]{1,0:T(8,128)(2,1)S(1)}, u32[]{:S(2)}, u32[]{:S(2)}) collective-permute-start(bf16[16,4096]{1,0:T(8,128)(2,1)S(1)} %slice.80), channel_id=1, source_target_pairs={{0,8},{2,10},{8,16},{10,18},{16,24},{18,26},{24,28},{26,30},{28,20... | collective-permute-start | bytes 393224 | tf_op jit(solution)/shard_map/ppermute | solution.py:213
  41.9 7.4 %collective-permute-start.25 = (bf16[16,4096]{1,0:T(8,128)(2,1)S(1)}, bf16[16,4096]{1,0:T(8,128)(2,1)S(1)}, u32[]{:S(2)}, u32[]{:S(2)}) collective-permute-start(bf16[16,4096]{1,0:T(8,128)(2,1)S(1)} %slice.81), channel_id=1, source_target_pairs={{0,4},{2,6},{8,0},{10,2},{16,8},{18,10},{24,16},{26,18},{28,24},{3... | collective-permute-start | bytes 393224 | tf_op jit(solution)/shard_map/ppermute | solution.py:213
  45.5 5.7 %collective-permute-start.18 = (bf16[32,4096]{1,0:T(8,128)(2,1)S(1)}, bf16[32,4096]{1,0:T(8,128)(2,1)S(1)}, u32[]{:S(2)}, u32[]{:S(2)}) collective-permute-start(bf16[32,4096]{1,0:T(8,128)(2,1)S(1)} %collective-permute-done.17.refs_9_), channel_id=1, source_target_pairs={{0,2},{2,0},{4,6},{6,4},{8,10},{10,8},{12,14},{14,12},{16,18},{18,... | collective-permute-start | bytes 786440 | tf_op jit(solution)/shard_map/ppermute | solution.py:187
  48.6 2.7 %collective-permute-start.20 = (bf16[32,4096]{1,0:T(8,128)(2,1)S(1)}, bf16[32,4096]{1,0:T(8,128)(2,1)S(1)}, u32[]{:S(2)}, u32[]{:S(2)}) collective-permute-start(bf16[32,4096]{1,0:T(8,128)(2,1)S(1)} %collective-permute-done.19.refs_11_), channel_id=1, source_target_pairs={{0,2},{2,0},{4,6},{6,4},{8,10},{10,8},{12,14},{14,12},{16,18},{18,... | collective-permute-start | bytes 786440 | tf_op jit(solution)/shard_map/ppermute | solution.py:187
  48.7 2.6 %collective-permute-start.22 = (bf16[32,4096]{1,0:T(8,128)(2,1)S(1)}, bf16[32,4096]{1,0:T(8,128)(2,1)S(1)}, u32[]{:S(2)}, u32[]{:S(2)}) collective-permute-start(bf16[32,4096]{1,0:T(8,128)(2,1)S(1)} %collective-permute-done.21.refs_13_), channel_id=1, source_target_pairs={{0,2},{2,0},{4,6},{6,4},{8,10},{10,8},{12,14},{14,12},{16,18},{18,... | collective-permute-start | bytes 786440 | tf_op jit(solution)/shard_map/ppermute | solution.py:187
  49.1 2.2 %collective-permute-start.24 = (bf16[16,4096]{1,0:T(8,128)(2,1)S(1)}, bf16[16,4096]{1,0:T(8,128)(2,1)S(1)}, u32[]{:S(2)}, u32[]{:S(2)}) collective-permute-start(bf16[16,4096]{1,0:T(8,128)(2,1)S(1)} %collective-permute-done.23.refs_15_), channel_id=1, source_target_pairs={{0,2},{2,0},{4,6},{6,4},{8,10},{10,8},{12,14},{14,12},{16,18},{18,... | collective-permute-start | bytes 393224 | tf_op jit(solution)/shard_map/ppermute | solution.py:187
  49.2 2.1 %collective-permute-start.26 = (bf16[16,4096]{1,0:T(8,128)(2,1)S(1)}, bf16[16,4096]{1,0:T(8,128)(2,1)S(1)}, u32[]{:S(2)}, u32[]{:S(2)}) collective-permute-start(bf16[16,4096]{1,0:T(8,128)(2,1)S(1)} %collective-permute-done.25.refs_17_), channel_id=1, source_target_pairs={{0,2},{2,0},{4,6},{6,4},{8,10},{10,8},{12,14},{14,12},{16,18},{18,... | collective-permute-start | bytes 393224 | tf_op jit(solution)/shard_map/ppermute | solution.py:187
  51.2 23.3 %collective-permute-start.4 = (bf16[8,16,2320]{2,1,0:T(8,128)(2,1)}, bf16[8,16,2320]{2,1,0:T(8,128)(2,1)S(1)}, u32[]{:S(2)}, u32[]{:S(2)}) collective-permute-start(bf16[8,16,2320]{2,1,0:T(8,128)(2,1)} %get-tuple-element.24), channel_id=1, source_target_pairs={{0,2},{2,0},{4,6},{6,4},{8,10},{10,8},{12,14},{14,12},{16,18},{18,... | collective-permute-start | bytes 1781768 | tf_op jit(solution)/shard_map/ppermute | solution.py:187
  64.6 65.7 %collective-permute-start.28 = (bf16[1392,256]{1,0:T(8,128)(2,1)}, bf16[1392,256]{1,0:T(8,128)(2,1)S(1)}, u32[]{:S(2)}, u32[]{:S(2)}) collective-permute-start(bf16[1392,256]{1,0:T(8,128)(2,1)} %get-tuple-element.31), channel_id=1, source_target_pairs={{0,1},{1,0},{2,3},{3,2},{4,5},{5,4},{6,7},{7,6},{8,9},{9,8},{10,11... | collective-permute-start | bytes 2138120 | tf_op jit(solution)/shard_map/ppermute | solution.py:191
  74.5 7.5 %collective-permute-start.5 = (bf16[2,16,2320]{2,1,0:T(8,128)(2,1)S(1)}, bf16[2,16,2320]{2,1,0:T(8,128)(2,1)S(1)}, u32[]{:S(2)}, u32[]{:S(2)}) collective-permute-start(bf16[2,16,2320]{2,1,0:T(8,128)(2,1)S(1)} %pad_maximum_fusion.1), channel_id=1, source_target_pairs={{0,4},{2,6},{4,0},{6,2},{8,12},{10,14},{12,8},{14,10},{16,20},{18,... | collective-permute-start | bytes 445448 | tf_op jit(solution)/shard_map/ppermute | solution.py:187
  76.3 14.5 %collective-permute-start.6 = (bf16[2,16,2320]{2,1,0:T(8,128)(2,1)S(1)}, bf16[2,16,2320]{2,1,0:T(8,128)(2,1)S(1)}, u32[]{:S(2)}, u32[]{:S(2)}) collective-permute-start(bf16[2,16,2320]{2,1,0:T(8,128)(2,1)S(1)} %pad_maximum_fusion.2), channel_id=1, source_target_pairs={{0,8},{2,10},{4,12},{6,14},{8,0},{10,2},{12,4},{14,6},{16,24},{18,... | collective-permute-start | bytes 445448 | tf_op jit(solution)/shard_map/ppermute | solution.py:187
  76.5 17.9 %collective-permute-start.7 = (bf16[2,16,2320]{2,1,0:T(8,128)(2,1)S(1)}, bf16[2,16,2320]{2,1,0:T(8,128)(2,1)S(1)}, u32[]{:S(2)}, u32[]{:S(2)}) collective-permute-start(bf16[2,16,2320]{2,1,0:T(8,128)(2,1)S(1)} %pad_maximum_fusion.3), channel_id=1, source_target_pairs={{0,12},{2,14},{4,8},{6,10},{8,4},{10,6},{12,0},{14,2},{16,28},{18,... | collective-permute-start | bytes 445448 | tf_op jit(solution)/shard_map/ppermute | solution.py:187
  77.7 17.5 %collective-permute-start.8 = (bf16[2,16,2320]{2,1,0:T(8,128)(2,1)S(1)}, bf16[2,16,2320]{2,1,0:T(8,128)(2,1)S(1)}, u32[]{:S(2)}, u32[]{:S(2)}) collective-permute-start(bf16[2,16,2320]{2,1,0:T(8,128)(2,1)S(1)} %pad_maximum_fusion.4), channel_id=1, source_target_pairs={{0,16},{2,18},{4,20},{6,22},{8,24},{10,26},{12,28},{14,30},{16,0},... | collective-permute-start | bytes 445448 | tf_op jit(solution)/shard_map/ppermute | solution.py:187
  82.1 20.1 %collective-permute-start.9 = (bf16[2,16,2320]{2,1,0:T(8,128)(2,1)S(1)}, bf16[2,16,2320]{2,1,0:T(8,128)(2,1)S(1)}, u32[]{:S(2)}, u32[]{:S(2)}) collective-permute-start(bf16[2,16,2320]{2,1,0:T(8,128)(2,1)S(1)} %pad_maximum_fusion.5), channel_id=1, source_target_pairs={{0,20},{2,22},{4,16},{6,18},{8,28},{10,30},{12,24},{14,26},{16,4},... | collective-permute-start | bytes 445448 | tf_op jit(solution)/shard_map/ppermute | solution.py:187
  90.8 16.5 %collective-permute-start.10 = (bf16[2,16,2320]{2,1,0:T(8,128)(2,1)S(1)}, bf16[2,16,2320]{2,1,0:T(8,128)(2,1)S(1)}, u32[]{:S(2)}, u32[]{:S(2)}) collective-permute-start(bf16[2,16,2320]{2,1,0:T(8,128)(2,1)S(1)} %pad_maximum_fusion.6), channel_id=1, source_target_pairs={{0,24},{2,26},{4,28},{6,30},{8,16},{10,18},{12,20},{14,22},{16,8},... | collective-permute-start | bytes 445448 | tf_op jit(solution)/shard_map/ppermute | solution.py:187
  94.4 16.4 %collective-permute-start.11 = (bf16[2,16,2320]{2,1,0:T(8,128)(2,1)S(1)}, bf16[2,16,2320]{2,1,0:T(8,128)(2,1)S(1)}, u32[]{:S(2)}, u32[]{:S(2)}) collective-permute-start(bf16[2,16,2320]{2,1,0:T(8,128)(2,1)S(1)} %pad_maximum_fusion.7), channel_id=1, source_target_pairs={{0,28},{2,30},{4,24},{6,26},{8,20},{10,22},{12,16},{14,18},{16,12}... | collective-permute-start | bytes 445448 | tf_op jit(solution)/shard_map/ppermute | solution.py:187
  95.2 35.0 %collective-permute-start.29 = (bf16[928,256]{1,0:T(8,128)(2,1)S(1)}, bf16[928,256]{1,0:T(8,128)(2,1)S(1)}, u32[]{:S(2)}, u32[]{:S(2)}) collective-permute-start(bf16[928,256]{1,0:T(8,128)(2,1)S(1)} %copy-done.30), channel_id=1, source_target_pairs={{0,1},{1,0},{2,3},{3,2},{4,5},{5,4},{6,7},{7,6},{8,9},{9,8},{10,11... | collective-permute-start | bytes 1425416 | tf_op jit(solution)/shard_map/ppermute | solution.py:191
  102.2 28.1 %collective-permute-start.27 = (f32[256,256]{1,0:T(8,128)}, f32[256,256]{1,0:T(8,128)S(1)}, u32[]{:S(2)}, u32[]{:S(2)}) collective-permute-start(f32[256,256]{1,0:T(8,128)} %get-tuple-element.28), channel_id=1, source_target_pairs={{0,1},{1,0},{2,3},{3,2},{4,5},{5,4},{6,7},{7,6},{8,9},{9,8},{10,11... | collective-permute-start | bytes 786440 | tf_op jit(solution)/shard_map/ppermute | solution.py:191
  (30 other events, 185.0 us)
Sparse Core Ops, SparseCore 0:
  42.2 48.9 all-gather.1

commit v2 on v1

v2 whole, which is shorter than its diff:
```python
import functools
import math

import jax
import jax.numpy as jnp
from jax import lax
from jax.experimental import pallas as pl
from jax.experimental.pallas import tpu as pltpu
from jax.sharding import PartitionSpec as P

adapter_scale = 4.0
rate = 0.2
beta_one = 0.9
beta_two = 0.999
bias_one = 1.0 - 0.9**20
bias_two = 1.0 - 0.999**20
eps_adam = 1e-08

F32 = jnp.float32
BF16 = jnp.bfloat16
MIB = 1024 * 1024


def adam_step(param, first, second, grad):
    first_new = beta_one * first + (1.0 - beta_one) * grad
    second_new = beta_two * second + (1.0 - beta_two) * grad * grad
    root = jnp.sqrt(second_new * (1.0 / bias_two)) + eps_adam
    return (param - (rate / bias_one) * first_new / root).astype(BF16)


def plain_call(kernel, flops, moved, limit, weight=1, **kw):
    return pl.pallas_call(
        kernel,
        compiler_params=pltpu.CompilerParams(vmem_limit_bytes=limit * MIB),
        cost_estimate=pl.CostEstimate(flops=weight * flops, bytes_accessed=moved, transcendentals=0),
        **kw,
    )


def in_vmem():
    return pl.BlockSpec(memory_space=pltpu.VMEM)


def split(value):
    top = value.astype(BF16)
    left = value - top.astype(F32)
    middle = left.astype(BF16)
    bottom = (left - middle.astype(F32)).astype(BF16)
    return jnp.concatenate([top, middle, bottom], axis=0)


def fold(value):
    rows = value.shape[0] // 3
    return value[:rows] + (value[rows : 2 * rows] + value[2 * rows :])


def dot_rows(value, other):
    return fold(
        lax.dot_general(
            value, split(other), (((1,), (1,)), ((), ())), preferred_element_type=F32
        ).T
    )


def dot_plain(parts, other):
    return fold(jnp.dot(parts, other, preferred_element_type=F32))


def column_tile(columns, most):
    count = columns // 128
    best = max(d for d in range(1, count + 1) if count % d == 0 and d * 128 <= most)
    return best * 128


def row_tile(rows, most):
    return max(d for d in range(16, most + 1, 16) if rows % d == 0)


def products(cache, factor_b, cotangent, factor_a):
    rank, columns = factor_a.shape
    tokens = cotangent.shape[0]
    pool, features = cache.shape

    tile = column_tile(columns, 4096)

    def kernel(cache_ref, b_ref, cot_ref, a_ref, out_ref):
        value = dot_rows(cot_ref[...], a_ref[...])

        @pl.when(pl.program_id(0) == 0)
        def _():
            out_ref[:rank] = dot_rows(cache_ref[...], b_ref[...])
            out_ref[rank:] = value

        @pl.when(pl.program_id(0) > 0)
        def _():
            out_ref[rank:] += value

    fixed = lambda i: (0, 0)
    return plain_call(
        kernel,
        6 * rank * (tokens * columns + pool * features),
        2 * tokens * columns + 4 * rank * columns + 2 * pool * features + 4 * rank * features,
        8,
        512,
        grid=(columns // tile,),
        in_specs=[
            pl.BlockSpec((pool, features), fixed),
            pl.BlockSpec((rank, features), fixed),
            pl.BlockSpec((tokens, tile), lambda i: (0, i)),
            pl.BlockSpec((rank, tile), lambda i: (0, i)),
        ],
        out_specs=pl.BlockSpec((2 * rank, tokens), fixed),
        out_shape=jax.ShapeDtypeStruct((2 * rank, tokens), F32),
        name="products",
    )(cache, factor_b, cotangent, factor_a)


def adam(ids, own, other, cache, b_set, cotangent, a_set, block_cols, inverse_root, early):
    rank, columns = a_set[0].shape
    tokens = cotangent.shape[0]
    pool, features = cache.shape
    tile = column_tile(columns, 4096)
    blocks = columns // block_cols

    def kernel(ids_ref, own_ref, other_ref, cache_ref, b0, b1, b2, cot_ref, a0, a1, a2, *rest):
        out_b, out_a, whole = rest[1:]
        sums = own_ref[...] + other_ref[...]
        chosen = lax.broadcasted_iota(jnp.int32, (pool, tokens), 0) == ids_ref[...]
        chosen = chosen.astype(F32).astype(BF16)
        hidden = split(dot_plain(split(sums[:rank] * inverse_root), chosen))
        upstream = split(
            fold(
                lax.dot_general(
                    split(sums[rank:]), chosen, (((1,), (1,)), ((), ())), preferred_element_type=F32
                )
            )
        )
        grad = (adapter_scale * inverse_root / tokens) * dot_plain(upstream, cache_ref[...])
        out_b[...] = adam_step(b0[...], b1[...], b2[...], grad)
        for at in range(0, columns, tile):
            part = slice(at, at + tile)
            grad = (adapter_scale / tokens) * dot_plain(hidden, cot_ref[:, part])
            whole[:, part] = adam_step(a0[:, part], a1[:, part], a2[:, part], grad)
        for c in range(blocks):
            out_a[c] = whole[:, c * block_cols : (c + 1) * block_cols]

    return plain_call(
        kernel,
        6 * rank * (tokens * columns + pool * features),
        2 * tokens * columns + 14 * rank * columns + 2 * pool * features + 14 * rank * features,
        10,
        64,
        in_specs=[in_vmem()] * 12,
        out_specs=[in_vmem()] * 2,
        out_shape=[
            jax.ShapeDtypeStruct((rank, features), BF16),
            jax.ShapeDtypeStruct((blocks, rank, block_cols), BF16),
        ],
        scratch_shapes=[pltpu.VMEM((rank, columns), BF16)],
        name="adam",
    )(ids, own, other, cache, *b_set, cotangent, *a_set, early)


def across(value, wide, flip):
    return lax.ppermute(value, "wide", [(i, i ^ flip) for i in range(wide)])


def other_side(value):
    return lax.ppermute(value, "narrow", [(0, 1), (1, 0)])


def ring_pair(at, pairs):
    return jnp.where(at < pairs // 2, 2 * at, 2 * pairs - 1 - 2 * at)


def ring_place(pair, pairs):
    return jnp.where(pair % 2 == 0, pair // 2, pairs - 1 - pair // 2)


def ring_links(wide, step):
    pairs = wide // 2
    order = list(range(0, pairs, 2)) + list(range(pairs - 1, 0, -2))
    return [
        (2 * pair + core, 2 * order[(at + step) % pairs] + core)
        for at, pair in enumerate(order)
        for core in (0, 1)
    ]


def along(value, wide, step):
    return lax.ppermute(value, "wide", ring_links(wide, step))


def piece_plan(wide):
    pairs = wide // 2
    plan = [0]
    for step in range(1, pairs // 2):
        plan += [-step, step]
    return plan + [pairs // 2]


def order_rows(pieces, plan, wide, by_side):
    rows, depth = pieces[0].shape
    total = wide * rows
    half = total // 2
    pairs = wide // 2

    def kernel(*refs):
        side = lax.axis_index("narrow") if by_side else 0
        device = lax.axis_index("wide")
        at = ring_place(device // 2, pairs)
        for i, ref in enumerate(refs[:-1]):
            pair = ring_pair((at + plan[i // 2] + pairs) % pairs, pairs)
            source = 2 * pair + (device + i) % 2
            row = ((source // pairs + side) % 2) * half + (source % pairs) * rows
            refs[-1][pl.ds(pl.multiple_of(row, 16), ref.shape[0]), :] = ref[...]

    return plain_call(
        kernel,
        0,
        4 * total * depth,
        4,
        in_specs=[in_vmem()] * len(pieces),
        out_specs=in_vmem(),
        out_shape=jax.ShapeDtypeStruct((total, depth), BF16),
        name="order_rows",
    )(*pieces)


def early_projection(resident, all_next, first, last, away):
    columns, depth = resident.shape
    half = all_next.shape[0] // 2
    kind = BF16 if away else F32

    def kernel(res_ref, rows_ref, out_ref):
        out_ref[...] = lax.dot_general(
            res_ref[first:last],
            rows_ref[away * half : (away + 1) * half],
            (((1,), (1,)), ((), ())),
            preferred_element_type=F32,
        ).astype(kind)

    return plain_call(
        kernel,
        2 * half * depth * (last - first),
        2 * depth * (last - first + half) + 4 * half * (last - first),
        16,
        in_specs=[in_vmem()] * 2,
        out_specs=in_vmem(),
        out_shape=jax.ShapeDtypeStruct((last - first, half), kind),
        name="early_projection",
    )(resident, all_next)


def low_rank_rows(all_next, left):
    total, depth = all_next.shape
    ranks = left.shape[0]
    half = total // 2

    def kernel(next_ref, left_ref, own_ref, away_ref):
        value = lax.dot_general(
            left_ref[...], next_ref[...], (((1,), (1,)), ((), ())), preferred_element_type=F32
        )
        own_ref[...] = value[:, :half]
        away_ref[...] = value[:, half:]

    return plain_call(
        kernel,
        2 * total * depth * ranks,
        2 * depth * (total + ranks) + 4 * total * ranks,
        4,
        64,
        in_specs=[in_vmem()] * 2,
        out_specs=[in_vmem()] * 2,
        out_shape=[jax.ShapeDtypeStruct((ranks, half), F32)] * 2,
        name="low_rank_rows",
    )(all_next, left)


def sort_blocks(block_owner, own, other, wide):
    blocks, rank, block_cols = own.shape
    pairs = wide // 2

    def kernel(owner_ref, own_ref, other_ref, mine_ref, yours_ref):
        side = lax.axis_index("narrow")
        device = lax.axis_index("wide")
        core = device % 2
        for flip in range(pairs):
            for o, out_ref in ((0, mine_ref), (1, yours_ref)):
                block = owner_ref[2 * ((device // 2) ^ flip) + (core + o) % 2]
                here = block // blocks == side

                @pl.when(here)
                def _():
                    out_ref[flip] = own_ref[block % blocks]

                @pl.when(jnp.logical_not(here))
                def _():
                    out_ref[flip] = other_ref[block % blocks]

    shape = jax.ShapeDtypeStruct((pairs, rank, block_cols), own.dtype)
    return plain_call(
        kernel,
        0,
        8 * pairs * rank * block_cols,
        4,
        in_specs=[pl.BlockSpec(memory_space=pltpu.SMEM), in_vmem(), in_vmem()],
        out_specs=[in_vmem(), in_vmem()],
        out_shape=[shape, shape],
        name="sort_blocks",
    )(block_owner, own, other)


def pair_blocks(mine, handed):
    pairs, rank, block_cols = mine.shape

    def kernel(mine_ref, handed_ref, *out_refs):
        for flip, ref in enumerate(out_refs):
            ref[0] = mine_ref[flip]
            ref[1] = handed_ref[flip]

    return plain_call(
        kernel,
        0,
        8 * pairs * rank * block_cols,
        4,
        in_specs=[in_vmem()] * 2,
        out_specs=[in_vmem()] * pairs,
        out_shape=[jax.ShapeDtypeStruct((2, rank, block_cols), mine.dtype)] * pairs,
        name="pair_blocks",
    )(mine, handed)


def merge(resident, left, pieces, scale):
    columns, depth = resident.shape
    ranks = left.shape[0]
    rank = pieces[0].shape[1]
    tile = row_tile(columns, 512)
    count = len(pieces)

    def kernel(res_ref, left_ref, *refs):
        out_ref, turned_ref, right_ref = refs[count:]
        step = pl.program_id(0)

        @pl.when(step == 0)
        def _():
            device = lax.axis_index("wide")
            for flip, ref in enumerate(refs[:count]):
                for o in (0, 1):
                    worker = 2 * ((device // 2) ^ flip) + (device + o) % 2
                    right_ref[pl.ds(pl.multiple_of(worker * rank, rank), rank), :] = ref[o]
            for at in range(0, columns, 256):
                width = min(256, columns - at)
                unit = lax.broadcasted_iota(jnp.int32, (width, width), 0)
                unit = unit == lax.broadcasted_iota(jnp.int32, (width, width), 1)
                turned_ref[at : at + width] = (
                    scale
                    * lax.dot_general(
                        unit.astype(F32).astype(BF16),
                        right_ref[:, at : at + width],
                        (((1,), (1,)), ((), ())),
                        preferred_element_type=F32,
                    )
                ).astype(BF16)

        rows = pl.ds(pl.multiple_of(step * tile, 16), tile)
        for at in range(0, depth, depth // 4):
            cols = slice(at, at + depth // 4)
            delta = jnp.dot(turned_ref[rows, :], left_ref[:, cols], preferred_element_type=F32)
            out_ref[:, cols] = (res_ref[rows, cols].astype(F32) + delta).astype(BF16)

    return plain_call(
        kernel,
        2 * depth * columns * ranks,
        4 * depth * columns + 2 * ranks * (depth + columns),
        16,
        grid=(columns // tile,),
        in_specs=[in_vmem()] * (2 + count),
        out_specs=[pl.BlockSpec((tile, depth), lambda i: (i, 0)), in_vmem()],
        out_shape=[
            jax.ShapeDtypeStruct((columns, depth), BF16),
            jax.ShapeDtypeStruct((columns, ranks), BF16),
        ],
        scratch_shapes=[pltpu.VMEM((ranks, columns), BF16)],
        name="merge",
    )(resident, left, *pieces)


def finish(own_part, others, low_own, low_other, turned, inverse_root):
    ranks, half = low_own.shape
    columns = turned.shape[0]

    def kernel(own_low_ref, other_low_ref, turned_ref, own_ref, *refs):
        out_ref = refs[-1]
        low = own_low_ref[...] + other_low_ref[...]
        high = low.astype(BF16)
        rest = (low - high.astype(F32)).astype(BF16)
        at = 0
        for other in refs[:-1]:
            part = slice(at, at + other.shape[0])
            shift = jnp.dot(turned_ref[part], high, preferred_element_type=F32) + jnp.dot(
                turned_ref[part], rest, preferred_element_type=F32
            )
            out_ref[part] = (
                (own_ref[part] + other[...].astype(F32) + shift) * inverse_root
            ).astype(BF16)
            at += other.shape[0]

    return plain_call(
        kernel,
        4 * half * ranks * columns,
        8 * half * columns + 2 * ranks * columns,
        8,
        in_specs=[in_vmem()] * (4 + len(others)),
        out_specs=in_vmem(),
        out_shape=jax.ShapeDtypeStruct((columns, half), BF16),
        name="finish",
    )(low_own, low_other, turned, own_part, *others)


def per_device(
    activation_cache,
    token_ids,
    cotangent,
    adapter_b,
    first_b,
    second_b,
    adapter_a,
    first_a,
    second_a,
    resident,
    block_owner,
    next_rows,
):
    inverse_root = 1.0 / math.sqrt(2 * next_rows.shape[1])
    wide = lax.axis_size("wide")
    pairs = wide // 2
    resident = resident.T
    block_cols = resident.shape[0]
    cache, incoming = activation_cache[0], cotangent[0]
    scale = adapter_scale / wide
    hold = lax.optimization_barrier

    plan = piece_plan(wide)
    pieces = [next_rows, across(next_rows, wide, 1)]

    def keep(pieces, *blocks):
        for block in blocks:
            pieces.extend([block, across(block, wide, 1)])

    def both_ways(ahead, behind):
        return along(ahead, wide, 1), along(behind, wide, -1)

    step_1 = both_ways(next_rows, next_rows)
    own_sums = products(cache, adapter_b[0], incoming, adapter_a[0])
    step_1, own_sums = hold((step_1, own_sums))
    keep(pieces, *step_1)
    other_sums = other_side(own_sums)
    step_2 = both_ways(*step_1)
    step_2, other_sums = hold((step_2, other_sums))
    keep(pieces, *step_2)
    new_b, own_blocks = adam(
        token_ids,
        own_sums,
        other_sums,
        cache,
        (adapter_b[0], first_b[0], second_b[0]),
        incoming,
        (adapter_a[0], first_a[0], second_a[0]),
        block_cols,
        inverse_root,
        resident,
    )
    left_pieces = [new_b, across(new_b, wide, 1)]
    other_blocks = other_side(own_blocks)
    step_3 = both_ways(*step_2)
    left_1 = both_ways(new_b, new_b)
    step_3, left_1 = hold((step_3, left_1))
    keep(pieces, *step_3)
    keep(left_pieces, *left_1)
    step_4 = along(step_3[0], wide, 1)
    left_2 = both_ways(*left_1)
    step_4, left_2, other_blocks = hold((step_4, left_2, other_blocks))
    keep(pieces, step_4)
    keep(left_pieces, *left_2)
    left_3 = both_ways(*left_2)
    keep(left_pieces, *left_3)
    keep(left_pieces, along(left_3[0], wide, 1))
    all_next = order_rows(pieces, plan, wide, True)
    left = order_rows(left_pieces, plan, wide, False)

    mine, yours = sort_blocks(block_owner, own_blocks, other_blocks, wide)
    handed = across(yours, wide, 1)
    right = list(pair_blocks(mine, handed))
    for flip in range(1, pairs):
        right[flip] = across(right[flip], wide, 2 * flip)

    cut = -(-block_cols // 32) * 16
    got_0 = other_side(early_projection(resident, all_next, 0, cut, 1))
    got_1 = other_side(early_projection(resident, all_next, cut, block_cols, 1))
    all_next, right[1], right[2], right[3] = hold(
        (all_next, right[1], right[2], right[3])
    )
    own_part = early_projection(resident, all_next, 0, block_cols, 0)
    low_own, low_away = low_rank_rows(all_next, left)
    low_other = other_side(low_away)
    merged, turned = merge(resident, left, right, scale)
    projected = finish(own_part, (got_0, got_1), low_own, low_other, turned, inverse_root)
    return (merged.T, projected.T)


def any_mesh(
    activation_cache,
    token_ids,
    cotangent,
    adapter_b,
    first_b,
    second_b,
    adapter_a,
    first_a,
    second_a,
    resident,
    block_owner,
    next_rows,
):
    inverse_root = 1.0 / math.sqrt(next_rows.shape[1] * lax.axis_size("narrow"))
    highest_precision = lax.Precision.HIGHEST
    worker_group = lax.axis_size("wide")
    block_cols = resident.shape[1]
    selected_rows = jnp.take(activation_cache[0], token_ids[0], axis=0).astype(jnp.float32)
    incoming_gradient = cotangent[0].astype(jnp.float32)
    factor_b = adapter_b[0]
    factor_a = adapter_a[0]
    part_hidden = jnp.dot(selected_rows, factor_b.T, precision=highest_precision)
    part_upstream = jnp.dot(incoming_gradient, factor_a.T, precision=highest_precision)
    hidden_state, upstream_gradient = lax.psum((part_hidden, part_upstream), "narrow")
    hidden_state = hidden_state * inverse_root
    gradient_left = (
        adapter_scale
        / token_ids.shape[1]
        * jnp.dot(hidden_state.T, incoming_gradient, precision=highest_precision)
    )
    gradient_right = (
        adapter_scale
        * inverse_root
        / token_ids.shape[1]
        * jnp.dot(upstream_gradient.T, selected_rows, precision=highest_precision)
    )
    new_b = adam_step(factor_b, first_b[0], second_b[0], gradient_right)
    new_a = adam_step(factor_a, first_a[0], second_a[0], gradient_left)
    full_a = lax.all_gather(new_a, "narrow", axis=1, tiled=True)
    blocks = full_a.reshape(full_a.shape[0], worker_group, block_cols)
    ordered = jnp.take(blocks, block_owner, axis=1)
    arrived = lax.all_to_all(ordered, "wide", split_axis=1, concat_axis=0, tiled=True)
    right_rows = arrived.reshape(worker_group * full_a.shape[0], block_cols)
    weight_change = lax.dot_general(
        lax.all_gather(new_b, "wide", axis=0, tiled=True),
        right_rows,
        (((0,), (0,)), ((), ())),
        preferred_element_type=jnp.float32,
    )
    merged = (resident.astype(jnp.float32) + adapter_scale / worker_group * weight_change).astype(
        jnp.bfloat16
    )
    all_next = lax.all_gather(next_rows, "wide", axis=0, tiled=True)
    summed = lax.psum_scatter(
        jnp.dot(all_next, merged, preferred_element_type=jnp.float32),
        "narrow",
        scatter_dimension=0,
        tiled=True,
    )
    projected = (summed * inverse_root).astype(jnp.bfloat16)
    return (merged, projected)


def solution(mesh):
    paired = mesh.shape["narrow"] == 2 and mesh.shape["wide"] == 16
    return jax.shard_map(
        per_device if paired else any_mesh,
        mesh=mesh,
        in_specs=(
            P("wide", None, "narrow"),
            P("wide", None),
            P("wide", None, "narrow"),
            P("wide", None, "narrow"),
            P("wide", None, "narrow"),
            P("wide", None, "narrow"),
            P("wide", None, "narrow"),
            P("wide", None, "narrow"),
            P("wide", None, "narrow"),
            P("narrow", "wide"),
            P(),
            P("wide", "narrow"),
        ),
        out_specs=(P("narrow", "wide"), P("narrow", "wide")),
        check_vma=False,
    )
```

time: 143 us -> 107 us (0.75)
  Pallas kernels: 66.2 us -> 30.2 us
  between operations: 14.4 us -> 0.95 us
  waiting for transfers between devices: 23.6 us -> 32.8 us
  starting transfers between devices: 32.4 us -> 35.7 us
    pallas_call x3 -> x7, Pallas kernels: 23.7 us -> 12.4 us  [the longest x3 10.6 us: early_projection(): plain_call(kernel, 2 * half * depth * (last - first), 2 * depth * (last -...]
    ppermute x8 -> x14, waiting for transfers between devices: 0.56 us -> 11.8 us  [along(): return lax.ppermute(value, 'wide', ring_links(wide, step))]
    pallas_call x1, Pallas kernels: 18.7 us -> 9.76 us  [merge(): plain_call(kernel, 2 * depth * columns * ranks, 4 * depth * columns + 2 *...]
    pallas_call x1, Pallas kernels: 7.73 us -> 1.65 us  [adam(): plain_call(kernel, 6 * rank * (tokens * columns + pool * features), 2 * t...]
    ppermute x8 -> x14, starting transfers between devices: 6.01 us -> 11.4 us  [along(): return lax.ppermute(value, 'wide', ring_links(wide, step))]
    pallas_call x1, Pallas kernels: 5.13 us -> 1.27 us  [low_rank_rows(): plain_call(kernel, 2 * total * depth * ranks, 2 * depth * (total + ranks)...]
    pallas_call x1, Pallas kernels: 6.6 us -> 3.2 us  [products(): plain_call(kernel, 6 * rank * (tokens * columns + pool * features), 2 * t...]
    pallas_call x1, Pallas kernels: 4.36 us -> 1.9 us  [finish(): plain_call(kernel, 4 * half * ranks * columns, 8 * half * columns + 2 * r...]
  transfers between devices with their start and end apart: 31 -> 43, of which waited for: 8 -> 13; matrix products, arithmetic and copies ran while one was open for 1% -> 0% of each run, Pallas kernels for 43% -> 25%
where the time goes in v2:
time: 107 us; the launch traced here: 105 us
  starting transfers between devices  35.7 us (33%)
  waiting for transfers between devices  32.8 us (31%)
  Pallas kernels  30.2 us (28%)
  local copies, waits for them, and re-layouts  5.84 us (5%)
    ppermute x24, starting transfers between devices, across(): return lax.ppermute(value, 'wide', [(i, i ^ flip) for i in range(wide)])  20 us
    ppermute x24, waiting for transfers between devices, across(): return lax.ppermute(value, 'wide', [(i, i ^ flip) for i in range(wide)])  19.6 us
    ppermute x14, waiting for transfers between devices, along(): return lax.ppermute(value, 'wide', ring_links(wide, step))  11.8 us
    ppermute x14, starting transfers between devices, along(): return lax.ppermute(value, 'wide', ring_links(wide, step))  11.4 us
    pallas_call x3, Pallas kernels, early_projection(): plain_call(kernel, 2 * half * depth * (last - first), 2 * depth * (last -...  10.6 us
    pallas_call x1, Pallas kernels, merge(): plain_call(kernel, 2 * depth * columns * ranks, 4 * depth * columns + 2 *...  9.76 us
    unnamed x30, local copies, waits for them, and re-layouts  5.84 us
    ppermute x5, starting transfers between devices, other_side(): return lax.ppermute(value, 'narrow', [(0, 1), (1, 0)])  4.34 us
  transfers between devices with their start and end apart: 43, of which 13 were waited for; matrix products, arithmetic and copies ran while one was open for 0% of the time, Pallas kernels for 25%

profile of v2, /device:TPU:9, one launch (start us, length us, event | category | flops | bytes accessed | tf_op | source)
XLA Modules:
  0.0 105.5 jit_solution(4578546448244802734)
XLA Ops:
  0.7 1.5 %collective-permute-start = (bf16[32,4096]{1,0:T(8,128)(2,1)}, bf16[32,4096]{1,0:T(8,128)(2,1)S(1)}, u32[]{:S(2)}, u32[]{:S(2)}) collective-permute-start(bf16[32,4096]{1,0:T(8,128)(2,1)} %refs_0_.1), channel_id=1, source_target_pairs={{0,8},{2,10},{8,16},{10,18},{16,24},{18,26},{24,28},{26,30},{28,20... | collective-permute-start | bytes 786440 | tf_op jit(solution)/shard_map/ppermute | solution.py:191
  2.2 2.3 %copy-done.3 = bf16[1,128,18560]{2,1,0:T(8,128)(2,1)S(1)} copy-done((bf16[1,128,18560]{2,1,0:T(8,128)(2,1)S(1)}, bf16[1,128,18560]{2,1,0:T(8,128)(2,1)}, u32[]{:S(2)}) %copy-start.3) | copy-done | bytes 4751384
  4.5 1.3 %copy-done.5 = f32[1,16,18560]{2,1,0:T(8,128)S(1)} copy-done((f32[1,16,18560]{2,1,0:T(8,128)S(1)}, f32[1,16,18560]{2,1,0:T(8,128)}, u32[]{:S(2)}) %copy-start.5) | copy-done | bytes 1187864
  8.0 3.2 %products.1.own_ref = f32[32,128]{1,0:T(8,128)S(1)} custom-call(bf16[128,4096]{1,0:T(8,128)(2,1)S(1)} %bitcast.22, f32[16,4096]{1,0:T(8,128)S(1)} %bitcast.24, bf16[128,18560]{1,0:T(8,128)(2,1)S(1)} %bitcast.16, f32[16,18560]{1,0:T(8,128)S(1)} %bitcast.18), custom_call_target="tpu_custom_call" | custom-call | flops 142539227136 | bytes 7249920 | tf_op jit(solution)/shard_map/products/pallas_call | solution.py:99
  11.3 1.4 %collective-permute-start.2 = (bf16[32,4096]{1,0:T(8,128)(2,1)S(1)}, bf16[32,4096]{1,0:T(8,128)(2,1)S(1)}, u32[]{:S(2)}, u32[]{:S(2)}) collective-permute-start(bf16[32,4096]{1,0:T(8,128)(2,1)S(1)} %collective-permute-done.refs_2_), channel_id=1, source_target_pairs={{0,8},{2,10},{8,16},{10,18},{16,24},{18,26},{24,28},{26,30},{28,20... | collective-permute-start | bytes 786440 | tf_op jit(solution)/shard_map/ppermute | solution.py:191
  14.0 1.4 %collective-permute-done.4.other_ref = f32[32,128]{1,0:T(8,128)S(1)} collective-permute-done((f32[32,128]{1,0:T(8,128)S(1)}, f32[32,128]{1,0:T(8,128)S(1)}, u32[]{:S(2)}, u32[]{:S(2)}) %collective-permute-start.4) | collective-permute-done | bytes 16416 | tf_op jit(solution)/shard_map/ppermute | solution.py:169
  15.4 2.5 %collective-permute-done.2.refs_6_ = bf16[32,4096]{1,0:T(8,128)(2,1)S(1)} collective-permute-done((bf16[32,4096]{1,0:T(8,128)(2,1)S(1)}, bf16[32,4096]{1,0:T(8,128)(2,1)S(1)}, u32[]{:S(2)}, u32[]{:S(2)}) %collective-permute-start.2) | collective-permute-done | bytes 262176 | tf_op jit(solution)/shard_map/ppermute | solution.py:191
  19.0 1.7 %adam.1 = (bf16[16,4096]{1,0:T(8,128)(2,1)S(1)}, bf16[8,16,2320]{2,1,0:T(8,128)(2,1)S(1)}) custom-call(s32[1,128]{1,0:T(1,128)S(1)} %copy-done.14, f32[32,128]{1,0:T(8,128)S(1)} %products.1.own_ref, f32[32,128]{1,0:T(8,128)S(1)} %collective-permute-done.4.other_ref, bf16[128,4096]{1,0:T(8,128)(2,1)S(1)} %bitcast.23, f32[16,4096]{1,0:T(8,128)S(1)} %bitcast.25, ...), custom_call_target="tpu_custom_call" | custom-call | flops 17817403392 | bytes 10874880 | tf_op jit(solution)/shard_map/adam/pallas_call | solution.py:147
  20.6 1.3 %collective-permute-start.15 = (bf16[8,16,2320]{2,1,0:T(8,128)(2,1)S(1)}, bf16[8,16,2320]{2,1,0:T(8,128)(2,1)S(1)}, u32[]{:S(2)}, u32[]{:S(2)}) collective-permute-start(bf16[8,16,2320]{2,1,0:T(8,128)(2,1)S(1)} %get-tuple-element.46.own_ref), channel_id=1, source_target_pairs={{0,1},{1,0},{2,3},{3,2},{4,5},{5,4},{6,7},{7,6},{8,9},{9,8},{10,11... | collective-permute-start | bytes 1781768 | tf_op jit(solution)/shard_map/ppermute | solution.py:169
  21.9 1.3 %collective-permute-start.6 = (bf16[32,4096]{1,0:T(8,128)(2,1)S(1)}, bf16[32,4096]{1,0:T(8,128)(2,1)S(1)}, u32[]{:S(2)}, u32[]{:S(2)}) collective-permute-start(bf16[32,4096]{1,0:T(8,128)(2,1)S(1)} %collective-permute-done.2.refs_6_), channel_id=1, source_target_pairs={{0,8},{2,10},{8,16},{10,18},{16,24},{18,26},{24,28},{26,30},{28,20... | collective-permute-start | bytes 786440 | tf_op jit(solution)/shard_map/ppermute | solution.py:191
  23.6 1.3 %collective-permute-start.8 = (bf16[16,4096]{1,0:T(8,128)(2,1)S(1)}, bf16[16,4096]{1,0:T(8,128)(2,1)S(1)}, u32[]{:S(2)}, u32[]{:S(2)}) collective-permute-start(bf16[16,4096]{1,0:T(8,128)(2,1)S(1)} %get-tuple-element.40.refs_0_), channel_id=1, source_target_pairs={{0,8},{2,10},{8,16},{10,18},{16,24},{18,26},{24,28},{26,30},{28,20... | collective-permute-start | bytes 393224 | tf_op jit(solution)/shard_map/ppermute | solution.py:191
  24.9 6.0 %collective-permute-done.9.refs_4_ = bf16[16,4096]{1,0:T(8,128)(2,1)S(1)} collective-permute-done((bf16[16,4096]{1,0:T(8,128)(2,1)S(1)}, bf16[16,4096]{1,0:T(8,128)(2,1)S(1)}, u32[]{:S(2)}, u32[]{:S(2)}) %collective-permute-start.9) | collective-permute-done | bytes 131104 | tf_op jit(solution)/shard_map/ppermute | solution.py:191
  30.9 1.2 %collective-permute-start.12 = (bf16[32,4096]{1,0:T(8,128)(2,1)S(1)}, bf16[32,4096]{1,0:T(8,128)(2,1)S(1)}, u32[]{:S(2)}, u32[]{:S(2)}) collective-permute-start(bf16[32,4096]{1,0:T(8,128)(2,1)S(1)} %collective-permute-done.6.refs_10_), channel_id=1, source_target_pairs={{0,8},{2,10},{8,16},{10,18},{16,24},{18,26},{24,28},{26,30},{28,20... | collective-permute-start | bytes 786440 | tf_op jit(solution)/shard_map/ppermute | solution.py:191
  33.6 4.8 %collective-permute-start.25 = (bf16[32,4096]{1,0:T(8,128)(2,1)S(1)}, bf16[32,4096]{1,0:T(8,128)(2,1)S(1)}, u32[]{:S(2)}, u32[]{:S(2)}) collective-permute-start(bf16[32,4096]{1,0:T(8,128)(2,1)S(1)} %copy-done.1), channel_id=1, source_target_pairs={{0,2},{2,0},{4,6},{6,4},{8,10},{10,8},{12,14},{14,12},{16,18},{18,... | collective-permute-start | bytes 786440 | tf_op jit(solution)/shard_map/ppermute | solution.py:165
  38.4 4.2 %collective-permute-start.26 = (bf16[32,4096]{1,0:T(8,128)(2,1)S(1)}, bf16[32,4096]{1,0:T(8,128)(2,1)S(1)}, u32[]{:S(2)}, u32[]{:S(2)}) collective-permute-start(bf16[32,4096]{1,0:T(8,128)(2,1)S(1)} %collective-permute-done.refs_2_), channel_id=1, source_target_pairs={{0,2},{2,0},{4,6},{6,4},{8,10},{10,8},{12,14},{14,12},{16,18},{18,... | collective-permute-start | bytes 786440 | tf_op jit(solution)/shard_map/ppermute | solution.py:165
  45.3 1.3 %collective-permute-done.29.refs_9_ = bf16[32,4096]{1,0:T(8,128)(2,1)S(1)} collective-permute-done((bf16[32,4096]{1,0:T(8,128)(2,1)S(1)}, bf16[32,4096]{1,0:T(8,128)(2,1)S(1)}, u32[]{:S(2)}, u32[]{:S(2)}) %collective-permute-start.29) | collective-permute-done | bytes 262176 | tf_op jit(solution)/shard_map/ppermute | solution.py:165
  47.7 1.3 %collective-permute-start.18 = (bf16[16,4096]{1,0:T(8,128)(2,1)S(1)}, bf16[16,4096]{1,0:T(8,128)(2,1)S(1)}, u32[]{:S(2)}, u32[]{:S(2)}) collective-permute-start(bf16[16,4096]{1,0:T(8,128)(2,1)S(1)} %collective-permute-done.13.refs_6_), channel_id=1, source_target_pairs={{0,8},{2,10},{8,16},{10,18},{16,24},{18,26},{24,28},{26,30},{28,20... | collective-permute-start | bytes 393224 | tf_op jit(solution)/shard_map/ppermute | solution.py:191
  50.4 2.2 %collective-permute-done.18.refs_10_ = bf16[16,4096]{1,0:T(8,128)(2,1)S(1)} collective-permute-done((bf16[16,4096]{1,0:T(8,128)(2,1)S(1)}, bf16[16,4096]{1,0:T(8,128)(2,1)S(1)}, u32[]{:S(2)}, u32[]{:S(2)}) %collective-permute-start.18) | collective-permute-done | bytes 131104 | tf_op jit(solution)/shard_map/ppermute | solution.py:191
  52.7 1.3 %collective-permute-start.22 = (bf16[16,4096]{1,0:T(8,128)(2,1)S(1)}, bf16[16,4096]{1,0:T(8,128)(2,1)S(1)}, u32[]{:S(2)}, u32[]{:S(2)}) collective-permute-start(bf16[16,4096]{1,0:T(8,128)(2,1)S(1)} %collective-permute-done.18.refs_10_), channel_id=1, source_target_pairs={{0,8},{2,10},{8,16},{10,18},{16,24},{18,26},{24,28},{26,30},{28,20... | collective-permute-start | bytes 393224 | tf_op jit(solution)/shard_map/ppermute | solution.py:191
  55.2 2.7 %early_projection.4 = bf16[1168,256]{1,0:T(8,128)(2,1)S(1)} custom-call(bf16[2320,4096]{1,0:T(8,128)(2,1)S(1)} %bitcast.12, bf16[512,4096]{1,0:T(8,128)(2,1)S(1)} %order_rows.3.next_ref.rows_ref), custom_call_target="tpu_custom_call" | custom-call | flops 2449473536 | bytes 12861440 | tf_op jit(solution)/shard_map/early_projection/pallas_call | solution.py:243
  59.0 2.3 %collective-permute-start.35 = (bf16[2,16,2320]{2,1,0:T(8,128)(2,1)S(1)}, bf16[2,16,2320]{2,1,0:T(8,128)(2,1)S(1)}, u32[]{:S(2)}, u32[]{:S(2)}) collective-permute-start(bf16[2,16,2320]{2,1,0:T(8,128)(2,1)S(1)} %get-tuple-element.57), channel_id=1, source_target_pairs={{0,12},{2,14},{4,8},{6,10},{8,4},{10,6},{12,0},{14,2},{16,28},{18,... | collective-permute-start | bytes 445448 | tf_op jit(solution)/shard_map/ppermute | solution.py:165
  61.3 2.6 %early_projection.5 = bf16[1152,256]{1,0:T(8,128)(2,1)S(1)} custom-call(bf16[2320,4096]{1,0:T(8,128)(2,1)S(1)} %bitcast.13, bf16[512,4096]{1,0:T(8,128)(2,1)S(1)} %order_rows.3.next_ref.rows_ref), custom_call_target="tpu_custom_call" | custom-call | flops 2415919104 | bytes 12713984 | tf_op jit(solution)/shard_map/early_projection/pallas_call | solution.py:243
  64.2 1.2 %collective-permute-start.41 = (bf16[1168,256]{1,0:T(8,128)(2,1)S(1)}, bf16[1168,256]{1,0:T(8,128)(2,1)S(1)}, u32[]{:S(2)}, u32[]{:S(2)}) collective-permute-start(bf16[1168,256]{1,0:T(8,128)(2,1)S(1)} %early_projection.4), channel_id=1, source_target_pairs={{0,1},{1,0},{2,3},{3,2},{4,5},{5,4},{6,7},{7,6},{8,9},{9,8},{10,11... | collective-permute-start | bytes 1794056 | tf_op jit(solution)/shard_map/ppermute | solution.py:169
  65.9 1.6 %collective-permute-start.36 = (bf16[2,16,2320]{2,1,0:T(8,128)(2,1)S(1)}, bf16[2,16,2320]{2,1,0:T(8,128)(2,1)S(1)}, u32[]{:S(2)}, u32[]{:S(2)}) collective-permute-start(bf16[2,16,2320]{2,1,0:T(8,128)(2,1)S(1)} %get-tuple-element.61), channel_id=1, source_target_pairs={{0,16},{2,18},{4,20},{6,22},{8,24},{10,26},{12,28},{14,30},{16,0},... | collective-permute-start | bytes 445448 | tf_op jit(solution)/shard_map/ppermute | solution.py:165
  68.4 1.3 %collective-permute-start.38 = (bf16[2,16,2320]{2,1,0:T(8,128)(2,1)S(1)}, bf16[2,16,2320]{2,1,0:T(8,128)(2,1)S(1)}, u32[]{:S(2)}, u32[]{:S(2)}) collective-permute-start(bf16[2,16,2320]{2,1,0:T(8,128)(2,1)S(1)} %get-tuple-element.63), channel_id=1, source_target_pairs={{0,24},{2,26},{4,28},{6,30},{8,16},{10,18},{12,20},{14,22},{16,8},... | collective-permute-start | bytes 445448 | tf_op jit(solution)/shard_map/ppermute | solution.py:165
  69.7 1.3 %low_rank_rows.1 = (f32[256,256]{1,0:T(8,128)S(1)}, f32[256,256]{1,0:T(8,128)S(1)}) custom-call(bf16[512,4096]{1,0:T(8,128)(2,1)S(1)} %order_rows.3.next_ref.rows_ref, bf16[256,4096]{1,0:T(8,128)(2,1)S(1)} %order_rows.2.left_ref), custom_call_target="tpu_custom_call" | custom-call | flops 68719476736 | bytes 6815744 | tf_op jit(solution)/shard_map/low_rank_rows/pallas_call | solution.py:267
  71.0 9.5 %collective-permute-done.36.refs_4_ = bf16[2,16,2320]{2,1,0:T(8,128)(2,1)S(1)} collective-permute-done((bf16[2,16,2320]{2,1,0:T(8,128)(2,1)S(1)}, bf16[2,16,2320]{2,1,0:T(8,128)(2,1)S(1)}, u32[]{:S(2)}, u32[]{:S(2)}) %collective-permute-start.36) | collective-permute-done | bytes 148512 | tf_op jit(solution)/shard_map/ppermute | solution.py:165
  80.5 5.3 %early_projection.3.own_ref = f32[2320,256]{1,0:T(8,128)S(1)} custom-call(bf16[2320,4096]{1,0:T(8,128)(2,1)S(1)} %bitcast.14, bf16[512,4096]{1,0:T(8,128)(2,1)S(1)} %order_rows.3.next_ref.rows_ref), custom_call_target="tpu_custom_call" | custom-call | flops 4865392640 | bytes 23478272 | tf_op jit(solution)/shard_map/early_projection/pallas_call | solution.py:243
  86.0 4.7 %collective-permute-done.38.refs_6_ = bf16[2,16,2320]{2,1,0:T(8,128)(2,1)S(1)} collective-permute-done((bf16[2,16,2320]{2,1,0:T(8,128)(2,1)S(1)}, bf16[2,16,2320]{2,1,0:T(8,128)(2,1)S(1)}, u32[]{:S(2)}, u32[]{:S(2)}) %collective-permute-start.38) | collective-permute-done | bytes 148512 | tf_op jit(solution)/shard_map/ppermute | solution.py:165
  90.7 3.1 %collective-permute-done.39.refs_7_ = bf16[2,16,2320]{2,1,0:T(8,128)(2,1)S(1)} collective-permute-done((bf16[2,16,2320]{2,1,0:T(8,128)(2,1)S(1)}, bf16[2,16,2320]{2,1,0:T(8,128)(2,1)S(1)}, u32[]{:S(2)}, u32[]{:S(2)}) %collective-permute-start.39) | collective-permute-done | bytes 148512 | tf_op jit(solution)/shard_map/ppermute | solution.py:165
  93.8 9.8 %merge.1 = (bf16[2320,4096]{1,0:T(8,128)(2,1)}, bf16[2320,256]{1,0:T(8,128)(2,1)S(1)}) custom-call(bf16[2320,4096]{1,0:T(8,128)(2,1)S(1)} %bitcast.15, bf16[256,4096]{1,0:T(8,128)(2,1)S(1)} %order_rows.2.left_ref, bf16[2,16,2320]{2,1,0:T(8,128)(2,1)S(1)} %get-tuple-element.52.refs_0_, bf16[2,16,2320]{2,1,0:T(8,128)(2,1)S(1)} %collective-permute-done.33.refs_1_, ...), custom_call_target="tpu_custom_call" | custom-call | flops 4865392640 | bytes 41295872 | tf_op jit(solution)/shard_map/merge/pallas_call | solution.py:372
  103.6 1.9 %finish.1 = bf16[2320,256]{1,0:T(8,128)(2,1)} custom-call(f32[256,256]{1,0:T(8,128)S(1)} %get-tuple-element.67.own_low_ref, f32[256,256]{1,0:T(8,128)S(1)} %collective-permute-done.40.other_low_ref, bf16[2320,256]{1,0:T(8,128)(2,1)S(1)} %get-tuple-element.69.turned_ref, f32[2320,256]{1,0:T(8,128)S(1)} %early_projection.3.own_ref, ...), custom_call_target="tpu_custom_call" | custom-call | flops 608174080 | bytes 5939200 | tf_op jit(solution)/shard_map/finish/pallas_call | solution.py:409
  (96 shorter events, 16.0 us)
Async XLA Ops:
  0.6 10.6 %collective-permute-start.1 = (bf16[32,4096]{1,0:T(8,128)(2,1)}, bf16[32,4096]{1,0:T(8,128)(2,1)S(1)}, u32[]{:S(2)}, u32[]{:S(2)}) collective-permute-start(bf16[32,4096]{1,0:T(8,128)(2,1)} %refs_0_.1), channel_id=1, source_target_pairs={{0,4},{2,6},{8,0},{10,2},{16,8},{18,10},{24,16},{26,18},{28,24},{3... | collective-permute-start | bytes 786440 | tf_op jit(solution)/shard_map/ppermute | solution.py:191
  0.7 10.5 %collective-permute-start = (bf16[32,4096]{1,0:T(8,128)(2,1)}, bf16[32,4096]{1,0:T(8,128)(2,1)S(1)}, u32[]{:S(2)}, u32[]{:S(2)}) collective-permute-start(bf16[32,4096]{1,0:T(8,128)(2,1)} %refs_0_.1), channel_id=1, source_target_pairs={{0,8},{2,10},{8,16},{10,18},{16,24},{18,26},{24,28},{26,30},{28,20... | collective-permute-start | bytes 786440 | tf_op jit(solution)/shard_map/ppermute | solution.py:191
  11.3 6.6 %collective-permute-start.2 = (bf16[32,4096]{1,0:T(8,128)(2,1)S(1)}, bf16[32,4096]{1,0:T(8,128)(2,1)S(1)}, u32[]{:S(2)}, u32[]{:S(2)}) collective-permute-start(bf16[32,4096]{1,0:T(8,128)(2,1)S(1)} %collective-permute-done.refs_2_), channel_id=1, source_target_pairs={{0,8},{2,10},{8,16},{10,18},{16,24},{18,26},{24,28},{26,30},{28,20... | collective-permute-start | bytes 786440 | tf_op jit(solution)/shard_map/ppermute | solution.py:191
  12.6 6.3 %collective-permute-start.3 = (bf16[32,4096]{1,0:T(8,128)(2,1)S(1)}, bf16[32,4096]{1,0:T(8,128)(2,1)S(1)}, u32[]{:S(2)}, u32[]{:S(2)}) collective-permute-start(bf16[32,4096]{1,0:T(8,128)(2,1)S(1)} %collective-permute-done.1.refs_4_), channel_id=1, source_target_pairs={{0,4},{2,6},{8,0},{10,2},{16,8},{18,10},{24,16},{26,18},{28,24},{3... | collective-permute-start | bytes 786440 | tf_op jit(solution)/shard_map/ppermute | solution.py:191
  20.6 22.5 %collective-permute-start.15 = (bf16[8,16,2320]{2,1,0:T(8,128)(2,1)S(1)}, bf16[8,16,2320]{2,1,0:T(8,128)(2,1)S(1)}, u32[]{:S(2)}, u32[]{:S(2)}) collective-permute-start(bf16[8,16,2320]{2,1,0:T(8,128)(2,1)S(1)} %get-tuple-element.46.own_ref), channel_id=1, source_target_pairs={{0,1},{1,0},{2,3},{3,2},{4,5},{5,4},{6,7},{7,6},{8,9},{9,8},{10,11... | collective-permute-start | bytes 1781768 | tf_op jit(solution)/shard_map/ppermute | solution.py:169
  21.9 8.9 %collective-permute-start.6 = (bf16[32,4096]{1,0:T(8,128)(2,1)S(1)}, bf16[32,4096]{1,0:T(8,128)(2,1)S(1)}, u32[]{:S(2)}, u32[]{:S(2)}) collective-permute-start(bf16[32,4096]{1,0:T(8,128)(2,1)S(1)} %collective-permute-done.2.refs_6_), channel_id=1, source_target_pairs={{0,8},{2,10},{8,16},{10,18},{16,24},{18,26},{24,28},{26,30},{28,20... | collective-permute-start | bytes 786440 | tf_op jit(solution)/shard_map/ppermute | solution.py:191
  23.2 7.6 %collective-permute-start.7 = (bf16[32,4096]{1,0:T(8,128)(2,1)S(1)}, bf16[32,4096]{1,0:T(8,128)(2,1)S(1)}, u32[]{:S(2)}, u32[]{:S(2)}) collective-permute-start(bf16[32,4096]{1,0:T(8,128)(2,1)S(1)} %collective-permute-done.3.refs_8_), channel_id=1, source_target_pairs={{0,4},{2,6},{8,0},{10,2},{16,8},{18,10},{24,16},{26,18},{28,24},{3... | collective-permute-start | bytes 786440 | tf_op jit(solution)/shard_map/ppermute | solution.py:191
  23.4 7.4 %collective-permute-start.9 = (bf16[16,4096]{1,0:T(8,128)(2,1)S(1)}, bf16[16,4096]{1,0:T(8,128)(2,1)S(1)}, u32[]{:S(2)}, u32[]{:S(2)}) collective-permute-start(bf16[16,4096]{1,0:T(8,128)(2,1)S(1)} %get-tuple-element.40.refs_0_), channel_id=1, source_target_pairs={{0,4},{2,6},{8,0},{10,2},{16,8},{18,10},{24,16},{26,18},{28,24},{3... | collective-permute-start | bytes 393224 | tf_op jit(solution)/shard_map/ppermute | solution.py:191
  23.6 7.3 %collective-permute-start.8 = (bf16[16,4096]{1,0:T(8,128)(2,1)S(1)}, bf16[16,4096]{1,0:T(8,128)(2,1)S(1)}, u32[]{:S(2)}, u32[]{:S(2)}) collective-permute-start(bf16[16,4096]{1,0:T(8,128)(2,1)S(1)} %get-tuple-element.40.refs_0_), channel_id=1, source_target_pairs={{0,8},{2,10},{8,16},{10,18},{16,24},{18,26},{24,28},{26,30},{28,20... | collective-permute-start | bytes 393224 | tf_op jit(solution)/shard_map/ppermute | solution.py:191
  30.9 11.8 %collective-permute-start.12 = (bf16[32,4096]{1,0:T(8,128)(2,1)S(1)}, bf16[32,4096]{1,0:T(8,128)(2,1)S(1)}, u32[]{:S(2)}, u32[]{:S(2)}) collective-permute-start(bf16[32,4096]{1,0:T(8,128)(2,1)S(1)} %collective-permute-done.6.refs_10_), channel_id=1, source_target_pairs={{0,8},{2,10},{8,16},{10,18},{16,24},{18,26},{24,28},{26,30},{28,20... | collective-permute-start | bytes 786440 | tf_op jit(solution)/shard_map/ppermute | solution.py:191
  32.1 6.3 %collective-permute-start.13 = (bf16[16,4096]{1,0:T(8,128)(2,1)S(1)}, bf16[16,4096]{1,0:T(8,128)(2,1)S(1)}, u32[]{:S(2)}, u32[]{:S(2)}) collective-permute-start(bf16[16,4096]{1,0:T(8,128)(2,1)S(1)} %collective-permute-done.8.refs_2_), channel_id=1, source_target_pairs={{0,8},{2,10},{8,16},{10,18},{16,24},{18,26},{24,28},{26,30},{28,20... | collective-permute-start | bytes 393224 | tf_op jit(solution)/shard_map/ppermute | solution.py:191
  32.5 10.1 %collective-permute-start.14 = (bf16[16,4096]{1,0:T(8,128)(2,1)S(1)}, bf16[16,4096]{1,0:T(8,128)(2,1)S(1)}, u32[]{:S(2)}, u32[]{:S(2)}) collective-permute-start(bf16[16,4096]{1,0:T(8,128)(2,1)S(1)} %collective-permute-done.9.refs_4_), channel_id=1, source_target_pairs={{0,4},{2,6},{8,0},{10,2},{16,8},{18,10},{24,16},{26,18},{28,24},{3... | collective-permute-start | bytes 393224 | tf_op jit(solution)/shard_map/ppermute | solution.py:191
  33.6 10.7 %collective-permute-start.25 = (bf16[32,4096]{1,0:T(8,128)(2,1)S(1)}, bf16[32,4096]{1,0:T(8,128)(2,1)S(1)}, u32[]{:S(2)}, u32[]{:S(2)}) collective-permute-start(bf16[32,4096]{1,0:T(8,128)(2,1)S(1)} %copy-done.1), channel_id=1, source_target_pairs={{0,2},{2,0},{4,6},{6,4},{8,10},{10,8},{12,14},{14,12},{16,18},{18,... | collective-permute-start | bytes 786440 | tf_op jit(solution)/shard_map/ppermute | solution.py:165
  38.4 6.3 %collective-permute-start.26 = (bf16[32,4096]{1,0:T(8,128)(2,1)S(1)}, bf16[32,4096]{1,0:T(8,128)(2,1)S(1)}, u32[]{:S(2)}, u32[]{:S(2)}) collective-permute-start(bf16[32,4096]{1,0:T(8,128)(2,1)S(1)} %collective-permute-done.refs_2_), channel_id=1, source_target_pairs={{0,2},{2,0},{4,6},{6,4},{8,10},{10,8},{12,14},{14,12},{16,18},{18,... | collective-permute-start | bytes 786440 | tf_op jit(solution)/shard_map/ppermute | solution.py:165
  44.1 9.8 %collective-permute-start.24 = (bf16[8,16,2320]{2,1,0:T(8,128)(2,1)S(1)}, bf16[8,16,2320]{2,1,0:T(8,128)(2,1)S(1)}, u32[]{:S(2)}, u32[]{:S(2)}) collective-permute-start(bf16[8,16,2320]{2,1,0:T(8,128)(2,1)S(1)} %get-tuple-element.51), channel_id=1, source_target_pairs={{0,2},{2,0},{4,6},{6,4},{8,10},{10,8},{12,14},{14,12},{16,18},{18,... | collective-permute-start | bytes 1781768 | tf_op jit(solution)/shard_map/ppermute | solution.py:165
  49.4 9.2 %collective-permute-start.16 = (bf16[16,4096]{1,0:T(8,128)(2,1)S(1)}, bf16[16,4096]{1,0:T(8,128)(2,1)S(1)}, u32[]{:S(2)}, u32[]{:S(2)}) collective-permute-start(bf16[16,4096]{1,0:T(8,128)(2,1)S(1)} %collective-permute-done.13.refs_6_), channel_id=1, source_target_pairs={{0,2},{2,0},{4,6},{6,4},{8,10},{10,8},{12,14},{14,12},{16,18},{18,... | collective-permute-start | bytes 393224 | tf_op jit(solution)/shard_map/ppermute | solution.py:165
  49.9 8.1 %collective-permute-start.20 = (bf16[16,4096]{1,0:T(8,128)(2,1)S(1)}, bf16[16,4096]{1,0:T(8,128)(2,1)S(1)}, u32[]{:S(2)}, u32[]{:S(2)}) collective-permute-start(bf16[16,4096]{1,0:T(8,128)(2,1)S(1)} %collective-permute-done.14.refs_8_), channel_id=1, source_target_pairs={{0,4},{2,6},{8,0},{10,2},{16,8},{18,10},{24,16},{26,18},{28,24},{3... | collective-permute-start | bytes 393224 | tf_op jit(solution)/shard_map/ppermute | solution.py:191
  50.1 8.5 %collective-permute-start.17 = (bf16[16,4096]{1,0:T(8,128)(2,1)S(1)}, bf16[16,4096]{1,0:T(8,128)(2,1)S(1)}, u32[]{:S(2)}, u32[]{:S(2)}) collective-permute-start(bf16[16,4096]{1,0:T(8,128)(2,1)S(1)} %collective-permute-done.14.refs_8_), channel_id=1, source_target_pairs={{0,2},{2,0},{4,6},{6,4},{8,10},{10,8},{12,14},{14,12},{16,18},{18,... | collective-permute-start | bytes 393224 | tf_op jit(solution)/shard_map/ppermute | solution.py:165
  52.7 5.4 %collective-permute-start.22 = (bf16[16,4096]{1,0:T(8,128)(2,1)S(1)}, bf16[16,4096]{1,0:T(8,128)(2,1)S(1)}, u32[]{:S(2)}, u32[]{:S(2)}) collective-permute-start(bf16[16,4096]{1,0:T(8,128)(2,1)S(1)} %collective-permute-done.18.refs_10_), channel_id=1, source_target_pairs={{0,8},{2,10},{8,16},{10,18},{16,24},{18,26},{24,28},{26,30},{28,20... | collective-permute-start | bytes 393224 | tf_op jit(solution)/shard_map/ppermute | solution.py:191
  53.9 5.0 %collective-permute-start.19 = (bf16[16,4096]{1,0:T(8,128)(2,1)S(1)}, bf16[16,4096]{1,0:T(8,128)(2,1)S(1)}, u32[]{:S(2)}, u32[]{:S(2)}) collective-permute-start(bf16[16,4096]{1,0:T(8,128)(2,1)S(1)} %collective-permute-done.18.refs_10_), channel_id=1, source_target_pairs={{0,2},{2,0},{4,6},{6,4},{8,10},{10,8},{12,14},{14,12},{16,18},{18,... | collective-permute-start | bytes 393224 | tf_op jit(solution)/shard_map/ppermute | solution.py:165
  58.0 6.0 %collective-permute-start.21 = (bf16[16,4096]{1,0:T(8,128)(2,1)S(1)}, bf16[16,4096]{1,0:T(8,128)(2,1)S(1)}, u32[]{:S(2)}, u32[]{:S(2)}) collective-permute-start(bf16[16,4096]{1,0:T(8,128)(2,1)S(1)} %collective-permute-done.20.refs_12_), channel_id=1, source_target_pairs={{0,2},{2,0},{4,6},{6,4},{8,10},{10,8},{12,14},{14,12},{16,18},{18,... | collective-permute-start | bytes 393224 | tf_op jit(solution)/shard_map/ppermute | solution.py:165
  58.1 6.2 %collective-permute-start.23 = (bf16[16,4096]{1,0:T(8,128)(2,1)S(1)}, bf16[16,4096]{1,0:T(8,128)(2,1)S(1)}, u32[]{:S(2)}, u32[]{:S(2)}) collective-permute-start(bf16[16,4096]{1,0:T(8,128)(2,1)S(1)} %collective-permute-done.22.refs_14_), channel_id=1, source_target_pairs={{0,2},{2,0},{4,6},{6,4},{8,10},{10,8},{12,14},{14,12},{16,18},{18,... | collective-permute-start | bytes 393224 | tf_op jit(solution)/shard_map/ppermute | solution.py:165
  58.6 7.3 %collective-permute-start.33 = (bf16[2,16,2320]{2,1,0:T(8,128)(2,1)S(1)}, bf16[2,16,2320]{2,1,0:T(8,128)(2,1)S(1)}, u32[]{:S(2)}, u32[]{:S(2)}) collective-permute-start(bf16[2,16,2320]{2,1,0:T(8,128)(2,1)S(1)} %get-tuple-element.55), channel_id=1, source_target_pairs={{0,4},{2,6},{4,0},{6,2},{8,12},{10,14},{12,8},{14,10},{16,20},{18,... | collective-permute-start | bytes 445448 | tf_op jit(solution)/shard_map/ppermute | solution.py:165
  58.6 8.8 %collective-permute-start.34 = (bf16[2,16,2320]{2,1,0:T(8,128)(2,1)S(1)}, bf16[2,16,2320]{2,1,0:T(8,128)(2,1)S(1)}, u32[]{:S(2)}, u32[]{:S(2)}) collective-permute-start(bf16[2,16,2320]{2,1,0:T(8,128)(2,1)S(1)} %get-tuple-element.56), channel_id=1, source_target_pairs={{0,8},{2,10},{4,12},{6,14},{8,0},{10,2},{12,4},{14,6},{16,24},{18,... | collective-permute-start | bytes 445448 | tf_op jit(solution)/shard_map/ppermute | solution.py:165
  59.0 9.5 %collective-permute-start.35 = (bf16[2,16,2320]{2,1,0:T(8,128)(2,1)S(1)}, bf16[2,16,2320]{2,1,0:T(8,128)(2,1)S(1)}, u32[]{:S(2)}, u32[]{:S(2)}) collective-permute-start(bf16[2,16,2320]{2,1,0:T(8,128)(2,1)S(1)} %get-tuple-element.57), channel_id=1, source_target_pairs={{0,12},{2,14},{4,8},{6,10},{8,4},{10,6},{12,0},{14,2},{16,28},{18,... | collective-permute-start | bytes 445448 | tf_op jit(solution)/shard_map/ppermute | solution.py:165
  63.9 39.6 %collective-permute-start.42 = (bf16[1152,256]{1,0:T(8,128)(2,1)S(1)}, bf16[1152,256]{1,0:T(8,128)(2,1)S(1)}, u32[]{:S(2)}, u32[]{:S(2)}) collective-permute-start(bf16[1152,256]{1,0:T(8,128)(2,1)S(1)} %early_projection.5), channel_id=1, source_target_pairs={{0,1},{1,0},{2,3},{3,2},{4,5},{5,4},{6,7},{7,6},{8,9},{9,8},{10,11... | collective-permute-start | bytes 1769480 | tf_op jit(solution)/shard_map/ppermute | solution.py:169
  64.2 39.4 %collective-permute-start.41 = (bf16[1168,256]{1,0:T(8,128)(2,1)S(1)}, bf16[1168,256]{1,0:T(8,128)(2,1)S(1)}, u32[]{:S(2)}, u32[]{:S(2)}) collective-permute-start(bf16[1168,256]{1,0:T(8,128)(2,1)S(1)} %early_projection.4), channel_id=1, source_target_pairs={{0,1},{1,0},{2,3},{3,2},{4,5},{5,4},{6,7},{7,6},{8,9},{9,8},{10,11... | collective-permute-start | bytes 1794056 | tf_op jit(solution)/shard_map/ppermute | solution.py:169
  65.9 14.6 %collective-permute-start.36 = (bf16[2,16,2320]{2,1,0:T(8,128)(2,1)S(1)}, bf16[2,16,2320]{2,1,0:T(8,128)(2,1)S(1)}, u32[]{:S(2)}, u32[]{:S(2)}) collective-permute-start(bf16[2,16,2320]{2,1,0:T(8,128)(2,1)S(1)} %get-tuple-element.61), channel_id=1, source_target_pairs={{0,16},{2,18},{4,20},{6,22},{8,24},{10,26},{12,28},{14,30},{16,0},... | collective-permute-start | bytes 445448 | tf_op jit(solution)/shard_map/ppermute | solution.py:165
  67.5 18.3 %collective-permute-start.37 = (bf16[2,16,2320]{2,1,0:T(8,128)(2,1)S(1)}, bf16[2,16,2320]{2,1,0:T(8,128)(2,1)S(1)}, u32[]{:S(2)}, u32[]{:S(2)}) collective-permute-start(bf16[2,16,2320]{2,1,0:T(8,128)(2,1)S(1)} %get-tuple-element.62), channel_id=1, source_target_pairs={{0,20},{2,22},{4,16},{6,18},{8,28},{10,30},{12,24},{14,26},{16,4},... | collective-permute-start | bytes 445448 | tf_op jit(solution)/shard_map/ppermute | solution.py:165
  68.4 22.3 %collective-permute-start.38 = (bf16[2,16,2320]{2,1,0:T(8,128)(2,1)S(1)}, bf16[2,16,2320]{2,1,0:T(8,128)(2,1)S(1)}, u32[]{:S(2)}, u32[]{:S(2)}) collective-permute-start(bf16[2,16,2320]{2,1,0:T(8,128)(2,1)S(1)} %get-tuple-element.63), channel_id=1, source_target_pairs={{0,24},{2,26},{4,28},{6,30},{8,16},{10,18},{12,20},{14,22},{16,8},... | collective-permute-start | bytes 445448 | tf_op jit(solution)/shard_map/ppermute | solution.py:165
  80.5 13.3 %collective-permute-start.39 = (bf16[2,16,2320]{2,1,0:T(8,128)(2,1)S(1)}, bf16[2,16,2320]{2,1,0:T(8,128)(2,1)S(1)}, u32[]{:S(2)}, u32[]{:S(2)}) collective-permute-start(bf16[2,16,2320]{2,1,0:T(8,128)(2,1)S(1)} %get-tuple-element.64), channel_id=1, source_target_pairs={{0,28},{2,30},{4,24},{6,26},{8,20},{10,22},{12,16},{14,18},{16,12}... | collective-permute-start | bytes 445448 | tf_op jit(solution)/shard_map/ppermute | solution.py:165
  85.8 17.8 %collective-permute-start.40 = (f32[256,256]{1,0:T(8,128)S(1)}, f32[256,256]{1,0:T(8,128)S(1)}, u32[]{:S(2)}, u32[]{:S(2)}) collective-permute-start(f32[256,256]{1,0:T(8,128)S(1)} %get-tuple-element.68), channel_id=1, source_target_pairs={{0,1},{1,0},{2,3},{3,2},{4,5},{5,4},{6,7},{7,6},{8,9},{9,8},{10,11... | collective-permute-start | bytes 786440 | tf_op jit(solution)/shard_map/ppermute | solution.py:169
  (26 other events, 173.5 us)

commit v3 on v2

--- a/solution.py
+++ b/solution.py
@@ -37,6 +37,10 @@
     )
 
 
+def anywhere():
+    return pl.BlockSpec(memory_space=pl.ANY)
+
+
 def in_vmem():
     return pl.BlockSpec(memory_space=pltpu.VMEM)
 
@@ -76,14 +80,29 @@
     return max(d for d in range(16, most + 1, 16) if rows % d == 0)
 
 
-def products(cache, factor_b, cotangent, factor_a):
+def opening():
+    def kernel(out_ref):
+        out_ref[...] = jnp.zeros_like(out_ref)
+
+    return plain_call(
+        kernel,
+        10**11,
+        0,
+        4,
+        out_specs=in_vmem(),
+        out_shape=jax.ShapeDtypeStruct((8, 128), F32),
+        name="opening",
+    )()
+
+
+def products(cache, factor_b, cotangent, factor_a, after):
     rank, columns = factor_a.shape
     tokens = cotangent.shape[0]
     pool, features = cache.shape
 
     tile = column_tile(columns, 4096)
 
-    def kernel(cache_ref, b_ref, cot_ref, a_ref, out_ref):
+    def kernel(cache_ref, b_ref, cot_ref, a_ref, _, out_ref):
         value = dot_rows(cot_ref[...], a_ref[...])
 
         @pl.when(pl.program_id(0) == 0)
@@ -108,11 +127,12 @@
             pl.BlockSpec((rank, features), fixed),
             pl.BlockSpec((tokens, tile), lambda i: (0, i)),
             pl.BlockSpec((rank, tile), lambda i: (0, i)),
+            anywhere(),
         ],
         out_specs=pl.BlockSpec((2 * rank, tokens), fixed),
         out_shape=jax.ShapeDtypeStruct((2 * rank, tokens), F32),
         name="products",
-    )(cache, factor_b, cotangent, factor_a)
+    )(cache, factor_b, cotangent, factor_a, after)
 
 
 def adam(ids, own, other, cache, b_set, cotangent, a_set, block_cols, inverse_root, early):
@@ -331,7 +351,7 @@
     )(mine, handed)
 
 
-def merge(resident, left, pieces, scale):
+def merge(resident, left, pieces, order, scale):
     columns, depth = resident.shape
     ranks = left.shape[0]
     rank = pieces[0].shape[1]
@@ -345,7 +365,7 @@
         @pl.when(step == 0)
         def _():
             device = lax.axis_index("wide")
-            for flip, ref in enumerate(refs[:count]):
+            for flip, ref in zip(order, refs):
                 for o in (0, 1):
                     worker = 2 * ((device // 2) ^ flip) + (device + o) % 2
                     right_ref[pl.ds(pl.multiple_of(worker * rank, rank), rank), :] = ref[o]
@@ -383,7 +403,7 @@
         ],
         scratch_shapes=[pltpu.VMEM((ranks, columns), BF16)],
         name="merge",
-    )(resident, left, *pieces)
+    )(resident, left, *[pieces[flip] for flip in order])
 
 
 def finish(own_part, others, low_own, low_other, turned, inverse_root):
@@ -452,12 +472,12 @@
         return along(ahead, wide, 1), along(behind, wide, -1)
 
     step_1 = both_ways(next_rows, next_rows)
-    own_sums = products(cache, adapter_b[0], incoming, adapter_a[0])
+    own_sums = products(cache, adapter_b[0], incoming, adapter_a[0], opening())
     step_1, own_sums = hold((step_1, own_sums))
     keep(pieces, *step_1)
     other_sums = other_side(own_sums)
     step_2 = both_ways(*step_1)
-    step_2, other_sums = hold((step_2, other_sums))
+
     keep(pieces, *step_2)
     new_b, own_blocks = adam(
         token_ids,
@@ -498,13 +518,11 @@
     cut = -(-block_cols // 32) * 16
     got_0 = other_side(early_projection(resident, all_next, 0, cut, 1))
     got_1 = other_side(early_projection(resident, all_next, cut, block_cols, 1))
-    all_next, right[1], right[2], right[3] = hold(
-        (all_next, right[1], right[2], right[3])
-    )
     own_part = early_projection(resident, all_next, 0, block_cols, 0)
     low_own, low_away = low_rank_rows(all_next, left)
+    order = (0,1,2,3,4,5,6,7)
     low_other = other_side(low_away)
-    merged, turned = merge(resident, left, right, scale)
+    merged, turned = merge(resident, left, right, order, scale)
     projected = finish(own_part, (got_0, got_1), low_own, low_other, turned, inverse_root)
     return (merged.T, projected.T)
 

time: 107 us -> 102 us (0.953)
  local copies, waits for them, and re-layouts: 5.84 us -> 1.53 us
  waiting for transfers between devices: 32.8 us -> 29.1 us
  starting transfers between devices: 35.7 us -> 38.6 us
  Pallas kernels: 30.2 us -> 31.3 us
    unnamed x30 -> x24, local copies, waits for them, and re-layouts: 5.84 us -> 1.53 us
    ppermute x14, waiting for transfers between devices: 11.8 us -> 8.78 us  [along(): return lax.ppermute(value, 'wide', ring_links(wide, step))]
    ppermute x24, starting transfers between devices: 20 us -> 22.1 us  [across(): return lax.ppermute(value, 'wide', [(i, i ^ flip) for i in range(wide)])]
    ppermute x5, waiting for transfers between devices: 1.36 us -> 0.01 us  [other_side(): return lax.ppermute(value, 'narrow', [(0, 1), (1, 0)])]
  transfers between devices with their start and end apart: 43 -> 43, of which waited for: 13 -> 9; matrix products, arithmetic and copies ran while one was open for 0% -> 0% of each run, Pallas kernels for 25% -> 29%
where the time goes in v3:
time: 102 us
  starting transfers between devices  38.6 us (38%)
  Pallas kernels  31.3 us (31%)
  waiting for transfers between devices  29.1 us (29%)
  local copies, waits for them, and re-layouts  1.53 us (2%)
    ppermute x24, starting transfers between devices, across(): return lax.ppermute(value, 'wide', [(i, i ^ flip) for i in range(wide)])  22.1 us
    ppermute x24, waiting for transfers between devices, across(): return lax.ppermute(value, 'wide', [(i, i ^ flip) for i in range(wide)])  20.4 us
    ppermute x14, starting transfers between devices, along(): return lax.ppermute(value, 'wide', ring_links(wide, step))  12.3 us
    pallas_call x3, Pallas kernels, early_projection(): plain_call(kernel, 2 * half * depth * (last - first), 2 * depth * (last -...  10.6 us
    pallas_call x1, Pallas kernels, merge(): plain_call(kernel, 2 * depth * columns * ranks, 4 * depth * columns + 2 *...  9.77 us
    ppermute x14, waiting for transfers between devices, along(): return lax.ppermute(value, 'wide', ring_links(wide, step))  8.78 us
    ppermute x5, starting transfers between devices, other_side(): return lax.ppermute(value, 'narrow', [(0, 1), (1, 0)])  4.17 us
    pallas_call x1, Pallas kernels, products(): plain_call(kernel, 6 * rank * (tokens * columns + pool * features), 2 * t...  3.21 us
  transfers between devices with their start and end apart: 43, of which 9 were waited for; matrix products, arithmetic and copies ran while one was open for 0% of the time, Pallas kernels for 29%

profile of v3, /device:TPU:9, one launch (start us, length us, event | category | flops | bytes accessed | tf_op | source)
XLA Modules:
  0.0 101.5 jit_solution(1662402553143571085)
XLA Ops:
  0.7 1.4 %collective-permute-start = (bf16[32,4096]{1,0:T(8,128)(2,1)}, bf16[32,4096]{1,0:T(8,128)(2,1)}, u32[]{:S(2)}, u32[]{:S(2)}) collective-permute-start(bf16[32,4096]{1,0:T(8,128)(2,1)} %refs_0_.1), channel_id=1, source_target_pairs={{0,8},{2,10},{8,16},{10,18},{16,24},{18,26},{24,28},{26,30},{28,20... | collective-permute-start | bytes 786440 | tf_op jit(solution)/shard_map/ppermute | solution.py:211
  2.2 1.2 %copy-done.3 = bf16[1,128,18560]{2,1,0:T(8,128)(2,1)S(1)} copy-done((bf16[1,128,18560]{2,1,0:T(8,128)(2,1)S(1)}, bf16[1,128,18560]{2,1,0:T(8,128)(2,1)}, u32[]{:S(2)}) %copy-start.3) | copy-done | bytes 4751384
  3.7 3.2 %products.1.own_ref = f32[32,128]{1,0:T(8,128)S(1)} custom-call(bf16[128,4096]{1,0:T(8,128)(2,1)S(1)} %bitcast.22, f32[16,4096]{1,0:T(8,128)S(1)} %bitcast.24, bf16[128,18560]{1,0:T(8,128)(2,1)S(1)} %bitcast.16, f32[16,18560]{1,0:T(8,128)S(1)} %bitcast.18, f32[8,128]{1,0:T(8,128)S(1)} %opening.1._), custom_call_target="tpu_custom_call" | custom-call | flops 142539227136 | bytes 7249920 | tf_op jit(solution)/shard_map/products/pallas_call | solution.py:118
  6.9 1.3 %collective-permute-done.1.refs_4_ = bf16[32,4096]{1,0:T(8,128)(2,1)} collective-permute-done((bf16[32,4096]{1,0:T(8,128)(2,1)}, bf16[32,4096]{1,0:T(8,128)(2,1)}, u32[]{:S(2)}, u32[]{:S(2)}) %collective-permute-start.1) | collective-permute-done | bytes 262176 | tf_op jit(solution)/shard_map/ppermute | solution.py:211
  8.3 1.2 %collective-permute-start.2 = (f32[32,128]{1,0:T(8,128)S(1)}, f32[32,128]{1,0:T(8,128)S(1)}, u32[]{:S(2)}, u32[]{:S(2)}) collective-permute-start(f32[32,128]{1,0:T(8,128)S(1)} %products.1.own_ref), channel_id=1, source_target_pairs={{0,1},{1,0},{2,3},{3,2},{4,5},{5,4},{6,7},{7,6},{8,9},{9,8},{10,11... | collective-permute-start | bytes 49160 | tf_op jit(solution)/shard_map/ppermute | solution.py:189
  9.5 1.3 %collective-permute-start.4 = (bf16[32,4096]{1,0:T(8,128)(2,1)}, bf16[32,4096]{1,0:T(8,128)(2,1)S(1)}, u32[]{:S(2)}, u32[]{:S(2)}) collective-permute-start(bf16[32,4096]{1,0:T(8,128)(2,1)} %collective-permute-done.refs_2_), channel_id=1, source_target_pairs={{0,8},{2,10},{8,16},{10,18},{16,24},{18,26},{24,28},{26,30},{28,20... | collective-permute-start | bytes 786440 | tf_op jit(solution)/shard_map/ppermute | solution.py:211
  11.0 1.7 %adam.1 = (bf16[16,4096]{1,0:T(8,128)(2,1)S(1)}, bf16[8,16,2320]{2,1,0:T(8,128)(2,1)S(1)}) custom-call(s32[1,128]{1,0:T(1,128)S(1)} %copy-done.11, f32[32,128]{1,0:T(8,128)S(1)} %products.1.own_ref, f32[32,128]{1,0:T(8,128)S(1)} %collective-permute-done.2.other_ref, bf16[128,4096]{1,0:T(8,128)(2,1)S(1)} %bitcast.23, f32[16,4096]{1,0:T(8,128)S(1)} %bitcast.25, ...), custom_call_target="tpu_custom_call" | custom-call | flops 17817403392 | bytes 10874880 | tf_op jit(solution)/shard_map/adam/pallas_call | solution.py:167
  12.7 1.2 %collective-permute-start.15 = (bf16[8,16,2320]{2,1,0:T(8,128)(2,1)S(1)}, bf16[8,16,2320]{2,1,0:T(8,128)(2,1)S(1)}, u32[]{:S(2)}, u32[]{:S(2)}) collective-permute-start(bf16[8,16,2320]{2,1,0:T(8,128)(2,1)S(1)} %get-tuple-element.36.own_ref), channel_id=1, source_target_pairs={{0,1},{1,0},{2,3},{3,2},{4,5},{5,4},{6,7},{7,6},{8,9},{9,8},{10,11... | collective-permute-start | bytes 1781768 | tf_op jit(solution)/shard_map/ppermute | solution.py:189
  13.9 1.6 %collective-permute-done.4.refs_6_ = bf16[32,4096]{1,0:T(8,128)(2,1)S(1)} collective-permute-done((bf16[32,4096]{1,0:T(8,128)(2,1)}, bf16[32,4096]{1,0:T(8,128)(2,1)S(1)}, u32[]{:S(2)}, u32[]{:S(2)}) %collective-permute-start.4) | collective-permute-done | bytes 262176 | tf_op jit(solution)/shard_map/ppermute | solution.py:211
  15.5 1.3 %collective-permute-start.5 = (bf16[32,4096]{1,0:T(8,128)(2,1)S(1)}, bf16[32,4096]{1,0:T(8,128)(2,1)S(1)}, u32[]{:S(2)}, u32[]{:S(2)}) collective-permute-start(bf16[32,4096]{1,0:T(8,128)(2,1)S(1)} %collective-permute-done.4.refs_6_), channel_id=1, source_target_pairs={{0,8},{2,10},{8,16},{10,18},{16,24},{18,26},{24,28},{26,30},{28,20... | collective-permute-start | bytes 786440 | tf_op jit(solution)/shard_map/ppermute | solution.py:211
  18.4 5.8 %collective-permute-done.9.refs_4_ = bf16[16,4096]{1,0:T(8,128)(2,1)S(1)} collective-permute-done((bf16[16,4096]{1,0:T(8,128)(2,1)S(1)}, bf16[16,4096]{1,0:T(8,128)(2,1)S(1)}, u32[]{:S(2)}, u32[]{:S(2)}) %collective-permute-start.9) | collective-permute-done | bytes 131104 | tf_op jit(solution)/shard_map/ppermute | solution.py:211
  24.2 1.3 %collective-permute-start.13 = (bf16[16,4096]{1,0:T(8,128)(2,1)S(1)}, bf16[16,4096]{1,0:T(8,128)(2,1)S(1)}, u32[]{:S(2)}, u32[]{:S(2)}) collective-permute-start(bf16[16,4096]{1,0:T(8,128)(2,1)S(1)} %collective-permute-done.8.refs_2_), channel_id=1, source_target_pairs={{0,8},{2,10},{8,16},{10,18},{16,24},{18,26},{24,28},{26,30},{28,20... | collective-permute-start | bytes 393224 | tf_op jit(solution)/shard_map/ppermute | solution.py:211
  27.0 5.0 %collective-permute-start.32 = (bf16[32,4096]{1,0:T(8,128)(2,1)S(1)}, bf16[32,4096]{1,0:T(8,128)(2,1)S(1)}, u32[]{:S(2)}, u32[]{:S(2)}) collective-permute-start(bf16[32,4096]{1,0:T(8,128)(2,1)S(1)} %copy-done.1), channel_id=1, source_target_pairs={{0,2},{2,0},{4,6},{6,4},{8,10},{10,8},{12,14},{14,12},{16,18},{18,... | collective-permute-start | bytes 786440 | tf_op jit(solution)/shard_map/ppermute | solution.py:185
  32.1 1.3 %collective-permute-start.34 = (bf16[32,4096]{1,0:T(8,128)(2,1)}, bf16[32,4096]{1,0:T(8,128)(2,1)S(1)}, u32[]{:S(2)}, u32[]{:S(2)}) collective-permute-start(bf16[32,4096]{1,0:T(8,128)(2,1)} %collective-permute-done.1.refs_4_), channel_id=1, source_target_pairs={{0,2},{2,0},{4,6},{6,4},{8,10},{10,8},{12,14},{14,12},{16,18},{18,... | collective-permute-start | bytes 786440 | tf_op jit(solution)/shard_map/ppermute | solution.py:185
  33.3 3.0 %collective-permute-start.35 = (bf16[32,4096]{1,0:T(8,128)(2,1)S(1)}, bf16[32,4096]{1,0:T(8,128)(2,1)S(1)}, u32[]{:S(2)}, u32[]{:S(2)}) collective-permute-start(bf16[32,4096]{1,0:T(8,128)(2,1)S(1)} %collective-permute-done.4.refs_6_), channel_id=1, source_target_pairs={{0,2},{2,0},{4,6},{6,4},{8,10},{10,8},{12,14},{14,12},{16,18},{18,... | collective-permute-start | bytes 786440 | tf_op jit(solution)/shard_map/ppermute | solution.py:185
  39.5 1.8 %collective-permute-start.18 = (bf16[16,4096]{1,0:T(8,128)(2,1)S(1)}, bf16[16,4096]{1,0:T(8,128)(2,1)S(1)}, u32[]{:S(2)}, u32[]{:S(2)}) collective-permute-start(bf16[16,4096]{1,0:T(8,128)(2,1)S(1)} %collective-permute-done.13.refs_6_), channel_id=1, source_target_pairs={{0,8},{2,10},{8,16},{10,18},{16,24},{18,26},{24,28},{26,30},{28,20... | collective-permute-start | bytes 393224 | tf_op jit(solution)/shard_map/ppermute | solution.py:211
  41.2 1.4 %order_rows.3.next_ref.rows_ref = bf16[512,4096]{1,0:T(8,128)(2,1)S(1)} custom-call(bf16[32,4096]{1,0:T(8,128)(2,1)S(1)} %copy-done.1, bf16[32,4096]{1,0:T(8,128)(2,1)S(1)} %collective-permute-done.32.refs_1_, bf16[32,4096]{1,0:T(8,128)(2,1)} %collective-permute-done.refs_2_, bf16[32,4096]{1,0:T(8,128)(2,1)S(1)} %collective-permute-done.33.refs_3_, ...), custom_call_target="tpu_custom_call" | custom-call | bytes 8388608 | tf_op jit(solution)/shard_map/order_rows/pallas_call | solution.py:238
  42.7 5.3 %early_projection.3.own_ref = f32[2320,256]{1,0:T(8,128)S(1)} custom-call(bf16[2320,4096]{1,0:T(8,128)(2,1)S(1)} %bitcast.12, bf16[512,4096]{1,0:T(8,128)(2,1)S(1)} %order_rows.3.next_ref.rows_ref), custom_call_target="tpu_custom_call" | custom-call | flops 4865392640 | bytes 23478272 | tf_op jit(solution)/shard_map/early_projection/pallas_call | solution.py:263
  48.6 1.8 %collective-permute-start.22 = (bf16[16,4096]{1,0:T(8,128)(2,1)S(1)}, bf16[16,4096]{1,0:T(8,128)(2,1)S(1)}, u32[]{:S(2)}, u32[]{:S(2)}) collective-permute-start(bf16[16,4096]{1,0:T(8,128)(2,1)S(1)} %collective-permute-done.18.refs_10_), channel_id=1, source_target_pairs={{0,8},{2,10},{8,16},{10,18},{16,24},{18,26},{24,28},{26,30},{28,20... | collective-permute-start | bytes 393224 | tf_op jit(solution)/shard_map/ppermute | solution.py:211
  51.0 2.7 %early_projection.4 = bf16[1168,256]{1,0:T(8,128)(2,1)S(1)} custom-call(bf16[2320,4096]{1,0:T(8,128)(2,1)S(1)} %bitcast.13, bf16[512,4096]{1,0:T(8,128)(2,1)S(1)} %order_rows.3.next_ref.rows_ref), custom_call_target="tpu_custom_call" | custom-call | flops 2449473536 | bytes 12861440 | tf_op jit(solution)/shard_map/early_projection/pallas_call | solution.py:263
  54.6 1.5 %collective-permute-start.25 = (bf16[2,16,2320]{2,1,0:T(8,128)(2,1)S(1)}, bf16[2,16,2320]{2,1,0:T(8,128)(2,1)S(1)}, u32[]{:S(2)}, u32[]{:S(2)}) collective-permute-start(bf16[2,16,2320]{2,1,0:T(8,128)(2,1)S(1)} %get-tuple-element.43), channel_id=1, source_target_pairs={{0,4},{2,6},{4,0},{6,2},{8,12},{10,14},{12,8},{14,10},{16,20},{18,... | collective-permute-start | bytes 445448 | tf_op jit(solution)/shard_map/ppermute | solution.py:185
  57.4 2.3 %collective-permute-start.28 = (bf16[2,16,2320]{2,1,0:T(8,128)(2,1)S(1)}, bf16[2,16,2320]{2,1,0:T(8,128)(2,1)S(1)}, u32[]{:S(2)}, u32[]{:S(2)}) collective-permute-start(bf16[2,16,2320]{2,1,0:T(8,128)(2,1)S(1)} %get-tuple-element.46), channel_id=1, source_target_pairs={{0,16},{2,18},{4,20},{6,22},{8,24},{10,26},{12,28},{14,30},{16,0},... | collective-permute-start | bytes 445448 | tf_op jit(solution)/shard_map/ppermute | solution.py:185
  59.7 2.6 %early_projection.5 = bf16[1152,256]{1,0:T(8,128)(2,1)S(1)} custom-call(bf16[2320,4096]{1,0:T(8,128)(2,1)S(1)} %bitcast.14, bf16[512,4096]{1,0:T(8,128)(2,1)S(1)} %order_rows.3.next_ref.rows_ref), custom_call_target="tpu_custom_call" | custom-call | flops 2415919104 | bytes 12713984 | tf_op jit(solution)/shard_map/early_projection/pallas_call | solution.py:263
  63.1 1.3 %collective-permute-start.41 = (bf16[1168,256]{1,0:T(8,128)(2,1)S(1)}, bf16[1168,256]{1,0:T(8,128)(2,1)S(1)}, u32[]{:S(2)}, u32[]{:S(2)}) collective-permute-start(bf16[1168,256]{1,0:T(8,128)(2,1)S(1)} %early_projection.4), channel_id=1, source_target_pairs={{0,1},{1,0},{2,3},{3,2},{4,5},{5,4},{6,7},{7,6},{8,9},{9,8},{10,11... | collective-permute-start | bytes 1794056 | tf_op jit(solution)/shard_map/ppermute | solution.py:189
  64.4 1.1 %collective-permute-start.29 = (bf16[2,16,2320]{2,1,0:T(8,128)(2,1)S(1)}, bf16[2,16,2320]{2,1,0:T(8,128)(2,1)S(1)}, u32[]{:S(2)}, u32[]{:S(2)}) collective-permute-start(bf16[2,16,2320]{2,1,0:T(8,128)(2,1)S(1)} %get-tuple-element.47), channel_id=1, source_target_pairs={{0,20},{2,22},{4,16},{6,18},{8,28},{10,30},{12,24},{14,26},{16,4},... | collective-permute-start | bytes 445448 | tf_op jit(solution)/shard_map/ppermute | solution.py:185
  66.1 2.1 %collective-permute-start.30 = (bf16[2,16,2320]{2,1,0:T(8,128)(2,1)S(1)}, bf16[2,16,2320]{2,1,0:T(8,128)(2,1)S(1)}, u32[]{:S(2)}, u32[]{:S(2)}) collective-permute-start(bf16[2,16,2320]{2,1,0:T(8,128)(2,1)S(1)} %get-tuple-element.48), channel_id=1, source_target_pairs={{0,24},{2,26},{4,28},{6,30},{8,16},{10,18},{12,20},{14,22},{16,8},... | collective-permute-start | bytes 445448 | tf_op jit(solution)/shard_map/ppermute | solution.py:185
  69.3 1.3 %low_rank_rows.1 = (f32[256,256]{1,0:T(8,128)S(1)}, f32[256,256]{1,0:T(8,128)S(1)}) custom-call(bf16[512,4096]{1,0:T(8,128)(2,1)S(1)} %order_rows.3.next_ref.rows_ref, bf16[256,4096]{1,0:T(8,128)(2,1)S(1)} %order_rows.2.left_ref), custom_call_target="tpu_custom_call" | custom-call | flops 68719476736 | bytes 6815744 | tf_op jit(solution)/shard_map/low_rank_rows/pallas_call | solution.py:287
  70.5 10.5 %collective-permute-done.29.refs_5_ = bf16[2,16,2320]{2,1,0:T(8,128)(2,1)S(1)} collective-permute-done((bf16[2,16,2320]{2,1,0:T(8,128)(2,1)S(1)}, bf16[2,16,2320]{2,1,0:T(8,128)(2,1)S(1)}, u32[]{:S(2)}, u32[]{:S(2)}) %collective-permute-start.29) | collective-permute-done | bytes 148512 | tf_op jit(solution)/shard_map/ppermute | solution.py:185
  81.3 4.9 %collective-permute-done.30.refs_6_ = bf16[2,16,2320]{2,1,0:T(8,128)(2,1)S(1)} collective-permute-done((bf16[2,16,2320]{2,1,0:T(8,128)(2,1)S(1)}, bf16[2,16,2320]{2,1,0:T(8,128)(2,1)S(1)}, u32[]{:S(2)}, u32[]{:S(2)}) %collective-permute-start.30) | collective-permute-done | bytes 148512 | tf_op jit(solution)/shard_map/ppermute | solution.py:185
  86.2 3.7 %collective-permute-done.31.refs_7_ = bf16[2,16,2320]{2,1,0:T(8,128)(2,1)S(1)} collective-permute-done((bf16[2,16,2320]{2,1,0:T(8,128)(2,1)S(1)}, bf16[2,16,2320]{2,1,0:T(8,128)(2,1)S(1)}, u32[]{:S(2)}, u32[]{:S(2)}) %collective-permute-start.31) | collective-permute-done | bytes 148512 | tf_op jit(solution)/shard_map/ppermute | solution.py:185
  89.8 9.8 %merge.1 = (bf16[2320,4096]{1,0:T(8,128)(2,1)}, bf16[2320,256]{1,0:T(8,128)(2,1)S(1)}) custom-call(bf16[2320,4096]{1,0:T(8,128)(2,1)S(1)} %bitcast.15, bf16[256,4096]{1,0:T(8,128)(2,1)S(1)} %order_rows.2.left_ref, bf16[2,16,2320]{2,1,0:T(8,128)(2,1)S(1)} %get-tuple-element.42.refs_0_, bf16[2,16,2320]{2,1,0:T(8,128)(2,1)S(1)} %collective-permute-done.25.refs_1_, ...), custom_call_target="tpu_custom_call" | custom-call | flops 4865392640 | bytes 41295872 | tf_op jit(solution)/shard_map/merge/pallas_call | solution.py:392
  99.6 1.9 %finish.1 = bf16[2320,256]{1,0:T(8,128)(2,1)} custom-call(f32[256,256]{1,0:T(8,128)S(1)} %get-tuple-element.53.own_low_ref, f32[256,256]{1,0:T(8,128)S(1)} %collective-permute-done.40.other_low_ref, bf16[2320,256]{1,0:T(8,128)(2,1)S(1)} %get-tuple-element.55.turned_ref, f32[2320,256]{1,0:T(8,128)S(1)} %early_projection.3.own_ref, ...), custom_call_target="tpu_custom_call" | custom-call | flops 608174080 | bytes 5939200 | tf_op jit(solution)/shard_map/finish/pallas_call | solution.py:429
  (91 shorter events, 12.8 us)
Async XLA Ops:
  0.7 7.5 %collective-permute-start.1 = (bf16[32,4096]{1,0:T(8,128)(2,1)}, bf16[32,4096]{1,0:T(8,128)(2,1)}, u32[]{:S(2)}, u32[]{:S(2)}) collective-permute-start(bf16[32,4096]{1,0:T(8,128)(2,1)} %refs_0_.1), channel_id=1, source_target_pairs={{0,4},{2,6},{8,0},{10,2},{16,8},{18,10},{24,16},{26,18},{28,24},{3... | collective-permute-start | bytes 786440 | tf_op jit(solution)/shard_map/ppermute | solution.py:211
  0.7 7.5 %collective-permute-start = (bf16[32,4096]{1,0:T(8,128)(2,1)}, bf16[32,4096]{1,0:T(8,128)(2,1)}, u32[]{:S(2)}, u32[]{:S(2)}) collective-permute-start(bf16[32,4096]{1,0:T(8,128)(2,1)} %refs_0_.1), channel_id=1, source_target_pairs={{0,8},{2,10},{8,16},{10,18},{16,24},{18,26},{24,28},{26,30},{28,20... | collective-permute-start | bytes 786440 | tf_op jit(solution)/shard_map/ppermute | solution.py:211
  9.5 6.0 %collective-permute-start.4 = (bf16[32,4096]{1,0:T(8,128)(2,1)}, bf16[32,4096]{1,0:T(8,128)(2,1)S(1)}, u32[]{:S(2)}, u32[]{:S(2)}) collective-permute-start(bf16[32,4096]{1,0:T(8,128)(2,1)} %collective-permute-done.refs_2_), channel_id=1, source_target_pairs={{0,8},{2,10},{8,16},{10,18},{16,24},{18,26},{24,28},{26,30},{28,20... | collective-permute-start | bytes 786440 | tf_op jit(solution)/shard_map/ppermute | solution.py:211
  10.8 6.0 %collective-permute-start.6 = (bf16[32,4096]{1,0:T(8,128)(2,1)}, bf16[32,4096]{1,0:T(8,128)(2,1)S(1)}, u32[]{:S(2)}, u32[]{:S(2)}) collective-permute-start(bf16[32,4096]{1,0:T(8,128)(2,1)} %collective-permute-done.1.refs_4_), channel_id=1, source_target_pairs={{0,4},{2,6},{8,0},{10,2},{16,8},{18,10},{24,16},{26,18},{28,24},{3... | collective-permute-start | bytes 786440 | tf_op jit(solution)/shard_map/ppermute | solution.py:211
  12.7 19.3 %collective-permute-start.15 = (bf16[8,16,2320]{2,1,0:T(8,128)(2,1)S(1)}, bf16[8,16,2320]{2,1,0:T(8,128)(2,1)S(1)}, u32[]{:S(2)}, u32[]{:S(2)}) collective-permute-start(bf16[8,16,2320]{2,1,0:T(8,128)(2,1)S(1)} %get-tuple-element.36.own_ref), channel_id=1, source_target_pairs={{0,1},{1,0},{2,3},{3,2},{4,5},{5,4},{6,7},{7,6},{8,9},{9,8},{10,11... | collective-permute-start | bytes 1781768 | tf_op jit(solution)/shard_map/ppermute | solution.py:189
  15.5 8.7 %collective-permute-start.5 = (bf16[32,4096]{1,0:T(8,128)(2,1)S(1)}, bf16[32,4096]{1,0:T(8,128)(2,1)S(1)}, u32[]{:S(2)}, u32[]{:S(2)}) collective-permute-start(bf16[32,4096]{1,0:T(8,128)(2,1)S(1)} %collective-permute-done.4.refs_6_), channel_id=1, source_target_pairs={{0,8},{2,10},{8,16},{10,18},{16,24},{18,26},{24,28},{26,30},{28,20... | collective-permute-start | bytes 786440 | tf_op jit(solution)/shard_map/ppermute | solution.py:211
  16.8 7.4 %collective-permute-start.7 = (bf16[32,4096]{1,0:T(8,128)(2,1)S(1)}, bf16[32,4096]{1,0:T(8,128)(2,1)S(1)}, u32[]{:S(2)}, u32[]{:S(2)}) collective-permute-start(bf16[32,4096]{1,0:T(8,128)(2,1)S(1)} %collective-permute-done.6.refs_8_), channel_id=1, source_target_pairs={{0,4},{2,6},{8,0},{10,2},{16,8},{18,10},{24,16},{26,18},{28,24},{3... | collective-permute-start | bytes 786440 | tf_op jit(solution)/shard_map/ppermute | solution.py:211
  16.9 7.3 %collective-permute-start.9 = (bf16[16,4096]{1,0:T(8,128)(2,1)S(1)}, bf16[16,4096]{1,0:T(8,128)(2,1)S(1)}, u32[]{:S(2)}, u32[]{:S(2)}) collective-permute-start(bf16[16,4096]{1,0:T(8,128)(2,1)S(1)} %get-tuple-element.30.refs_0_), channel_id=1, source_target_pairs={{0,4},{2,6},{8,0},{10,2},{16,8},{18,10},{24,16},{26,18},{28,24},{3... | collective-permute-start | bytes 393224 | tf_op jit(solution)/shard_map/ppermute | solution.py:211
  17.9 6.3 %collective-permute-start.8 = (bf16[16,4096]{1,0:T(8,128)(2,1)S(1)}, bf16[16,4096]{1,0:T(8,128)(2,1)S(1)}, u32[]{:S(2)}, u32[]{:S(2)}) collective-permute-start(bf16[16,4096]{1,0:T(8,128)(2,1)S(1)} %get-tuple-element.30.refs_0_), channel_id=1, source_target_pairs={{0,8},{2,10},{8,16},{10,18},{16,24},{18,26},{24,28},{26,30},{28,20... | collective-permute-start | bytes 393224 | tf_op jit(solution)/shard_map/ppermute | solution.py:211
  24.2 7.8 %collective-permute-start.13 = (bf16[16,4096]{1,0:T(8,128)(2,1)S(1)}, bf16[16,4096]{1,0:T(8,128)(2,1)S(1)}, u32[]{:S(2)}, u32[]{:S(2)}) collective-permute-start(bf16[16,4096]{1,0:T(8,128)(2,1)S(1)} %collective-permute-done.8.refs_2_), channel_id=1, source_target_pairs={{0,8},{2,10},{8,16},{10,18},{16,24},{18,26},{24,28},{26,30},{28,20... | collective-permute-start | bytes 393224 | tf_op jit(solution)/shard_map/ppermute | solution.py:211
  25.5 10.8 %collective-permute-start.12 = (bf16[32,4096]{1,0:T(8,128)(2,1)S(1)}, bf16[32,4096]{1,0:T(8,128)(2,1)S(1)}, u32[]{:S(2)}, u32[]{:S(2)}) collective-permute-start(bf16[32,4096]{1,0:T(8,128)(2,1)S(1)} %collective-permute-done.5.refs_10_), channel_id=1, source_target_pairs={{0,8},{2,10},{8,16},{10,18},{16,24},{18,26},{24,28},{26,30},{28,20... | collective-permute-start | bytes 786440 | tf_op jit(solution)/shard_map/ppermute | solution.py:211
  26.6 6.8 %collective-permute-start.14 = (bf16[16,4096]{1,0:T(8,128)(2,1)S(1)}, bf16[16,4096]{1,0:T(8,128)(2,1)S(1)}, u32[]{:S(2)}, u32[]{:S(2)}) collective-permute-start(bf16[16,4096]{1,0:T(8,128)(2,1)S(1)} %collective-permute-done.9.refs_4_), channel_id=1, source_target_pairs={{0,4},{2,6},{8,0},{10,2},{16,8},{18,10},{24,16},{26,18},{28,24},{3... | collective-permute-start | bytes 393224 | tf_op jit(solution)/shard_map/ppermute | solution.py:211
  27.0 9.3 %collective-permute-start.32 = (bf16[32,4096]{1,0:T(8,128)(2,1)S(1)}, bf16[32,4096]{1,0:T(8,128)(2,1)S(1)}, u32[]{:S(2)}, u32[]{:S(2)}) collective-permute-start(bf16[32,4096]{1,0:T(8,128)(2,1)S(1)} %copy-done.1), channel_id=1, source_target_pairs={{0,2},{2,0},{4,6},{6,4},{8,10},{10,8},{12,14},{14,12},{16,18},{18,... | collective-permute-start | bytes 786440 | tf_op jit(solution)/shard_map/ppermute | solution.py:185
  38.4 12.6 %collective-permute-start.24 = (bf16[8,16,2320]{2,1,0:T(8,128)(2,1)S(1)}, bf16[8,16,2320]{2,1,0:T(8,128)(2,1)S(1)}, u32[]{:S(2)}, u32[]{:S(2)}) collective-permute-start(bf16[8,16,2320]{2,1,0:T(8,128)(2,1)S(1)} %get-tuple-element.41), channel_id=1, source_target_pairs={{0,2},{2,0},{4,6},{6,4},{8,10},{10,8},{12,14},{14,12},{16,18},{18,... | collective-permute-start | bytes 1781768 | tf_op jit(solution)/shard_map/ppermute | solution.py:185
  39.0 9.0 %collective-permute-start.10 = (bf16[16,4096]{1,0:T(8,128)(2,1)S(1)}, bf16[16,4096]{1,0:T(8,128)(2,1)S(1)}, u32[]{:S(2)}, u32[]{:S(2)}) collective-permute-start(bf16[16,4096]{1,0:T(8,128)(2,1)S(1)} %collective-permute-done.8.refs_2_), channel_id=1, source_target_pairs={{0,2},{2,0},{4,6},{6,4},{8,10},{10,8},{12,14},{14,12},{16,18},{18,... | collective-permute-start | bytes 393224 | tf_op jit(solution)/shard_map/ppermute | solution.py:185
  39.0 9.4 %collective-permute-start.11 = (bf16[16,4096]{1,0:T(8,128)(2,1)S(1)}, bf16[16,4096]{1,0:T(8,128)(2,1)S(1)}, u32[]{:S(2)}, u32[]{:S(2)}) collective-permute-start(bf16[16,4096]{1,0:T(8,128)(2,1)S(1)} %collective-permute-done.9.refs_4_), channel_id=1, source_target_pairs={{0,2},{2,0},{4,6},{6,4},{8,10},{10,8},{12,14},{14,12},{16,18},{18,... | collective-permute-start | bytes 393224 | tf_op jit(solution)/shard_map/ppermute | solution.py:185
  39.5 9.1 %collective-permute-start.18 = (bf16[16,4096]{1,0:T(8,128)(2,1)S(1)}, bf16[16,4096]{1,0:T(8,128)(2,1)S(1)}, u32[]{:S(2)}, u32[]{:S(2)}) collective-permute-start(bf16[16,4096]{1,0:T(8,128)(2,1)S(1)} %collective-permute-done.13.refs_6_), channel_id=1, source_target_pairs={{0,8},{2,10},{8,16},{10,18},{16,24},{18,26},{24,28},{26,30},{28,20... | collective-permute-start | bytes 393224 | tf_op jit(solution)/shard_map/ppermute | solution.py:211
  42.6 7.7 %collective-permute-start.20 = (bf16[16,4096]{1,0:T(8,128)(2,1)S(1)}, bf16[16,4096]{1,0:T(8,128)(2,1)S(1)}, u32[]{:S(2)}, u32[]{:S(2)}) collective-permute-start(bf16[16,4096]{1,0:T(8,128)(2,1)S(1)} %collective-permute-done.14.refs_8_), channel_id=1, source_target_pairs={{0,4},{2,6},{8,0},{10,2},{16,8},{18,10},{24,16},{26,18},{28,24},{3... | collective-permute-start | bytes 393224 | tf_op jit(solution)/shard_map/ppermute | solution.py:211
  48.0 6.6 %collective-permute-start.16 = (bf16[16,4096]{1,0:T(8,128)(2,1)S(1)}, bf16[16,4096]{1,0:T(8,128)(2,1)S(1)}, u32[]{:S(2)}, u32[]{:S(2)}) collective-permute-start(bf16[16,4096]{1,0:T(8,128)(2,1)S(1)} %collective-permute-done.13.refs_6_), channel_id=1, source_target_pairs={{0,2},{2,0},{4,6},{6,4},{8,10},{10,8},{12,14},{14,12},{16,18},{18,... | collective-permute-start | bytes 393224 | tf_op jit(solution)/shard_map/ppermute | solution.py:185
  48.4 7.7 %collective-permute-start.17 = (bf16[16,4096]{1,0:T(8,128)(2,1)S(1)}, bf16[16,4096]{1,0:T(8,128)(2,1)S(1)}, u32[]{:S(2)}, u32[]{:S(2)}) collective-permute-start(bf16[16,4096]{1,0:T(8,128)(2,1)S(1)} %collective-permute-done.14.refs_8_), channel_id=1, source_target_pairs={{0,2},{2,0},{4,6},{6,4},{8,10},{10,8},{12,14},{14,12},{16,18},{18,... | collective-permute-start | bytes 393224 | tf_op jit(solution)/shard_map/ppermute | solution.py:185
  50.9 6.4 %collective-permute-start.21 = (bf16[16,4096]{1,0:T(8,128)(2,1)S(1)}, bf16[16,4096]{1,0:T(8,128)(2,1)S(1)}, u32[]{:S(2)}, u32[]{:S(2)}) collective-permute-start(bf16[16,4096]{1,0:T(8,128)(2,1)S(1)} %collective-permute-done.20.refs_12_), channel_id=1, source_target_pairs={{0,2},{2,0},{4,6},{6,4},{8,10},{10,8},{12,14},{14,12},{16,18},{18,... | collective-permute-start | bytes 393224 | tf_op jit(solution)/shard_map/ppermute | solution.py:185
  53.8 8.6 %collective-permute-start.23 = (bf16[16,4096]{1,0:T(8,128)(2,1)S(1)}, bf16[16,4096]{1,0:T(8,128)(2,1)S(1)}, u32[]{:S(2)}, u32[]{:S(2)}) collective-permute-start(bf16[16,4096]{1,0:T(8,128)(2,1)S(1)} %collective-permute-done.22.refs_14_), channel_id=1, source_target_pairs={{0,2},{2,0},{4,6},{6,4},{8,10},{10,8},{12,14},{14,12},{16,18},{18,... | collective-permute-start | bytes 393224 | tf_op jit(solution)/shard_map/ppermute | solution.py:185
  54.6 8.5 %collective-permute-start.25 = (bf16[2,16,2320]{2,1,0:T(8,128)(2,1)S(1)}, bf16[2,16,2320]{2,1,0:T(8,128)(2,1)S(1)}, u32[]{:S(2)}, u32[]{:S(2)}) collective-permute-start(bf16[2,16,2320]{2,1,0:T(8,128)(2,1)S(1)} %get-tuple-element.43), channel_id=1, source_target_pairs={{0,4},{2,6},{4,0},{6,2},{8,12},{10,14},{12,8},{14,10},{16,20},{18,... | collective-permute-start | bytes 445448 | tf_op jit(solution)/shard_map/ppermute | solution.py:185
  56.1 8.3 %collective-permute-start.26 = (bf16[2,16,2320]{2,1,0:T(8,128)(2,1)S(1)}, bf16[2,16,2320]{2,1,0:T(8,128)(2,1)S(1)}, u32[]{:S(2)}, u32[]{:S(2)}) collective-permute-start(bf16[2,16,2320]{2,1,0:T(8,128)(2,1)S(1)} %get-tuple-element.44), channel_id=1, source_target_pairs={{0,8},{2,10},{4,12},{6,14},{8,0},{10,2},{12,4},{14,6},{16,24},{18,... | collective-permute-start | bytes 445448 | tf_op jit(solution)/shard_map/ppermute | solution.py:185
  56.3 9.8 %collective-permute-start.27 = (bf16[2,16,2320]{2,1,0:T(8,128)(2,1)S(1)}, bf16[2,16,2320]{2,1,0:T(8,128)(2,1)S(1)}, u32[]{:S(2)}, u32[]{:S(2)}) collective-permute-start(bf16[2,16,2320]{2,1,0:T(8,128)(2,1)S(1)} %get-tuple-element.45), channel_id=1, source_target_pairs={{0,12},{2,14},{4,8},{6,10},{8,4},{10,6},{12,0},{14,2},{16,28},{18,... | collective-permute-start | bytes 445448 | tf_op jit(solution)/shard_map/ppermute | solution.py:185
  57.4 11.5 %collective-permute-start.28 = (bf16[2,16,2320]{2,1,0:T(8,128)(2,1)S(1)}, bf16[2,16,2320]{2,1,0:T(8,128)(2,1)S(1)}, u32[]{:S(2)}, u32[]{:S(2)}) collective-permute-start(bf16[2,16,2320]{2,1,0:T(8,128)(2,1)S(1)} %get-tuple-element.46), channel_id=1, source_target_pairs={{0,16},{2,18},{4,20},{6,22},{8,24},{10,26},{12,28},{14,30},{16,0},... | collective-permute-start | bytes 445448 | tf_op jit(solution)/shard_map/ppermute | solution.py:185
  62.4 37.2 %collective-permute-start.42 = (bf16[1152,256]{1,0:T(8,128)(2,1)S(1)}, bf16[1152,256]{1,0:T(8,128)(2,1)S(1)}, u32[]{:S(2)}, u32[]{:S(2)}) collective-permute-start(bf16[1152,256]{1,0:T(8,128)(2,1)S(1)} %early_projection.5), channel_id=1, source_target_pairs={{0,1},{1,0},{2,3},{3,2},{4,5},{5,4},{6,7},{7,6},{8,9},{9,8},{10,11... | collective-permute-start | bytes 1769480 | tf_op jit(solution)/shard_map/ppermute | solution.py:189
  63.1 36.5 %collective-permute-start.41 = (bf16[1168,256]{1,0:T(8,128)(2,1)S(1)}, bf16[1168,256]{1,0:T(8,128)(2,1)S(1)}, u32[]{:S(2)}, u32[]{:S(2)}) collective-permute-start(bf16[1168,256]{1,0:T(8,128)(2,1)S(1)} %early_projection.4), channel_id=1, source_target_pairs={{0,1},{1,0},{2,3},{3,2},{4,5},{5,4},{6,7},{7,6},{8,9},{9,8},{10,11... | collective-permute-start | bytes 1794056 | tf_op jit(solution)/shard_map/ppermute | solution.py:189
  64.4 16.7 %collective-permute-start.29 = (bf16[2,16,2320]{2,1,0:T(8,128)(2,1)S(1)}, bf16[2,16,2320]{2,1,0:T(8,128)(2,1)S(1)}, u32[]{:S(2)}, u32[]{:S(2)}) collective-permute-start(bf16[2,16,2320]{2,1,0:T(8,128)(2,1)S(1)} %get-tuple-element.47), channel_id=1, source_target_pairs={{0,20},{2,22},{4,16},{6,18},{8,28},{10,30},{12,24},{14,26},{16,4},... | collective-permute-start | bytes 445448 | tf_op jit(solution)/shard_map/ppermute | solution.py:185
  66.1 20.1 %collective-permute-start.30 = (bf16[2,16,2320]{2,1,0:T(8,128)(2,1)S(1)}, bf16[2,16,2320]{2,1,0:T(8,128)(2,1)S(1)}, u32[]{:S(2)}, u32[]{:S(2)}) collective-permute-start(bf16[2,16,2320]{2,1,0:T(8,128)(2,1)S(1)} %get-tuple-element.48), channel_id=1, source_target_pairs={{0,24},{2,26},{4,28},{6,30},{8,16},{10,18},{12,20},{14,22},{16,8},... | collective-permute-start | bytes 445448 | tf_op jit(solution)/shard_map/ppermute | solution.py:185
  68.9 20.9 %collective-permute-start.31 = (bf16[2,16,2320]{2,1,0:T(8,128)(2,1)S(1)}, bf16[2,16,2320]{2,1,0:T(8,128)(2,1)S(1)}, u32[]{:S(2)}, u32[]{:S(2)}) collective-permute-start(bf16[2,16,2320]{2,1,0:T(8,128)(2,1)S(1)} %get-tuple-element.49), channel_id=1, source_target_pairs={{0,28},{2,30},{4,24},{6,26},{8,20},{10,22},{12,16},{14,18},{16,12}... | collective-permute-start | bytes 445448 | tf_op jit(solution)/shard_map/ppermute | solution.py:185
  81.1 18.6 %collective-permute-start.40 = (f32[256,256]{1,0:T(8,128)S(1)}, f32[256,256]{1,0:T(8,128)S(1)}, u32[]{:S(2)}, u32[]{:S(2)}) collective-permute-start(f32[256,256]{1,0:T(8,128)S(1)} %get-tuple-element.54), channel_id=1, source_target_pairs={{0,1},{1,0},{2,3},{3,2},{4,5},{5,4},{6,7},{7,6},{8,9},{9,8},{10,11... | collective-permute-start | bytes 786440 | tf_op jit(solution)/shard_map/ppermute | solution.py:189
  (23 other events, 137.1 us)

commit v4 on v3

--- a/solution.py
+++ b/solution.py
@@ -369,7 +369,11 @@
                 for o in (0, 1):
                     worker = 2 * ((device // 2) ^ flip) + (device + o) % 2
                     right_ref[pl.ds(pl.multiple_of(worker * rank, rank), rank), :] = ref[o]
-            for at in range(0, columns, 256):
+
+        for at in range(0, columns, 256):
+
+            @pl.when(step == at // tile)
+            def _():
                 width = min(256, columns - at)
                 unit = lax.broadcasted_iota(jnp.int32, (width, width), 0)
                 unit = unit == lax.broadcasted_iota(jnp.int32, (width, width), 1)

time: 102 us -> 102 us (level)
  no operation moved by 1% of the time
where the time goes in v4:
time: 102 us
  starting transfers between devices  38.6 us (38%)
  Pallas kernels  31.5 us (31%)
  waiting for transfers between devices  29.1 us (29%)
  local copies, waits for them, and re-layouts  1.53 us (2%)
    ppermute x24, starting transfers between devices, across(): return lax.ppermute(value, 'wide', [(i, i ^ flip) for i in range(wide)])  22.1 us
    ppermute x24, waiting for transfers between devices, across(): return lax.ppermute(value, 'wide', [(i, i ^ flip) for i in range(wide)])  20.4 us
    ppermute x14, starting transfers between devices, along(): return lax.ppermute(value, 'wide', ring_links(wide, step))  12.3 us
    pallas_call x3, Pallas kernels, early_projection(): plain_call(kernel, 2 * half * depth * (last - first), 2 * depth * (last -...  10.6 us
    pallas_call x1, Pallas kernels, merge(): plain_call(kernel, 2 * depth * columns * ranks, 4 * depth * columns + 2 *...  10 us
    ppermute x14, waiting for transfers between devices, along(): return lax.ppermute(value, 'wide', ring_links(wide, step))  8.78 us
    ppermute x5, starting transfers between devices, other_side(): return lax.ppermute(value, 'narrow', [(0, 1), (1, 0)])  4.17 us
    pallas_call x1, Pallas kernels, products(): plain_call(kernel, 6 * rank * (tokens * columns + pool * features), 2 * t...  3.21 us
  transfers between devices with their start and end apart: 43, of which 9 were waited for; matrix products, arithmetic and copies ran while one was open for 0% of the time, Pallas kernels for 29%

profile of v4, /device:TPU:9, one launch (start us, length us, event | category | flops | bytes accessed | tf_op | source)
XLA Modules:
  0.0 101.8 jit_solution(17672568644297154474)
XLA Ops:
  0.7 1.4 %collective-permute-start = (bf16[32,4096]{1,0:T(8,128)(2,1)}, bf16[32,4096]{1,0:T(8,128)(2,1)}, u32[]{:S(2)}, u32[]{:S(2)}) collective-permute-start(bf16[32,4096]{1,0:T(8,128)(2,1)} %refs_0_.1), channel_id=1, source_target_pairs={{0,8},{2,10},{8,16},{10,18},{16,24},{18,26},{24,28},{26,30},{28,20... | collective-permute-start | bytes 786440 | tf_op jit(solution)/shard_map/ppermute | solution.py:211
  2.2 1.2 %copy-done.3 = bf16[1,128,18560]{2,1,0:T(8,128)(2,1)S(1)} copy-done((bf16[1,128,18560]{2,1,0:T(8,128)(2,1)S(1)}, bf16[1,128,18560]{2,1,0:T(8,128)(2,1)}, u32[]{:S(2)}) %copy-start.3) | copy-done | bytes 4751384
  3.7 3.2 %products.1.own_ref = f32[32,128]{1,0:T(8,128)S(1)} custom-call(bf16[128,4096]{1,0:T(8,128)(2,1)S(1)} %bitcast.22, f32[16,4096]{1,0:T(8,128)S(1)} %bitcast.24, bf16[128,18560]{1,0:T(8,128)(2,1)S(1)} %bitcast.16, f32[16,18560]{1,0:T(8,128)S(1)} %bitcast.18, f32[8,128]{1,0:T(8,128)S(1)} %opening.1._), custom_call_target="tpu_custom_call" | custom-call | flops 142539227136 | bytes 7249920 | tf_op jit(solution)/shard_map/products/pallas_call | solution.py:118
  6.9 1.3 %collective-permute-done.1.refs_4_ = bf16[32,4096]{1,0:T(8,128)(2,1)} collective-permute-done((bf16[32,4096]{1,0:T(8,128)(2,1)}, bf16[32,4096]{1,0:T(8,128)(2,1)}, u32[]{:S(2)}, u32[]{:S(2)}) %collective-permute-start.1) | collective-permute-done | bytes 262176 | tf_op jit(solution)/shard_map/ppermute | solution.py:211
  8.3 1.2 %collective-permute-start.2 = (f32[32,128]{1,0:T(8,128)S(1)}, f32[32,128]{1,0:T(8,128)S(1)}, u32[]{:S(2)}, u32[]{:S(2)}) collective-permute-start(f32[32,128]{1,0:T(8,128)S(1)} %products.1.own_ref), channel_id=1, source_target_pairs={{0,1},{1,0},{2,3},{3,2},{4,5},{5,4},{6,7},{7,6},{8,9},{9,8},{10,11... | collective-permute-start | bytes 49160 | tf_op jit(solution)/shard_map/ppermute | solution.py:189
  9.5 1.3 %collective-permute-start.4 = (bf16[32,4096]{1,0:T(8,128)(2,1)}, bf16[32,4096]{1,0:T(8,128)(2,1)S(1)}, u32[]{:S(2)}, u32[]{:S(2)}) collective-permute-start(bf16[32,4096]{1,0:T(8,128)(2,1)} %collective-permute-done.refs_2_), channel_id=1, source_target_pairs={{0,8},{2,10},{8,16},{10,18},{16,24},{18,26},{24,28},{26,30},{28,20... | collective-permute-start | bytes 786440 | tf_op jit(solution)/shard_map/ppermute | solution.py:211
  11.0 1.7 %adam.1 = (bf16[16,4096]{1,0:T(8,128)(2,1)S(1)}, bf16[8,16,2320]{2,1,0:T(8,128)(2,1)S(1)}) custom-call(s32[1,128]{1,0:T(1,128)S(1)} %copy-done.11, f32[32,128]{1,0:T(8,128)S(1)} %products.1.own_ref, f32[32,128]{1,0:T(8,128)S(1)} %collective-permute-done.2.other_ref, bf16[128,4096]{1,0:T(8,128)(2,1)S(1)} %bitcast.23, f32[16,4096]{1,0:T(8,128)S(1)} %bitcast.25, ...), custom_call_target="tpu_custom_call" | custom-call | flops 17817403392 | bytes 10874880 | tf_op jit(solution)/shard_map/adam/pallas_call | solution.py:167
  12.7 1.2 %collective-permute-start.15 = (bf16[8,16,2320]{2,1,0:T(8,128)(2,1)S(1)}, bf16[8,16,2320]{2,1,0:T(8,128)(2,1)S(1)}, u32[]{:S(2)}, u32[]{:S(2)}) collective-permute-start(bf16[8,16,2320]{2,1,0:T(8,128)(2,1)S(1)} %get-tuple-element.36.own_ref), channel_id=1, source_target_pairs={{0,1},{1,0},{2,3},{3,2},{4,5},{5,4},{6,7},{7,6},{8,9},{9,8},{10,11... | collective-permute-start | bytes 1781768 | tf_op jit(solution)/shard_map/ppermute | solution.py:189
  13.9 1.6 %collective-permute-done.4.refs_6_ = bf16[32,4096]{1,0:T(8,128)(2,1)S(1)} collective-permute-done((bf16[32,4096]{1,0:T(8,128)(2,1)}, bf16[32,4096]{1,0:T(8,128)(2,1)S(1)}, u32[]{:S(2)}, u32[]{:S(2)}) %collective-permute-start.4) | collective-permute-done | bytes 262176 | tf_op jit(solution)/shard_map/ppermute | solution.py:211
  15.5 1.3 %collective-permute-start.5 = (bf16[32,4096]{1,0:T(8,128)(2,1)S(1)}, bf16[32,4096]{1,0:T(8,128)(2,1)S(1)}, u32[]{:S(2)}, u32[]{:S(2)}) collective-permute-start(bf16[32,4096]{1,0:T(8,128)(2,1)S(1)} %collective-permute-done.4.refs_6_), channel_id=1, source_target_pairs={{0,8},{2,10},{8,16},{10,18},{16,24},{18,26},{24,28},{26,30},{28,20... | collective-permute-start | bytes 786440 | tf_op jit(solution)/shard_map/ppermute | solution.py:211
  18.4 5.8 %collective-permute-done.9.refs_4_ = bf16[16,4096]{1,0:T(8,128)(2,1)S(1)} collective-permute-done((bf16[16,4096]{1,0:T(8,128)(2,1)S(1)}, bf16[16,4096]{1,0:T(8,128)(2,1)S(1)}, u32[]{:S(2)}, u32[]{:S(2)}) %collective-permute-start.9) | collective-permute-done | bytes 131104 | tf_op jit(solution)/shard_map/ppermute | solution.py:211
  24.2 1.3 %collective-permute-start.13 = (bf16[16,4096]{1,0:T(8,128)(2,1)S(1)}, bf16[16,4096]{1,0:T(8,128)(2,1)S(1)}, u32[]{:S(2)}, u32[]{:S(2)}) collective-permute-start(bf16[16,4096]{1,0:T(8,128)(2,1)S(1)} %collective-permute-done.8.refs_2_), channel_id=1, source_target_pairs={{0,8},{2,10},{8,16},{10,18},{16,24},{18,26},{24,28},{26,30},{28,20... | collective-permute-start | bytes 393224 | tf_op jit(solution)/shard_map/ppermute | solution.py:211
  27.0 5.0 %collective-permute-start.32 = (bf16[32,4096]{1,0:T(8,128)(2,1)S(1)}, bf16[32,4096]{1,0:T(8,128)(2,1)S(1)}, u32[]{:S(2)}, u32[]{:S(2)}) collective-permute-start(bf16[32,4096]{1,0:T(8,128)(2,1)S(1)} %copy-done.1), channel_id=1, source_target_pairs={{0,2},{2,0},{4,6},{6,4},{8,10},{10,8},{12,14},{14,12},{16,18},{18,... | collective-permute-start | bytes 786440 | tf_op jit(solution)/shard_map/ppermute | solution.py:185
  32.1 1.3 %collective-permute-start.34 = (bf16[32,4096]{1,0:T(8,128)(2,1)}, bf16[32,4096]{1,0:T(8,128)(2,1)S(1)}, u32[]{:S(2)}, u32[]{:S(2)}) collective-permute-start(bf16[32,4096]{1,0:T(8,128)(2,1)} %collective-permute-done.1.refs_4_), channel_id=1, source_target_pairs={{0,2},{2,0},{4,6},{6,4},{8,10},{10,8},{12,14},{14,12},{16,18},{18,... | collective-permute-start | bytes 786440 | tf_op jit(solution)/shard_map/ppermute | solution.py:185
  33.3 3.0 %collective-permute-start.35 = (bf16[32,4096]{1,0:T(8,128)(2,1)S(1)}, bf16[32,4096]{1,0:T(8,128)(2,1)S(1)}, u32[]{:S(2)}, u32[]{:S(2)}) collective-permute-start(bf16[32,4096]{1,0:T(8,128)(2,1)S(1)} %collective-permute-done.4.refs_6_), channel_id=1, source_target_pairs={{0,2},{2,0},{4,6},{6,4},{8,10},{10,8},{12,14},{14,12},{16,18},{18,... | collective-permute-start | bytes 786440 | tf_op jit(solution)/shard_map/ppermute | solution.py:185
  39.5 1.8 %collective-permute-start.18 = (bf16[16,4096]{1,0:T(8,128)(2,1)S(1)}, bf16[16,4096]{1,0:T(8,128)(2,1)S(1)}, u32[]{:S(2)}, u32[]{:S(2)}) collective-permute-start(bf16[16,4096]{1,0:T(8,128)(2,1)S(1)} %collective-permute-done.13.refs_6_), channel_id=1, source_target_pairs={{0,8},{2,10},{8,16},{10,18},{16,24},{18,26},{24,28},{26,30},{28,20... | collective-permute-start | bytes 393224 | tf_op jit(solution)/shard_map/ppermute | solution.py:211
  41.2 1.4 %order_rows.3.next_ref.rows_ref = bf16[512,4096]{1,0:T(8,128)(2,1)S(1)} custom-call(bf16[32,4096]{1,0:T(8,128)(2,1)S(1)} %copy-done.1, bf16[32,4096]{1,0:T(8,128)(2,1)S(1)} %collective-permute-done.32.refs_1_, bf16[32,4096]{1,0:T(8,128)(2,1)} %collective-permute-done.refs_2_, bf16[32,4096]{1,0:T(8,128)(2,1)S(1)} %collective-permute-done.33.refs_3_, ...), custom_call_target="tpu_custom_call" | custom-call | bytes 8388608 | tf_op jit(solution)/shard_map/order_rows/pallas_call | solution.py:238
  42.7 5.3 %early_projection.3.own_ref = f32[2320,256]{1,0:T(8,128)S(1)} custom-call(bf16[2320,4096]{1,0:T(8,128)(2,1)S(1)} %bitcast.12, bf16[512,4096]{1,0:T(8,128)(2,1)S(1)} %order_rows.3.next_ref.rows_ref), custom_call_target="tpu_custom_call" | custom-call | flops 4865392640 | bytes 23478272 | tf_op jit(solution)/shard_map/early_projection/pallas_call | solution.py:263
  48.6 1.8 %collective-permute-start.22 = (bf16[16,4096]{1,0:T(8,128)(2,1)S(1)}, bf16[16,4096]{1,0:T(8,128)(2,1)S(1)}, u32[]{:S(2)}, u32[]{:S(2)}) collective-permute-start(bf16[16,4096]{1,0:T(8,128)(2,1)S(1)} %collective-permute-done.18.refs_10_), channel_id=1, source_target_pairs={{0,8},{2,10},{8,16},{10,18},{16,24},{18,26},{24,28},{26,30},{28,20... | collective-permute-start | bytes 393224 | tf_op jit(solution)/shard_map/ppermute | solution.py:211
  51.0 2.7 %early_projection.4 = bf16[1168,256]{1,0:T(8,128)(2,1)S(1)} custom-call(bf16[2320,4096]{1,0:T(8,128)(2,1)S(1)} %bitcast.13, bf16[512,4096]{1,0:T(8,128)(2,1)S(1)} %order_rows.3.next_ref.rows_ref), custom_call_target="tpu_custom_call" | custom-call | flops 2449473536 | bytes 12861440 | tf_op jit(solution)/shard_map/early_projection/pallas_call | solution.py:263
  54.6 1.5 %collective-permute-start.25 = (bf16[2,16,2320]{2,1,0:T(8,128)(2,1)S(1)}, bf16[2,16,2320]{2,1,0:T(8,128)(2,1)S(1)}, u32[]{:S(2)}, u32[]{:S(2)}) collective-permute-start(bf16[2,16,2320]{2,1,0:T(8,128)(2,1)S(1)} %get-tuple-element.43), channel_id=1, source_target_pairs={{0,4},{2,6},{4,0},{6,2},{8,12},{10,14},{12,8},{14,10},{16,20},{18,... | collective-permute-start | bytes 445448 | tf_op jit(solution)/shard_map/ppermute | solution.py:185
  57.4 2.3 %collective-permute-start.28 = (bf16[2,16,2320]{2,1,0:T(8,128)(2,1)S(1)}, bf16[2,16,2320]{2,1,0:T(8,128)(2,1)S(1)}, u32[]{:S(2)}, u32[]{:S(2)}) collective-permute-start(bf16[2,16,2320]{2,1,0:T(8,128)(2,1)S(1)} %get-tuple-element.46), channel_id=1, source_target_pairs={{0,16},{2,18},{4,20},{6,22},{8,24},{10,26},{12,28},{14,30},{16,0},... | collective-permute-start | bytes 445448 | tf_op jit(solution)/shard_map/ppermute | solution.py:185
  59.7 2.6 %early_projection.5 = bf16[1152,256]{1,0:T(8,128)(2,1)S(1)} custom-call(bf16[2320,4096]{1,0:T(8,128)(2,1)S(1)} %bitcast.14, bf16[512,4096]{1,0:T(8,128)(2,1)S(1)} %order_rows.3.next_ref.rows_ref), custom_call_target="tpu_custom_call" | custom-call | flops 2415919104 | bytes 12713984 | tf_op jit(solution)/shard_map/early_projection/pallas_call | solution.py:263
  63.1 1.3 %collective-permute-start.41 = (bf16[1168,256]{1,0:T(8,128)(2,1)S(1)}, bf16[1168,256]{1,0:T(8,128)(2,1)S(1)}, u32[]{:S(2)}, u32[]{:S(2)}) collective-permute-start(bf16[1168,256]{1,0:T(8,128)(2,1)S(1)} %early_projection.4), channel_id=1, source_target_pairs={{0,1},{1,0},{2,3},{3,2},{4,5},{5,4},{6,7},{7,6},{8,9},{9,8},{10,11... | collective-permute-start | bytes 1794056 | tf_op jit(solution)/shard_map/ppermute | solution.py:189
  64.4 1.1 %collective-permute-start.29 = (bf16[2,16,2320]{2,1,0:T(8,128)(2,1)S(1)}, bf16[2,16,2320]{2,1,0:T(8,128)(2,1)S(1)}, u32[]{:S(2)}, u32[]{:S(2)}) collective-permute-start(bf16[2,16,2320]{2,1,0:T(8,128)(2,1)S(1)} %get-tuple-element.47), channel_id=1, source_target_pairs={{0,20},{2,22},{4,16},{6,18},{8,28},{10,30},{12,24},{14,26},{16,4},... | collective-permute-start | bytes 445448 | tf_op jit(solution)/shard_map/ppermute | solution.py:185
  66.1 2.1 %collective-permute-start.30 = (bf16[2,16,2320]{2,1,0:T(8,128)(2,1)S(1)}, bf16[2,16,2320]{2,1,0:T(8,128)(2,1)S(1)}, u32[]{:S(2)}, u32[]{:S(2)}) collective-permute-start(bf16[2,16,2320]{2,1,0:T(8,128)(2,1)S(1)} %get-tuple-element.48), channel_id=1, source_target_pairs={{0,24},{2,26},{4,28},{6,30},{8,16},{10,18},{12,20},{14,22},{16,8},... | collective-permute-start | bytes 445448 | tf_op jit(solution)/shard_map/ppermute | solution.py:185
  69.3 1.3 %low_rank_rows.1 = (f32[256,256]{1,0:T(8,128)S(1)}, f32[256,256]{1,0:T(8,128)S(1)}) custom-call(bf16[512,4096]{1,0:T(8,128)(2,1)S(1)} %order_rows.3.next_ref.rows_ref, bf16[256,4096]{1,0:T(8,128)(2,1)S(1)} %order_rows.2.left_ref), custom_call_target="tpu_custom_call" | custom-call | flops 68719476736 | bytes 6815744 | tf_op jit(solution)/shard_map/low_rank_rows/pallas_call | solution.py:287
  70.5 10.5 %collective-permute-done.29.refs_5_ = bf16[2,16,2320]{2,1,0:T(8,128)(2,1)S(1)} collective-permute-done((bf16[2,16,2320]{2,1,0:T(8,128)(2,1)S(1)}, bf16[2,16,2320]{2,1,0:T(8,128)(2,1)S(1)}, u32[]{:S(2)}, u32[]{:S(2)}) %collective-permute-start.29) | collective-permute-done | bytes 148512 | tf_op jit(solution)/shard_map/ppermute | solution.py:185
  81.3 4.9 %collective-permute-done.30.refs_6_ = bf16[2,16,2320]{2,1,0:T(8,128)(2,1)S(1)} collective-permute-done((bf16[2,16,2320]{2,1,0:T(8,128)(2,1)S(1)}, bf16[2,16,2320]{2,1,0:T(8,128)(2,1)S(1)}, u32[]{:S(2)}, u32[]{:S(2)}) %collective-permute-start.30) | collective-permute-done | bytes 148512 | tf_op jit(solution)/shard_map/ppermute | solution.py:185
  86.2 3.7 %collective-permute-done.31.refs_7_ = bf16[2,16,2320]{2,1,0:T(8,128)(2,1)S(1)} collective-permute-done((bf16[2,16,2320]{2,1,0:T(8,128)(2,1)S(1)}, bf16[2,16,2320]{2,1,0:T(8,128)(2,1)S(1)}, u32[]{:S(2)}, u32[]{:S(2)}) %collective-permute-start.31) | collective-permute-done | bytes 148512 | tf_op jit(solution)/shard_map/ppermute | solution.py:185
  89.8 10.0 %merge.1 = (bf16[2320,4096]{1,0:T(8,128)(2,1)}, bf16[2320,256]{1,0:T(8,128)(2,1)S(1)}) custom-call(bf16[2320,4096]{1,0:T(8,128)(2,1)S(1)} %bitcast.15, bf16[256,4096]{1,0:T(8,128)(2,1)S(1)} %order_rows.2.left_ref, bf16[2,16,2320]{2,1,0:T(8,128)(2,1)S(1)} %get-tuple-element.42.refs_0_, bf16[2,16,2320]{2,1,0:T(8,128)(2,1)S(1)} %collective-permute-done.25.refs_1_, ...), custom_call_target="tpu_custom_call" | custom-call | flops 4865392640 | bytes 41295872 | tf_op jit(solution)/shard_map/merge/pallas_call | solution.py:396
  99.9 1.9 %finish.1 = bf16[2320,256]{1,0:T(8,128)(2,1)} custom-call(f32[256,256]{1,0:T(8,128)S(1)} %get-tuple-element.53.own_low_ref, f32[256,256]{1,0:T(8,128)S(1)} %collective-permute-done.40.other_low_ref, bf16[2320,256]{1,0:T(8,128)(2,1)S(1)} %get-tuple-element.55.turned_ref, f32[2320,256]{1,0:T(8,128)S(1)} %early_projection.3.own_ref, ...), custom_call_target="tpu_custom_call" | custom-call | flops 608174080 | bytes 5939200 | tf_op jit(solution)/shard_map/finish/pallas_call | solution.py:433
  (91 shorter events, 12.8 us)
Async XLA Ops:
  0.7 7.5 %collective-permute-start.1 = (bf16[32,4096]{1,0:T(8,128)(2,1)}, bf16[32,4096]{1,0:T(8,128)(2,1)}, u32[]{:S(2)}, u32[]{:S(2)}) collective-permute-start(bf16[32,4096]{1,0:T(8,128)(2,1)} %refs_0_.1), channel_id=1, source_target_pairs={{0,4},{2,6},{8,0},{10,2},{16,8},{18,10},{24,16},{26,18},{28,24},{3... | collective-permute-start | bytes 786440 | tf_op jit(solution)/shard_map/ppermute | solution.py:211
  0.7 7.5 %collective-permute-start = (bf16[32,4096]{1,0:T(8,128)(2,1)}, bf16[32,4096]{1,0:T(8,128)(2,1)}, u32[]{:S(2)}, u32[]{:S(2)}) collective-permute-start(bf16[32,4096]{1,0:T(8,128)(2,1)} %refs_0_.1), channel_id=1, source_target_pairs={{0,8},{2,10},{8,16},{10,18},{16,24},{18,26},{24,28},{26,30},{28,20... | collective-permute-start | bytes 786440 | tf_op jit(solution)/shard_map/ppermute | solution.py:211
  9.5 6.0 %collective-permute-start.4 = (bf16[32,4096]{1,0:T(8,128)(2,1)}, bf16[32,4096]{1,0:T(8,128)(2,1)S(1)}, u32[]{:S(2)}, u32[]{:S(2)}) collective-permute-start(bf16[32,4096]{1,0:T(8,128)(2,1)} %collective-permute-done.refs_2_), channel_id=1, source_target_pairs={{0,8},{2,10},{8,16},{10,18},{16,24},{18,26},{24,28},{26,30},{28,20... | collective-permute-start | bytes 786440 | tf_op jit(solution)/shard_map/ppermute | solution.py:211
  10.8 6.0 %collective-permute-start.6 = (bf16[32,4096]{1,0:T(8,128)(2,1)}, bf16[32,4096]{1,0:T(8,128)(2,1)S(1)}, u32[]{:S(2)}, u32[]{:S(2)}) collective-permute-start(bf16[32,4096]{1,0:T(8,128)(2,1)} %collective-permute-done.1.refs_4_), channel_id=1, source_target_pairs={{0,4},{2,6},{8,0},{10,2},{16,8},{18,10},{24,16},{26,18},{28,24},{3... | collective-permute-start | bytes 786440 | tf_op jit(solution)/shard_map/ppermute | solution.py:211
  12.7 19.3 %collective-permute-start.15 = (bf16[8,16,2320]{2,1,0:T(8,128)(2,1)S(1)}, bf16[8,16,2320]{2,1,0:T(8,128)(2,1)S(1)}, u32[]{:S(2)}, u32[]{:S(2)}) collective-permute-start(bf16[8,16,2320]{2,1,0:T(8,128)(2,1)S(1)} %get-tuple-element.36.own_ref), channel_id=1, source_target_pairs={{0,1},{1,0},{2,3},{3,2},{4,5},{5,4},{6,7},{7,6},{8,9},{9,8},{10,11... | collective-permute-start | bytes 1781768 | tf_op jit(solution)/shard_map/ppermute | solution.py:189
  15.5 8.7 %collective-permute-start.5 = (bf16[32,4096]{1,0:T(8,128)(2,1)S(1)}, bf16[32,4096]{1,0:T(8,128)(2,1)S(1)}, u32[]{:S(2)}, u32[]{:S(2)}) collective-permute-start(bf16[32,4096]{1,0:T(8,128)(2,1)S(1)} %collective-permute-done.4.refs_6_), channel_id=1, source_target_pairs={{0,8},{2,10},{8,16},{10,18},{16,24},{18,26},{24,28},{26,30},{28,20... | collective-permute-start | bytes 786440 | tf_op jit(solution)/shard_map/ppermute | solution.py:211
  16.8 7.4 %collective-permute-start.7 = (bf16[32,4096]{1,0:T(8,128)(2,1)S(1)}, bf16[32,4096]{1,0:T(8,128)(2,1)S(1)}, u32[]{:S(2)}, u32[]{:S(2)}) collective-permute-start(bf16[32,4096]{1,0:T(8,128)(2,1)S(1)} %collective-permute-done.6.refs_8_), channel_id=1, source_target_pairs={{0,4},{2,6},{8,0},{10,2},{16,8},{18,10},{24,16},{26,18},{28,24},{3... | collective-permute-start | bytes 786440 | tf_op jit(solution)/shard_map/ppermute | solution.py:211
  16.9 7.3 %collective-permute-start.9 = (bf16[16,4096]{1,0:T(8,128)(2,1)S(1)}, bf16[16,4096]{1,0:T(8,128)(2,1)S(1)}, u32[]{:S(2)}, u32[]{:S(2)}) collective-permute-start(bf16[16,4096]{1,0:T(8,128)(2,1)S(1)} %get-tuple-element.30.refs_0_), channel_id=1, source_target_pairs={{0,4},{2,6},{8,0},{10,2},{16,8},{18,10},{24,16},{26,18},{28,24},{3... | collective-permute-start | bytes 393224 | tf_op jit(solution)/shard_map/ppermute | solution.py:211
  17.9 6.3 %collective-permute-start.8 = (bf16[16,4096]{1,0:T(8,128)(2,1)S(1)}, bf16[16,4096]{1,0:T(8,128)(2,1)S(1)}, u32[]{:S(2)}, u32[]{:S(2)}) collective-permute-start(bf16[16,4096]{1,0:T(8,128)(2,1)S(1)} %get-tuple-element.30.refs_0_), channel_id=1, source_target_pairs={{0,8},{2,10},{8,16},{10,18},{16,24},{18,26},{24,28},{26,30},{28,20... | collective-permute-start | bytes 393224 | tf_op jit(solution)/shard_map/ppermute | solution.py:211
  24.2 7.8 %collective-permute-start.13 = (bf16[16,4096]{1,0:T(8,128)(2,1)S(1)}, bf16[16,4096]{1,0:T(8,128)(2,1)S(1)}, u32[]{:S(2)}, u32[]{:S(2)}) collective-permute-start(bf16[16,4096]{1,0:T(8,128)(2,1)S(1)} %collective-permute-done.8.refs_2_), channel_id=1, source_target_pairs={{0,8},{2,10},{8,16},{10,18},{16,24},{18,26},{24,28},{26,30},{28,20... | collective-permute-start | bytes 393224 | tf_op jit(solution)/shard_map/ppermute | solution.py:211
  25.5 10.8 %collective-permute-start.12 = (bf16[32,4096]{1,0:T(8,128)(2,1)S(1)}, bf16[32,4096]{1,0:T(8,128)(2,1)S(1)}, u32[]{:S(2)}, u32[]{:S(2)}) collective-permute-start(bf16[32,4096]{1,0:T(8,128)(2,1)S(1)} %collective-permute-done.5.refs_10_), channel_id=1, source_target_pairs={{0,8},{2,10},{8,16},{10,18},{16,24},{18,26},{24,28},{26,30},{28,20... | collective-permute-start | bytes 786440 | tf_op jit(solution)/shard_map/ppermute | solution.py:211
  26.6 6.8 %collective-permute-start.14 = (bf16[16,4096]{1,0:T(8,128)(2,1)S(1)}, bf16[16,4096]{1,0:T(8,128)(2,1)S(1)}, u32[]{:S(2)}, u32[]{:S(2)}) collective-permute-start(bf16[16,4096]{1,0:T(8,128)(2,1)S(1)} %collective-permute-done.9.refs_4_), channel_id=1, source_target_pairs={{0,4},{2,6},{8,0},{10,2},{16,8},{18,10},{24,16},{26,18},{28,24},{3... | collective-permute-start | bytes 393224 | tf_op jit(solution)/shard_map/ppermute | solution.py:211
  27.0 9.3 %collective-permute-start.32 = (bf16[32,4096]{1,0:T(8,128)(2,1)S(1)}, bf16[32,4096]{1,0:T(8,128)(2,1)S(1)}, u32[]{:S(2)}, u32[]{:S(2)}) collective-permute-start(bf16[32,4096]{1,0:T(8,128)(2,1)S(1)} %copy-done.1), channel_id=1, source_target_pairs={{0,2},{2,0},{4,6},{6,4},{8,10},{10,8},{12,14},{14,12},{16,18},{18,... | collective-permute-start | bytes 786440 | tf_op jit(solution)/shard_map/ppermute | solution.py:185
  38.4 12.6 %collective-permute-start.24 = (bf16[8,16,2320]{2,1,0:T(8,128)(2,1)S(1)}, bf16[8,16,2320]{2,1,0:T(8,128)(2,1)S(1)}, u32[]{:S(2)}, u32[]{:S(2)}) collective-permute-start(bf16[8,16,2320]{2,1,0:T(8,128)(2,1)S(1)} %get-tuple-element.41), channel_id=1, source_target_pairs={{0,2},{2,0},{4,6},{6,4},{8,10},{10,8},{12,14},{14,12},{16,18},{18,... | collective-permute-start | bytes 1781768 | tf_op jit(solution)/shard_map/ppermute | solution.py:185
  39.0 9.0 %collective-permute-start.10 = (bf16[16,4096]{1,0:T(8,128)(2,1)S(1)}, bf16[16,4096]{1,0:T(8,128)(2,1)S(1)}, u32[]{:S(2)}, u32[]{:S(2)}) collective-permute-start(bf16[16,4096]{1,0:T(8,128)(2,1)S(1)} %collective-permute-done.8.refs_2_), channel_id=1, source_target_pairs={{0,2},{2,0},{4,6},{6,4},{8,10},{10,8},{12,14},{14,12},{16,18},{18,... | collective-permute-start | bytes 393224 | tf_op jit(solution)/shard_map/ppermute | solution.py:185
  39.0 9.4 %collective-permute-start.11 = (bf16[16,4096]{1,0:T(8,128)(2,1)S(1)}, bf16[16,4096]{1,0:T(8,128)(2,1)S(1)}, u32[]{:S(2)}, u32[]{:S(2)}) collective-permute-start(bf16[16,4096]{1,0:T(8,128)(2,1)S(1)} %collective-permute-done.9.refs_4_), channel_id=1, source_target_pairs={{0,2},{2,0},{4,6},{6,4},{8,10},{10,8},{12,14},{14,12},{16,18},{18,... | collective-permute-start | bytes 393224 | tf_op jit(solution)/shard_map/ppermute | solution.py:185
  39.5 9.1 %collective-permute-start.18 = (bf16[16,4096]{1,0:T(8,128)(2,1)S(1)}, bf16[16,4096]{1,0:T(8,128)(2,1)S(1)}, u32[]{:S(2)}, u32[]{:S(2)}) collective-permute-start(bf16[16,4096]{1,0:T(8,128)(2,1)S(1)} %collective-permute-done.13.refs_6_), channel_id=1, source_target_pairs={{0,8},{2,10},{8,16},{10,18},{16,24},{18,26},{24,28},{26,30},{28,20... | collective-permute-start | bytes 393224 | tf_op jit(solution)/shard_map/ppermute | solution.py:211
  42.6 7.7 %collective-permute-start.20 = (bf16[16,4096]{1,0:T(8,128)(2,1)S(1)}, bf16[16,4096]{1,0:T(8,128)(2,1)S(1)}, u32[]{:S(2)}, u32[]{:S(2)}) collective-permute-start(bf16[16,4096]{1,0:T(8,128)(2,1)S(1)} %collective-permute-done.14.refs_8_), channel_id=1, source_target_pairs={{0,4},{2,6},{8,0},{10,2},{16,8},{18,10},{24,16},{26,18},{28,24},{3... | collective-permute-start | bytes 393224 | tf_op jit(solution)/shard_map/ppermute | solution.py:211
  48.0 6.6 %collective-permute-start.16 = (bf16[16,4096]{1,0:T(8,128)(2,1)S(1)}, bf16[16,4096]{1,0:T(8,128)(2,1)S(1)}, u32[]{:S(2)}, u32[]{:S(2)}) collective-permute-start(bf16[16,4096]{1,0:T(8,128)(2,1)S(1)} %collective-permute-done.13.refs_6_), channel_id=1, source_target_pairs={{0,2},{2,0},{4,6},{6,4},{8,10},{10,8},{12,14},{14,12},{16,18},{18,... | collective-permute-start | bytes 393224 | tf_op jit(solution)/shard_map/ppermute | solution.py:185
  48.4 7.7 %collective-permute-start.17 = (bf16[16,4096]{1,0:T(8,128)(2,1)S(1)}, bf16[16,4096]{1,0:T(8,128)(2,1)S(1)}, u32[]{:S(2)}, u32[]{:S(2)}) collective-permute-start(bf16[16,4096]{1,0:T(8,128)(2,1)S(1)} %collective-permute-done.14.refs_8_), channel_id=1, source_target_pairs={{0,2},{2,0},{4,6},{6,4},{8,10},{10,8},{12,14},{14,12},{16,18},{18,... | collective-permute-start | bytes 393224 | tf_op jit(solution)/shard_map/ppermute | solution.py:185
  50.9 6.4 %collective-permute-start.21 = (bf16[16,4096]{1,0:T(8,128)(2,1)S(1)}, bf16[16,4096]{1,0:T(8,128)(2,1)S(1)}, u32[]{:S(2)}, u32[]{:S(2)}) collective-permute-start(bf16[16,4096]{1,0:T(8,128)(2,1)S(1)} %collective-permute-done.20.refs_12_), channel_id=1, source_target_pairs={{0,2},{2,0},{4,6},{6,4},{8,10},{10,8},{12,14},{14,12},{16,18},{18,... | collective-permute-start | bytes 393224 | tf_op jit(solution)/shard_map/ppermute | solution.py:185
  53.8 8.6 %collective-permute-start.23 = (bf16[16,4096]{1,0:T(8,128)(2,1)S(1)}, bf16[16,4096]{1,0:T(8,128)(2,1)S(1)}, u32[]{:S(2)}, u32[]{:S(2)}) collective-permute-start(bf16[16,4096]{1,0:T(8,128)(2,1)S(1)} %collective-permute-done.22.refs_14_), channel_id=1, source_target_pairs={{0,2},{2,0},{4,6},{6,4},{8,10},{10,8},{12,14},{14,12},{16,18},{18,... | collective-permute-start | bytes 393224 | tf_op jit(solution)/shard_map/ppermute | solution.py:185
  54.6 8.5 %collective-permute-start.25 = (bf16[2,16,2320]{2,1,0:T(8,128)(2,1)S(1)}, bf16[2,16,2320]{2,1,0:T(8,128)(2,1)S(1)}, u32[]{:S(2)}, u32[]{:S(2)}) collective-permute-start(bf16[2,16,2320]{2,1,0:T(8,128)(2,1)S(1)} %get-tuple-element.43), channel_id=1, source_target_pairs={{0,4},{2,6},{4,0},{6,2},{8,12},{10,14},{12,8},{14,10},{16,20},{18,... | collective-permute-start | bytes 445448 | tf_op jit(solution)/shard_map/ppermute | solution.py:185
  56.1 8.3 %collective-permute-start.26 = (bf16[2,16,2320]{2,1,0:T(8,128)(2,1)S(1)}, bf16[2,16,2320]{2,1,0:T(8,128)(2,1)S(1)}, u32[]{:S(2)}, u32[]{:S(2)}) collective-permute-start(bf16[2,16,2320]{2,1,0:T(8,128)(2,1)S(1)} %get-tuple-element.44), channel_id=1, source_target_pairs={{0,8},{2,10},{4,12},{6,14},{8,0},{10,2},{12,4},{14,6},{16,24},{18,... | collective-permute-start | bytes 445448 | tf_op jit(solution)/shard_map/ppermute | solution.py:185
  56.3 9.8 %collective-permute-start.27 = (bf16[2,16,2320]{2,1,0:T(8,128)(2,1)S(1)}, bf16[2,16,2320]{2,1,0:T(8,128)(2,1)S(1)}, u32[]{:S(2)}, u32[]{:S(2)}) collective-permute-start(bf16[2,16,2320]{2,1,0:T(8,128)(2,1)S(1)} %get-tuple-element.45), channel_id=1, source_target_pairs={{0,12},{2,14},{4,8},{6,10},{8,4},{10,6},{12,0},{14,2},{16,28},{18,... | collective-permute-start | bytes 445448 | tf_op jit(solution)/shard_map/ppermute | solution.py:185
  57.4 11.5 %collective-permute-start.28 = (bf16[2,16,2320]{2,1,0:T(8,128)(2,1)S(1)}, bf16[2,16,2320]{2,1,0:T(8,128)(2,1)S(1)}, u32[]{:S(2)}, u32[]{:S(2)}) collective-permute-start(bf16[2,16,2320]{2,1,0:T(8,128)(2,1)S(1)} %get-tuple-element.46), channel_id=1, source_target_pairs={{0,16},{2,18},{4,20},{6,22},{8,24},{10,26},{12,28},{14,30},{16,0},... | collective-permute-start | bytes 445448 | tf_op jit(solution)/shard_map/ppermute | solution.py:185
  62.4 37.5 %collective-permute-start.42 = (bf16[1152,256]{1,0:T(8,128)(2,1)S(1)}, bf16[1152,256]{1,0:T(8,128)(2,1)S(1)}, u32[]{:S(2)}, u32[]{:S(2)}) collective-permute-start(bf16[1152,256]{1,0:T(8,128)(2,1)S(1)} %early_projection.5), channel_id=1, source_target_pairs={{0,1},{1,0},{2,3},{3,2},{4,5},{5,4},{6,7},{7,6},{8,9},{9,8},{10,11... | collective-permute-start | bytes 1769480 | tf_op jit(solution)/shard_map/ppermute | solution.py:189
  63.1 36.8 %collective-permute-start.41 = (bf16[1168,256]{1,0:T(8,128)(2,1)S(1)}, bf16[1168,256]{1,0:T(8,128)(2,1)S(1)}, u32[]{:S(2)}, u32[]{:S(2)}) collective-permute-start(bf16[1168,256]{1,0:T(8,128)(2,1)S(1)} %early_projection.4), channel_id=1, source_target_pairs={{0,1},{1,0},{2,3},{3,2},{4,5},{5,4},{6,7},{7,6},{8,9},{9,8},{10,11... | collective-permute-start | bytes 1794056 | tf_op jit(solution)/shard_map/ppermute | solution.py:189
  64.4 16.7 %collective-permute-start.29 = (bf16[2,16,2320]{2,1,0:T(8,128)(2,1)S(1)}, bf16[2,16,2320]{2,1,0:T(8,128)(2,1)S(1)}, u32[]{:S(2)}, u32[]{:S(2)}) collective-permute-start(bf16[2,16,2320]{2,1,0:T(8,128)(2,1)S(1)} %get-tuple-element.47), channel_id=1, source_target_pairs={{0,20},{2,22},{4,16},{6,18},{8,28},{10,30},{12,24},{14,26},{16,4},... | collective-permute-start | bytes 445448 | tf_op jit(solution)/shard_map/ppermute | solution.py:185
  66.1 20.1 %collective-permute-start.30 = (bf16[2,16,2320]{2,1,0:T(8,128)(2,1)S(1)}, bf16[2,16,2320]{2,1,0:T(8,128)(2,1)S(1)}, u32[]{:S(2)}, u32[]{:S(2)}) collective-permute-start(bf16[2,16,2320]{2,1,0:T(8,128)(2,1)S(1)} %get-tuple-element.48), channel_id=1, source_target_pairs={{0,24},{2,26},{4,28},{6,30},{8,16},{10,18},{12,20},{14,22},{16,8},... | collective-permute-start | bytes 445448 | tf_op jit(solution)/shard_map/ppermute | solution.py:185
  68.9 20.9 %collective-permute-start.31 = (bf16[2,16,2320]{2,1,0:T(8,128)(2,1)S(1)}, bf16[2,16,2320]{2,1,0:T(8,128)(2,1)S(1)}, u32[]{:S(2)}, u32[]{:S(2)}) collective-permute-start(bf16[2,16,2320]{2,1,0:T(8,128)(2,1)S(1)} %get-tuple-element.49), channel_id=1, source_target_pairs={{0,28},{2,30},{4,24},{6,26},{8,20},{10,22},{12,16},{14,18},{16,12}... | collective-permute-start | bytes 445448 | tf_op jit(solution)/shard_map/ppermute | solution.py:185
  81.1 18.8 %collective-permute-start.40 = (f32[256,256]{1,0:T(8,128)S(1)}, f32[256,256]{1,0:T(8,128)S(1)}, u32[]{:S(2)}, u32[]{:S(2)}) collective-permute-start(f32[256,256]{1,0:T(8,128)S(1)} %get-tuple-element.54), channel_id=1, source_target_pairs={{0,1},{1,0},{2,3},{3,2},{4,5},{5,4},{6,7},{7,6},{8,9},{9,8},{10,11... | collective-permute-start | bytes 786440 | tf_op jit(solution)/shard_map/ppermute | solution.py:189
  (23 other events, 137.1 us)
